TPU v7x, 512 devices: a whole 4x4x16 slice. The times are simulated.
512 devices in a mesh: row: 32 (over z, core), col: 16 (over x, y).
Axes of the slice: x: 4, y: 4, z: 16, core: 2. Of those that a mesh axis runs over, the one named last changes fastest.
Arguments:
- covariance: float32 [8192, 8192], P('row', 'col'), as said below
- state_mean: float32 [8192], P('row'), may hold values from -6 to 6
- obs_values: float32 [2, 256], replicated, may hold values from -8 to 8
- obs_cells: int32 [2, 4, 256], replicated, may hold values from 0 to 8191
- obs_weights: float32 [2, 4, 256], replicated, may hold values from 0.2 to 1
- obs_variance: float32 [2, 256], replicated, may hold values from 0.05 to 1
Outputs:
- covariance_after: float32 [8192, 8192], P('row', 'col')
- state_after: float32 [8192], P('row')
Inputs may be any that keep to these rules, and one draw needn't show every extreme that they name: `covariance`: symmetric and positive definite.
All inputs are finite; a program needn't handle non-finite values.
Results may differ from a plain program's by a relative error of at most 0.0001.
Values sent between devices are 32-bit elements; how exact they have to be, the bound alone decides.
No kernel may reach another device: no remote copies, remote signals or barrier semaphores. Data moves between devices by JAX's collectives and lax.ppermute only.
A program may use at most 64 MiB of HBM per device.

v0:
```python
import jax
import jax.numpy as jnp
from jax import lax
from jax.experimental import pallas as pl
from jax.experimental.pallas import tpu as pltpu
from jax.sharding import PartitionSpec as P

SUB = 8
LANES = 128
GROUPS = LANES // SUB
HI = lax.Precision.HIGHEST
VMEM = pl.BlockSpec(memory_space=pltpu.VMEM)
SMEM = pl.BlockSpec(memory_space=pltpu.SMEM)
LIMIT = 48 * 1024 * 1024


def dot(a, b):
    return jnp.dot(a, b, precision=HI, preferred_element_type=jnp.float32)


def dot_dims(a, b, da, db):
    return lax.dot_general(
        a, b, (((da,), (db,)), ((), ())), precision=HI, preferred_element_type=jnp.float32
    )


def wide(x):
    return jnp.broadcast_to(x, (SUB, LANES))


def lower_blocks(n):
    return [(i, j) for i in range(n) for j in range(i + 1)]


def call(kernel, out_shape, specs, scratch=(), flops=0, name=None):
    return pl.pallas_call(
        kernel,
        out_shape=out_shape,
        in_specs=specs,
        out_specs=jax.tree.map(lambda _: VMEM, out_shape),
        scratch_shapes=list(scratch),
        compiler_params=pltpu.CompilerParams(vmem_limit_bytes=LIMIT),
        cost_estimate=pl.CostEstimate(flops=flops, bytes_accessed=1 << 20, transcendentals=0),
        name=name,
    )


def shape(*dims):
    return jax.ShapeDtypeStruct(dims, jnp.float32)


def operator(cells_ref, weights_ref, batch, start, count):
    foot, obs = cells_ref.shape[1], cells_ref.shape[2]
    positions = start + lax.broadcasted_iota(jnp.int32, (count, obs), 0)
    total = jnp.zeros((count, obs), jnp.float32)
    for f in range(foot):
        hit = cells_ref[batch, f:f + 1, :] == positions
        total = total + jnp.where(hit, weights_ref[batch, f:f + 1, :], 0.0)
    return total


def project_kernel(at_ref, cov_ref, mean_ref, cells_ref, weights_ref, send_ref, c_ref, s_ref):
    rows, cols = cov_ref.shape
    batches, _, obs = cells_ref.shape
    plane = send_ref.shape[0]
    nb = batches * obs // LANES
    per = obs // LANES
    row_ops = []
    cov = cov_ref[...]
    for b in range(batches):
        col_op = operator(cells_ref, weights_ref, b, at_ref[1] * cols, cols)
        row_ops.append(operator(cells_ref, weights_ref, b, at_ref[0] * rows, rows))
        c_ref[:, b * obs:(b + 1) * obs] = dot(cov, col_op)
    for i in range(batches):
        for j in range(i + 1):
            s_ref[i * obs:(i + 1) * obs, j * obs:(j + 1) * obs] = dot_dims(
                row_ops[i], c_ref[:, j * obs:(j + 1) * obs], 0, 0
            )
    low = lower_blocks(nb)
    tiles = len(low) * GROUPS // plane
    lane = lax.broadcasted_iota(jnp.int32, (SUB, LANES), 1)
    sub = lax.broadcasted_iota(jnp.int32, (SUB, LANES), 0)
    mean = jnp.broadcast_to(mean_ref[...], (SUB, rows))
    mean = jnp.where(at_ref[1] == 0, mean, 0.0)
    preds = [dot(mean, row_ops[b]) for b in range(batches)]
    for n, (i, j) in enumerate(low):
        for g in range(GROUPS):
            t = s_ref[i * LANES + g * SUB:i * LANES + (g + 1) * SUB, j * LANES:(j + 1) * LANES]
            if i == j and g == 0:
                p = preds[i // per][:, (i % per) * LANES:(i % per + 1) * LANES]
                t = jnp.where((sub == 0) & (lane > 0), p, t)
                t = jnp.where((sub == 1) & (lane == LANES - 1), wide(p[:, :1]), t)
            q = n * GROUPS + g
            send_ref[q // tiles, (q % tiles) * SUB:(q % tiles + 1) * SUB, :] = t
    own = rows // plane
    for i in range(plane):
        for j in range(nb):
            at = (tiles + j) * SUB
            send_ref[i, at:at + own, :] = c_ref[i * own:(i + 1) * own, j * LANES:(j + 1) * LANES]


def inverse_factor(v):
    v = list(v)
    lane = lax.broadcasted_iota(jnp.int32, (SUB, LANES), 1)
    sub = lax.broadcasted_iota(jnp.int32, (SUB, LANES), 0)
    odd = (sub % 2) == 1

    def swap(z):
        return jnp.where(odd, pltpu.roll(z, 1, 0), pltpu.roll(z, SUB - 1, 0))

    out = []
    for p in range(len(v)):
        t = v[p]
        base = p * SUB
        inside = (lane >= base) & (lane < base + SUB)
        col = [wide(t[:, base + s:base + s + 1]) for s in range(SUB)]
        t = jnp.where(inside, jnp.where(lane - base == sub, 1.0, 0.0), t)
        low = t
        same = cross = step = jnp.zeros((SUB, LANES), jnp.float32)
        piv = jnp.ones((SUB, LANES), jnp.float32)
        for u in range(0, SUB, 2):
            a = wide(col[u][u:u + 1])
            b = wide(col[u + 1][u:u + 1])
            c = wide(col[u + 1][u + 1:u + 2])
            det = a * c - b * b
            rd = pltpu.reciprocal(det, approx=True)
            ra = pltpu.reciprocal(a, approx=True)
            here = (sub == u) | (sub == u + 1)
            c1 = jnp.where(here, 0.0, col[u])
            c2 = jnp.where(here, 0.0, col[u + 1])
            m1 = (c1 * c - c2 * b) * rd
            m2 = (c2 * a - c1 * b) * rd
            for w in range(u + 2, SUB):
                col[w] = col[w] - (m1 * wide(col[w][u:u + 1]) + m2 * wide(col[w][u + 1:u + 2]))
            t = t - (m1 * wide(t[u:u + 1]) + m2 * wide(t[u + 1:u + 2]))
            low = low - jnp.where(
                sub > u + 1, m1 * wide(low[u:u + 1]) + m2 * wide(low[u + 1:u + 2]), 0.0
            )
            same = jnp.where(sub == u, c * rd, jnp.where(sub == u + 1, a * rd, same))
            cross = jnp.where(here, b * rd, cross)
            step = jnp.where(sub == u + 1, b * ra, step)
            piv = jnp.where(sub == u, a, jnp.where(sub == u + 1, det * ra, piv))
        q = t * same - swap(t) * cross
        x = (low - step * swap(low)) * lax.rsqrt(piv)
        out.append(jnp.where(lane <= sub + base, x, 0.0))
        for j in range(p + 1, len(v)):
            w = v[j]
            c = [wide(w[:, base + s:base + s + 1]) * wide(q[s:s + 1]) for s in range(SUB)]
            w = jnp.where(inside, 0.0, w)
            v[j] = w - (((c[0] + c[1]) + (c[2] + c[3])) + ((c[4] + c[5]) + (c[6] + c[7])))
    return out


def factor_kernel(got_ref, values_ref, variance_ref, linv_ref, white_ref, a_ref, l_ref):
    nb = values_ref.shape[0]
    low = lower_blocks(nb)
    plane = got_ref.shape[0]
    tiles = len(low) * GROUPS // plane
    for n, (i, j) in enumerate(low):
        for g in range(GROUPS):
            q = n * GROUPS + g
            a_ref[i, j, g * SUB:(g + 1) * SUB, :] = got_ref[
                q // tiles, (q % tiles) * SUB:(q % tiles + 1) * SUB, :
            ]
    r_io = lax.broadcasted_iota(jnp.int32, (LANES, LANES), 0)
    l_io = lax.broadcasted_iota(jnp.int32, (LANES, LANES), 1)
    lane = lax.broadcasted_iota(jnp.int32, (SUB, LANES), 1)
    innov = []
    for i in range(nb):
        first = a_ref[i, i, 0:SUB, :]
        pred = jnp.where(lane == 0, wide(first[1:2, LANES - 1:LANES]), wide(first[0:1, :]))
        innov.append(wide(values_ref[i:i + 1, :]) - pred)
        d = a_ref[i, i]
        below = jnp.where(r_io > l_io, d, 0.0)
        diag = jnp.where(r_io == l_io, d + variance_ref[i:i + 1, :], 0.0)
        a_ref[i, i] = below + below.T + diag
    for i in range(nb):
        for j in range(i + 1, nb):
            linv_ref[i * LANES:(i + 1) * LANES, j * LANES:(j + 1) * LANES] = jnp.zeros(
                (LANES, LANES), jnp.float32
            )
    for i in range(nb):
        x = jnp.concatenate(
            inverse_factor([a_ref[i, i, g * SUB:(g + 1) * SUB, :] for g in range(GROUPS)]), axis=0
        )
        at = slice(i * LANES, (i + 1) * LANES)
        for j in range(i + 1, nb):
            l_ref[j, i] = dot_dims(a_ref[j, i], x, 1, 1)
        for k in range(i + 1, nb):
            for j in range(k, nb):
                a_ref[j, k] = a_ref[j, k] - dot_dims(l_ref[j, i], l_ref[k, i], 1, 1)
        linv_ref[at, at] = x
        if i > 0:
            acc = dot(l_ref[i, 0], linv_ref[0:LANES, 0:i * LANES])
            for k in range(1, i):
                acc = acc + dot(l_ref[i, k], linv_ref[k * LANES:(k + 1) * LANES, 0:i * LANES])
            linv_ref[at, 0:i * LANES] = -dot(x, acc)
    white_ref[...] = dot_dims(jnp.concatenate(innov, axis=1), linv_ref[...], 1, 1)


def rows_kernel(got_ref, linv_ref, white_ref, mean_ref, gain_ref, after_ref, c_ref):
    plane = got_ref.shape[0]
    rows, m = gain_ref.shape
    own = rows // plane
    nb = m // LANES
    skip = got_ref.shape[1] - nb * own
    for i in range(plane):
        for j in range(nb):
            at = skip + j * own
            c_ref[i * own:(i + 1) * own, j * LANES:(j + 1) * LANES] = got_ref[i, at:at + own, :]
    gain = dot_dims(c_ref[...], linv_ref[...], 1, 1)
    gain_ref[...] = gain
    after_ref[...] = dot_dims(white_ref[...], gain, 1, 1) + mean_ref[...]


def update_kernel(at_ref, cov_ref, mine_ref, other_ref, linv_ref, gain_ref, out_ref, c_ref):
    n_z, halves, tall, _ = mine_ref.shape
    cols, m = c_ref.shape
    nb = m // LANES
    own = tall // nb
    core = at_ref[2]
    for ref, k in ((mine_ref, core), (other_ref, 1 - core)):
        start = pl.multiple_of(k * (n_z * own), n_z * own)
        for h in range(halves):
            for z in range(n_z):
                for j in range(nb):
                    at = h * (cols // halves) + z * own
                    c_ref[pl.ds(start + at, own), j * LANES:(j + 1) * LANES] = ref[
                        z, h, j * own:(j + 1) * own, :
                    ]
    gain_cols = dot_dims(c_ref[...], linv_ref[...], 1, 1)
    out_ref[...] = cov_ref[...] - dot_dims(gain_ref[...], gain_cols, 1, 1)


def on_device(covariance, state_mean, obs_values, obs_cells, obs_weights, obs_variance):
    rows, cols = covariance.shape
    n_row, n_col = lax.axis_size("row"), lax.axis_size("col")
    n_z = n_row // 2
    row, col = lax.axis_index("row"), lax.axis_index("col")
    core = lax.rem(row, 2)
    plane = 2 * n_col
    batches, _, obs = obs_cells.shape
    m = batches * obs
    nb = m // LANES
    own = rows // plane
    c_rows = own * nb
    s_rows = nb * (nb + 1) // 2 * LANES // plane
    chunk = s_rows + c_rows
    at = jnp.stack([row, col, core]).astype(jnp.int32)
    mean = state_mean.reshape(1, rows)

    plane_groups = [[z * plane + i for i in range(plane)] for z in range(n_z)]
    z_groups = [[2 * z + k for z in range(n_z)] for k in range(2)]
    pairs = []
    for idx in range(n_row * n_col):
        r, c = divmod(idx, n_col)
        z, k = divmod(r, 2)
        pairs.append((idx, (2 * c + k) * n_col + z))

    send = call(
        project_kernel,
        shape(plane, chunk, LANES),
        [SMEM, VMEM, VMEM, VMEM, VMEM],
        [pltpu.VMEM((rows, m), jnp.float32), pltpu.VMEM((m, m), jnp.float32)],
        flops=2 * rows * m * (cols + m),
        name="project",
    )(at, covariance, mean, obs_cells, obs_weights)
    got = lax.all_to_all(send, ("row", "col"), 0, 0, axis_index_groups=plane_groups)
    s_chunk = jnp.sum(got[:, :s_rows], axis=0)
    c_own = jnp.sum(got[:, s_rows:].reshape(2, n_col, c_rows, LANES), axis=1)

    c_tr = lax.ppermute(c_own, ("row", "col"), pairs)
    s_all = lax.all_to_all(
        jnp.broadcast_to(s_chunk[None], (n_z, s_rows, LANES)), "row", 0, 0, axis_index_groups=z_groups
    )
    s_full = jnp.sum(s_all, axis=0)
    send2 = jnp.concatenate(
        [
            jnp.broadcast_to(s_full[None], (plane, s_rows, LANES)),
            jnp.broadcast_to(c_own[:, None], (2, n_col, c_rows, LANES)).reshape(plane, c_rows, LANES),
        ],
        axis=1,
    )
    got2 = lax.all_to_all(send2, ("row", "col"), 0, 0, axis_index_groups=plane_groups)

    c_tr, got2 = lax.optimization_barrier((c_tr, got2))
    c_z = lax.all_to_all(
        jnp.broadcast_to(c_tr[None], (n_z,) + c_tr.shape), "row", 0, 0, axis_index_groups=z_groups
    )
    linv, white = call(
        factor_kernel,
        (shape(m, m), shape(SUB, m)),
        [VMEM] * 3,
        [pltpu.VMEM((nb, nb, LANES, LANES), jnp.float32), pltpu.VMEM((nb, nb, LANES, LANES), jnp.float32)],
        flops=1 << 34,
        name="factor",
    )(got2, obs_values.reshape(nb, LANES), obs_variance.reshape(nb, LANES))
    c_other = lax.ppermute(c_z, "row", [(i, i ^ 1) for i in range(n_row)])
    gain, after = call(
        rows_kernel,
        (shape(rows, m), shape(SUB, rows)),
        [VMEM] * 4,
        [pltpu.VMEM((rows, m), jnp.float32)],
        flops=1 << 31,
        name="rows",
    )(got2, linv, white, mean)
    updated = call(
        update_kernel,
        shape(rows, cols),
        [SMEM] + [VMEM] * 5,
        [pltpu.VMEM((cols, m), jnp.float32)],
        flops=1 << 31,
        name="update",
    )(at, covariance, c_z, c_other, linv, gain)
    return (updated, after[0])


def solution(mesh):
    return jax.shard_map(
        on_device,
        mesh=mesh,
        in_specs=(P("row", "col"), P("row"), P(), P(), P(), P()),
        out_specs=(P("row", "col"), P("row")),
        check_vma=False,
    )
```

profile of v0, /device:TPU:1, one launch (start us, length us, event | category | flops | bytes accessed | tf_op | source)
XLA Modules:
  0.0 166.3 jit_solution(7417093577363845927)
XLA Ops:
  0.6 0.1 pad_add_fusion.at_ref
  0.7 1.0 copy-done
  1.8 0.7 copy-done.2
  2.5 0.7 copy-done.3
  3.2 0.7 copy-done.4
  3.8 3.0 %project.1 = f32[32,72,128]{2,1,0:T(8,128)S(1)} custom-call(s32[3]{0:T(128)S(1)} %pad_add_fusion.at_ref, f32[256,512]{1,0:T(8,128)S(1)} %copy-done, f32[1,256]{1,0:T(1,128)S(1)} %bitcast.8, s32[2,4,256]{2,1,0:T(4,128)S(1)} %copy-done.2, f32[2,4,256]{2,1,0:T(4,128)S(1)} %copy-done.3), custom_call_target="tpu_custom_call" | custom-call | flops 268435456 | bytes 1048576 | tf_op jit(solution)/shard_map/project/pallas_call | solution.py:260
  6.9 28.5 %all_to_all.20 = f32[32,72,128]{2,1,0:T(8,128)S(1)} all-to-all(f32[32,72,128]{2,1,0:T(8,128)S(1)} %project.1), channel_id=1, replica_groups={{0,1,2,3,4,5,6,7,8,9,10,11,12,13,14,15,16,17,18,19,20,21,22,23,24,25,26..., dimensions={0} | all-to-all | bytes 2359296 | tf_op jit(solution)/shard_map/all_to_all | solution.py:268
  35.4 0.1 slice_reduce_fusion
  35.4 0.7 broadcast_in_dim.8
  36.2 13.7 %all-to-all-start.1 = ((f32[16,40,128]{2,1,0:T(8,128)}), f32[16,40,128]{2,1,0:T(8,128)S(1)}, u32[]{:S(2)}, u32[]{:S(2)}) async-start(f32[16,40,128]{2,1,0:T(8,128)} %broadcast_in_dim.8), calls=%async_computation.1 | async-start | bytes 655360 | tf_op jit(solution)/shard_map/all_to_all | solution.py:273
  49.9 15.2 %all-to-all-done.1 = f32[16,40,128]{2,1,0:T(8,128)S(1)} async-done(((f32[16,40,128]{2,1,0:T(8,128)}), f32[16,40,128]{2,1,0:T(8,128)S(1)}, u32[]{:S(2)}, u32[]{:S(2)}) %all-to-all-start.1) | async-done | bytes 327712 | tf_op jit(solution)/shard_map/all_to_all | solution.py:273
  65.1 0.1 broadcast_in_dim.10
  65.2 1.1 pad_maximum_fusion
  66.3 10.3 %all-to-all-start.2 = ((f32[32,72,128]{2,1,0:T(8,128)}), f32[32,72,128]{2,1,0:T(8,128)S(1)}, u32[]{:S(2)}, u32[]{:S(2)}) async-start(f32[32,72,128]{2,1,0:T(8,128)} %pad_maximum_fusion), calls=%async_computation.2 | async-start | bytes 2359296 | tf_op jit(solution)/shard_map/all_to_all | solution.py:284
  76.6 0.7 collective-permute-start
  77.3 18.0 %all-to-all-done.2.got_ref = f32[32,72,128]{2,1,0:T(8,128)S(1)} async-done(((f32[32,72,128]{2,1,0:T(8,128)}), f32[32,72,128]{2,1,0:T(8,128)S(1)}, u32[]{:S(2)}, u32[]{:S(2)}) %all-to-all-start.2) | async-done | bytes 1179680 | tf_op jit(solution)/shard_map/all_to_all | solution.py:284
  95.2 0.9 broadcast_in_dim.11
  96.1 10.8 %all-to-all-start.3 = ((f32[16,2,32,128]{3,2,1,0:T(8,128)}), f32[16,2,32,128]{3,2,1,0:T(8,128)S(1)}, u32[]{:S(2)}, u32[]{:S(2)}) async-start(f32[16,2,32,128]{3,2,1,0:T(8,128)} %broadcast_in_dim.11), calls=%async_computation.3 | async-start | bytes 1048576 | tf_op jit(solution)/shard_map/all_to_all | solution.py:287
  107.0 22.7 %all-to-all-done.3.mine_ref = f32[16,2,32,128]{3,2,1,0:T(8,128)S(1)} async-done(((f32[16,2,32,128]{3,2,1,0:T(8,128)}), f32[16,2,32,128]{3,2,1,0:T(8,128)S(1)}, u32[]{:S(2)}, u32[]{:S(2)}) %all-to-all-start.3) | async-done | bytes 524320 | tf_op jit(solution)/shard_map/all_to_all | solution.py:287
  129.7 9.0 %collective-permute-start.1 = (f32[16,2,32,128]{3,2,1,0:T(8,128)S(1)}, f32[16,2,32,128]{3,2,1,0:T(8,128)S(1)}, u32[]{:S(2)}, u32[]{:S(2)}) collective-permute-start(f32[16,2,32,128]{3,2,1,0:T(8,128)S(1)} %all-to-all-done.3.mine_ref), channel_id=1, source_target_pairs={{0,16},{16,0},{32,48},{48,32},{64,80},{80,64},{96,112},{112,96},{1... | collective-permute-start | bytes 1572872 | tf_op jit(solution)/shard_map/ppermute | solution.py:298
  138.8 20.8 %factor.1 = (f32[512,512]{1,0:T(8,128)S(1)}, f32[8,512]{1,0:T(8,128)S(1)}) custom-call(f32[32,72,128]{2,1,0:T(8,128)S(1)} %all-to-all-done.2.got_ref, f32[4,128]{1,0:T(4,128)S(1)} %reshape.26.values_ref, f32[4,128]{1,0:T(4,128)S(1)} %reshape.27.variance_ref), custom_call_target="tpu_custom_call" | custom-call | flops 17179869184 | bytes 1048576 | tf_op jit(solution)/shard_map/factor/pallas_call | solution.py:290
  159.6 1.9 %rows.1 = (f32[256,512]{1,0:T(8,128)S(1)}, f32[8,256]{1,0:T(8,128)S(1)}) custom-call(f32[32,72,128]{2,1,0:T(8,128)S(1)} %all-to-all-done.2.got_ref, f32[512,512]{1,0:T(8,128)S(1)} %get-tuple-element.10.linv_ref, f32[8,512]{1,0:T(8,128)S(1)} %get-tuple-element.11.white_ref, f32[1,256]{1,0:T(1,128)S(1)} %bitcast.9), custom_call_target="tpu_custom_call" | custom-call | flops 2147483648 | bytes 1048576 | tf_op jit(solution)/shard_map/rows/pallas_call | solution.py:299
  161.4 0.6 slice.11
  162.1 4.3 %update.1 = f32[256,512]{1,0:T(8,128)} custom-call(s32[3]{0:T(128)S(1)} %pad_add_fusion.at_ref, f32[256,512]{1,0:T(8,128)S(1)} %copy-done.1, f32[16,2,32,128]{3,2,1,0:T(8,128)S(1)} %all-to-all-done.3.mine_ref, f32[16,2,32,128]{3,2,1,0:T(8,128)S(1)} %collective-permute-done.1.other_ref, f32[512,512]{1,0:T(8,128)S(1)} %get-tuple-element.10.linv_ref, ...), custom_call_target="tpu_custom_call" | custom-call | flops 2147483648 | bytes 1048576 | tf_op jit(solution)/shard_map/update/pallas_call | solution.py:307
  (19 shorter events, 0.2 us)
Async XLA Ops:
  0.7 1.0 copy-start
  1.8 0.7 copy-start.2
  2.5 0.7 copy-start.3
  3.1 0.7 copy-start.4
  36.2 28.9 %all-to-all-start.1 = ((f32[16,40,128]{2,1,0:T(8,128)}), f32[16,40,128]{2,1,0:T(8,128)S(1)}, u32[]{:S(2)}, u32[]{:S(2)}) async-start(f32[16,40,128]{2,1,0:T(8,128)} %broadcast_in_dim.8), calls=%async_computation.1 | async-start | bytes 655360 | tf_op jit(solution)/shard_map/all_to_all | solution.py:273
  66.3 28.9 %all-to-all-start.2 = ((f32[32,72,128]{2,1,0:T(8,128)}), f32[32,72,128]{2,1,0:T(8,128)S(1)}, u32[]{:S(2)}, u32[]{:S(2)}) async-start(f32[32,72,128]{2,1,0:T(8,128)} %pad_maximum_fusion), calls=%async_computation.2 | async-start | bytes 2359296 | tf_op jit(solution)/shard_map/all_to_all | solution.py:284
  76.5 30.4 %copy-start.6 = (f32[2,256]{1,0:T(2,128)S(1)}, f32[2,256]{1,0:T(2,128)}, u32[]{:S(2)}) copy-start(f32[2,256]{1,0:T(2,128)} %param.8) | copy-start | bytes 6148
  76.6 30.4 %copy-start.7 = (f32[2,256]{1,0:T(2,128)S(1)}, f32[2,256]{1,0:T(2,128)}, u32[]{:S(2)}) copy-start(f32[2,256]{1,0:T(2,128)} %param.11) | copy-start | bytes 6148
  76.6 0.7 collective-permute-start
  96.1 33.7 %all-to-all-start.3 = ((f32[16,2,32,128]{3,2,1,0:T(8,128)}), f32[16,2,32,128]{3,2,1,0:T(8,128)S(1)}, u32[]{:S(2)}, u32[]{:S(2)}) async-start(f32[16,2,32,128]{3,2,1,0:T(8,128)} %broadcast_in_dim.11), calls=%async_computation.3 | async-start | bytes 1048576 | tf_op jit(solution)/shard_map/all_to_all | solution.py:287
  107.0 52.6 %copy-start.5 = (f32[256]{0:T(256)S(1)}, f32[256]{0:T(256)}, u32[]{:S(2)}) copy-start(f32[256]{0:T(256)} %param.7) | copy-start | bytes 3076
  129.7 32.3 %collective-permute-start.1 = (f32[16,2,32,128]{3,2,1,0:T(8,128)S(1)}, f32[16,2,32,128]{3,2,1,0:T(8,128)S(1)}, u32[]{:S(2)}, u32[]{:S(2)}) collective-permute-start(f32[16,2,32,128]{3,2,1,0:T(8,128)S(1)} %all-to-all-done.3.mine_ref), channel_id=1, source_target_pairs={{0,16},{16,0},{32,48},{48,32},{64,80},{80,64},{96,112},{112,96},{1... | collective-permute-start | bytes 1572872 | tf_op jit(solution)/shard_map/ppermute | solution.py:298
  159.6 2.5 %copy-start.1 = (f32[256,512]{1,0:T(8,128)S(1)}, f32[256,512]{1,0:T(8,128)}, u32[]{:S(2)}) copy-start(f32[256,512]{1,0:T(8,128)} %cov_ref.3) | copy-start | bytes 1572868
where the time goes:
time: 167 us; the launch traced here: 166 us
  waiting for transfers between devices  55.9 us (33%)
  starting transfers between devices  44.5 us (27%)
  Pallas kernels  30 us (18%)
  blocking collectives  28.5 us (17%)
  local copies, waits for them, and re-layouts  5.46 us (3%)
    all_to_all x1, blocking collectives, on_device(): lax.all_to_all(send, ('row', 'col'), 0, 0, axis_index_groups=plane_groups)  28.5 us
    all_to_all x1, waiting for transfers between devices, on_device(): lax.all_to_all(jnp.broadcast_to(c_tr[None], (n_z,) + c_tr.shape), 'row',...  22.7 us
    pallas_call x1, Pallas kernels, on_device(): call(factor_kernel, (shape(m, m), shape(SUB, m)), [VMEM] * 3, [pltpu.VMEM...  20.8 us
    all_to_all x1, waiting for transfers between devices, on_device(): lax.all_to_all(send2, ('row', 'col'), 0, 0, axis_index_groups=plane_groups)  18 us
    all_to_all x1, waiting for transfers between devices, on_device(): lax.all_to_all(jnp.broadcast_to(s_chunk[None], (n_z, s_rows, LANES)), 'ro...  15.2 us
    all_to_all x1, starting transfers between devices, on_device(): lax.all_to_all(jnp.broadcast_to(s_chunk[None], (n_z, s_rows, LANES)), 'ro...  13.7 us
    all_to_all x1, starting transfers between devices, on_device(): lax.all_to_all(jnp.broadcast_to(c_tr[None], (n_z,) + c_tr.shape), 'row',...  10.8 us
    all_to_all x1, starting transfers between devices, on_device(): lax.all_to_all(send2, ('row', 'col'), 0, 0, axis_index_groups=plane_groups)  10.3 us
  transfers between devices with their start and end apart: 5, of which 3 were waited for; matrix products, arithmetic and copies ran while one was open for 0% of the time, Pallas kernels for 14%

commit v1 on v0

--- a/solution.py
+++ b/solution.py
@@ -269,10 +269,12 @@
     s_chunk = jnp.sum(got[:, :s_rows], axis=0)
     c_own = jnp.sum(got[:, s_rows:].reshape(2, n_col, c_rows, LANES), axis=1)
 
+    s_send, c_own = lax.optimization_barrier(
+        (jnp.broadcast_to(s_chunk[None], (n_z, s_rows, LANES)), c_own)
+    )
+    s_all = lax.all_to_all(s_send, "row", 0, 0, axis_index_groups=z_groups)
+    s_all, c_own = lax.optimization_barrier((s_all, c_own))
     c_tr = lax.ppermute(c_own, ("row", "col"), pairs)
-    s_all = lax.all_to_all(
-        jnp.broadcast_to(s_chunk[None], (n_z, s_rows, LANES)), "row", 0, 0, axis_index_groups=z_groups
-    )
     s_full = jnp.sum(s_all, axis=0)
     send2 = jnp.concatenate(
         [
@@ -295,6 +297,7 @@
         flops=1 << 34,
         name="factor",
     )(got2, obs_values.reshape(nb, LANES), obs_variance.reshape(nb, LANES))
+    c_z, linv = lax.optimization_barrier((c_z, linv))
     c_other = lax.ppermute(c_z, "row", [(i, i ^ 1) for i in range(n_row)])
     gain, after = call(
         rows_kernel,

time: 167 us -> 145 us (0.87)
  waiting for transfers between devices: 55.9 us -> 19.7 us
  blocking collectives: 28.5 us -> 57.2 us
  starting transfers between devices: 44.5 us -> 30.8 us
    all_to_all x0 -> x1, blocking collectives: none -> 28.7 us  [on_device(): s_all = lax.all_to_all(s_send, 'row', 0, 0, axis_index_groups=z_groups)]
    all_to_all x1, waiting for transfers between devices: 22.7 us -> 1.75 us  [on_device(): lax.all_to_all(jnp.broadcast_to(c_tr[None], (n_z,) + c_tr.shape), 'row',...]
    all_to_all x1 -> x0, waiting for transfers between devices: 15.2 us -> none  [on_device(): lax.all_to_all(jnp.broadcast_to(s_chunk[None], (n_z, s_rows, LANES)), 'ro...]
    all_to_all x1 -> x0, starting transfers between devices: 13.7 us -> none  [on_device(): lax.all_to_all(jnp.broadcast_to(s_chunk[None], (n_z, s_rows, LANES)), 'ro...]
  transfers between devices with their start and end apart: 5 -> 4, of which waited for: 3 -> 2; matrix products, arithmetic and copies ran while one was open for 0% -> 0% of each run, Pallas kernels for 14% -> 16%
where the time goes in v1:
time: 145 us; the launch traced here: 144 us
  blocking collectives  57.2 us (39%)
  starting transfers between devices  30.8 us (21%)
  Pallas kernels  29.9 us (21%)
  waiting for transfers between devices  19.7 us (14%)
  local copies, waits for them, and re-layouts  4.73 us (3%)
    all_to_all x1, blocking collectives, on_device(): s_all = lax.all_to_all(s_send, 'row', 0, 0, axis_index_groups=z_groups)  28.7 us
    all_to_all x1, blocking collectives, on_device(): lax.all_to_all(send, ('row', 'col'), 0, 0, axis_index_groups=plane_groups)  28.5 us
    pallas_call x1, Pallas kernels, on_device(): call(factor_kernel, (shape(m, m), shape(SUB, m)), [VMEM] * 3, [pltpu.VMEM...  20.8 us
    all_to_all x1, waiting for transfers between devices, on_device(): lax.all_to_all(send2, ('row', 'col'), 0, 0, axis_index_groups=plane_groups)  18 us
    all_to_all x1, starting transfers between devices, on_device(): lax.all_to_all(jnp.broadcast_to(c_tr[None], (n_z,) + c_tr.shape), 'row',...  11 us
    all_to_all x1, starting transfers between devices, on_device(): lax.all_to_all(send2, ('row', 'col'), 0, 0, axis_index_groups=plane_groups)  10.2 us
    ppermute x1, starting transfers between devices, on_device(): c_other = lax.ppermute(c_z, 'row', [(i, i ^ 1) for i in range(n_row)])  8.84 us
    pallas_call x1, Pallas kernels, on_device(): call(update_kernel, shape(rows, cols), [SMEM] + [VMEM] * 5, [pltpu.VMEM((...  4.28 us
  transfers between devices with their start and end apart: 4, of which 2 were waited for; matrix products, arithmetic and copies ran while one was open for 0% of the time, Pallas kernels for 16%

profile of v1, /device:TPU:1, one launch (start us, length us, event | category | flops | bytes accessed | tf_op | source)
XLA Modules:
  0.0 144.4 jit_solution(3788582879566389297)
XLA Ops:
  0.6 0.1 pad_add_fusion.at_ref
  0.7 1.0 copy-done
  1.8 0.7 copy-done.2
  2.5 0.7 copy-done.3
  3.2 0.7 copy-done.4
  3.8 3.0 %project.1 = f32[32,72,128]{2,1,0:T(8,128)S(1)} custom-call(s32[3]{0:T(128)S(1)} %pad_add_fusion.at_ref, f32[256,512]{1,0:T(8,128)S(1)} %copy-done, f32[1,256]{1,0:T(1,128)S(1)} %bitcast.8, s32[2,4,256]{2,1,0:T(4,128)S(1)} %copy-done.2, f32[2,4,256]{2,1,0:T(4,128)S(1)} %copy-done.3), custom_call_target="tpu_custom_call" | custom-call | flops 268435456 | bytes 1048576 | tf_op jit(solution)/shard_map/project/pallas_call | solution.py:260
  6.9 28.5 %all_to_all.20 = f32[32,72,128]{2,1,0:T(8,128)S(1)} all-to-all(f32[32,72,128]{2,1,0:T(8,128)S(1)} %project.1), channel_id=1, replica_groups={{0,1,2,3,4,5,6,7,8,9,10,11,12,13,14,15,16,17,18,19,20,21,22,23,24,25,26..., dimensions={0} | all-to-all | bytes 2359296 | tf_op jit(solution)/shard_map/all_to_all | solution.py:268
  35.4 0.1 slice_reduce_fusion
  35.5 28.7 %all_to_all.21 = f32[16,40,128]{2,1,0:T(8,128)S(1)} all-to-all(f32[16,40,128]{2,1,0:T(8,128)S(1)} %broadcast_in_dim.8), channel_id=1, replica_groups={{0,32,64,96,128,160,192,224,256,288,320,352,384,416,448,480},{16,48,80,..., dimensions={0} | all-to-all | bytes 655360 | tf_op jit(solution)/shard_map/all_to_all | solution.py:275
  64.2 0.1 broadcast_in_dim.10
  64.3 1.1 pad_maximum_fusion
  65.4 10.2 %all-to-all-start.2 = ((f32[32,72,128]{2,1,0:T(8,128)}), f32[32,72,128]{2,1,0:T(8,128)S(1)}, u32[]{:S(2)}, u32[]{:S(2)}) async-start(f32[32,72,128]{2,1,0:T(8,128)} %pad_maximum_fusion), calls=%async_computation.2 | async-start | bytes 2359296 | tf_op jit(solution)/shard_map/all_to_all | solution.py:286
  75.6 0.0 copy-start.6
  75.7 0.0 copy-start.7
  75.7 0.7 collective-permute-start
  76.4 18.0 %all-to-all-done.2.got_ref = f32[32,72,128]{2,1,0:T(8,128)S(1)} async-done(((f32[32,72,128]{2,1,0:T(8,128)}), f32[32,72,128]{2,1,0:T(8,128)S(1)}, u32[]{:S(2)}, u32[]{:S(2)}) %all-to-all-start.2) | async-done | bytes 1179680 | tf_op jit(solution)/shard_map/all_to_all | solution.py:286
  94.3 0.9 broadcast_in_dim.11
  95.2 11.0 %all-to-all-start.3 = ((f32[16,2,32,128]{3,2,1,0:T(8,128)}), f32[16,2,32,128]{3,2,1,0:T(8,128)S(1)}, u32[]{:S(2)}, u32[]{:S(2)}) async-start(f32[16,2,32,128]{3,2,1,0:T(8,128)} %broadcast_in_dim.11), calls=%async_computation.3 | async-start | bytes 1048576 | tf_op jit(solution)/shard_map/all_to_all | solution.py:289
  106.3 20.8 %factor.1 = (f32[512,512]{1,0:T(8,128)S(1)}, f32[8,512]{1,0:T(8,128)S(1)}) custom-call(f32[32,72,128]{2,1,0:T(8,128)S(1)} %all-to-all-done.2.got_ref, f32[4,128]{1,0:T(4,128)S(1)} %reshape.26.values_ref, f32[4,128]{1,0:T(4,128)S(1)} %reshape.27.variance_ref), custom_call_target="tpu_custom_call" | custom-call | flops 17179869184 | bytes 1048576 | tf_op jit(solution)/shard_map/factor/pallas_call | solution.py:292
  127.1 1.8 %all-to-all-done.3.mine_ref = f32[16,2,32,128]{3,2,1,0:T(8,128)S(1)} async-done(((f32[16,2,32,128]{3,2,1,0:T(8,128)}), f32[16,2,32,128]{3,2,1,0:T(8,128)S(1)}, u32[]{:S(2)}, u32[]{:S(2)}) %all-to-all-start.3) | async-done | bytes 524320 | tf_op jit(solution)/shard_map/all_to_all | solution.py:289
  128.8 8.8 %collective-permute-start.1 = (f32[16,2,32,128]{3,2,1,0:T(8,128)S(1)}, f32[16,2,32,128]{3,2,1,0:T(8,128)S(1)}, u32[]{:S(2)}, u32[]{:S(2)}) collective-permute-start(f32[16,2,32,128]{3,2,1,0:T(8,128)S(1)} %all-to-all-done.3.mine_ref), channel_id=1, source_target_pairs={{0,16},{16,0},{32,48},{48,32},{64,80},{80,64},{96,112},{112,96},{1... | collective-permute-start | bytes 1572872 | tf_op jit(solution)/shard_map/ppermute | solution.py:301
  137.7 1.8 %rows.1 = (f32[256,512]{1,0:T(8,128)S(1)}, f32[8,256]{1,0:T(8,128)S(1)}) custom-call(f32[32,72,128]{2,1,0:T(8,128)S(1)} %all-to-all-done.2.got_ref, f32[512,512]{1,0:T(8,128)S(1)} %get-tuple-element.22.linv_ref, f32[8,512]{1,0:T(8,128)S(1)} %get-tuple-element.23.white_ref, f32[1,256]{1,0:T(1,128)S(1)} %bitcast.9), custom_call_target="tpu_custom_call" | custom-call | flops 2147483648 | bytes 1048576 | tf_op jit(solution)/shard_map/rows/pallas_call | solution.py:302
  139.5 0.6 slice.11
  140.1 4.3 %update.1 = f32[256,512]{1,0:T(8,128)} custom-call(s32[3]{0:T(128)S(1)} %pad_add_fusion.at_ref, f32[256,512]{1,0:T(8,128)S(1)} %copy-done.1, f32[16,2,32,128]{3,2,1,0:T(8,128)S(1)} %all-to-all-done.3.mine_ref, f32[16,2,32,128]{3,2,1,0:T(8,128)S(1)} %collective-permute-done.1.other_ref, f32[512,512]{1,0:T(8,128)S(1)} %get-tuple-element.22.linv_ref, ...), custom_call_target="tpu_custom_call" | custom-call | flops 2147483648 | bytes 1048576 | tf_op jit(solution)/shard_map/update/pallas_call | solution.py:310
  (18 shorter events, 0.2 us)
Async XLA Ops:
  0.7 1.0 copy-start
  1.8 0.7 copy-start.2
  2.5 0.7 copy-start.3
  3.1 0.7 copy-start.4
  65.4 28.9 %all-to-all-start.2 = ((f32[32,72,128]{2,1,0:T(8,128)}), f32[32,72,128]{2,1,0:T(8,128)S(1)}, u32[]{:S(2)}, u32[]{:S(2)}) async-start(f32[32,72,128]{2,1,0:T(8,128)} %pad_maximum_fusion), calls=%async_computation.2 | async-start | bytes 2359296 | tf_op jit(solution)/shard_map/all_to_all | solution.py:286
  75.6 30.6 %copy-start.6 = (f32[2,256]{1,0:T(2,128)S(1)}, f32[2,256]{1,0:T(2,128)}, u32[]{:S(2)}) copy-start(f32[2,256]{1,0:T(2,128)} %param.8) | copy-start | bytes 6148
  75.7 30.6 %copy-start.7 = (f32[2,256]{1,0:T(2,128)S(1)}, f32[2,256]{1,0:T(2,128)}, u32[]{:S(2)}) copy-start(f32[2,256]{1,0:T(2,128)} %param.11) | copy-start | bytes 6148
  75.7 0.7 collective-permute-start
  95.2 33.7 %all-to-all-start.3 = ((f32[16,2,32,128]{3,2,1,0:T(8,128)}), f32[16,2,32,128]{3,2,1,0:T(8,128)S(1)}, u32[]{:S(2)}, u32[]{:S(2)}) async-start(f32[16,2,32,128]{3,2,1,0:T(8,128)} %broadcast_in_dim.11), calls=%async_computation.3 | async-start | bytes 1048576 | tf_op jit(solution)/shard_map/all_to_all | solution.py:289
  106.3 31.4 %copy-start.5 = (f32[256]{0:T(256)S(1)}, f32[256]{0:T(256)}, u32[]{:S(2)}) copy-start(f32[256]{0:T(256)} %param.7) | copy-start | bytes 3076
  128.8 11.3 %collective-permute-start.1 = (f32[16,2,32,128]{3,2,1,0:T(8,128)S(1)}, f32[16,2,32,128]{3,2,1,0:T(8,128)S(1)}, u32[]{:S(2)}, u32[]{:S(2)}) collective-permute-start(f32[16,2,32,128]{3,2,1,0:T(8,128)S(1)} %all-to-all-done.3.mine_ref), channel_id=1, source_target_pairs={{0,16},{16,0},{32,48},{48,32},{64,80},{80,64},{96,112},{112,96},{1... | collective-permute-start | bytes 1572872 | tf_op jit(solution)/shard_map/ppermute | solution.py:301
  137.7 2.4 %copy-start.1 = (f32[256,512]{1,0:T(8,128)S(1)}, f32[256,512]{1,0:T(8,128)}, u32[]{:S(2)}) copy-start(f32[256,512]{1,0:T(8,128)} %cov_ref.3) | copy-start | bytes 1572868

commit v2 on v0

v2 whole, which is shorter than its diff:
```python
import jax
import jax.numpy as jnp
from jax import lax
from jax.experimental import pallas as pl
from jax.experimental.pallas import tpu as pltpu
from jax.sharding import PartitionSpec as P

SUB = 8
LANES = 128
GROUPS = LANES // SUB
HI = lax.Precision.HIGHEST
HBM = pl.BlockSpec(memory_space=pltpu.HBM)
VMEM = pl.BlockSpec(memory_space=pltpu.VMEM)
SMEM = pl.BlockSpec(memory_space=pltpu.SMEM)
LIMIT = 48 * 1024 * 1024


def dot(a, b):
    return jnp.dot(a, b, precision=HI, preferred_element_type=jnp.float32)


def dot_dims(a, b, da, db):
    return lax.dot_general(
        a, b, (((da,), (db,)), ((), ())), precision=HI, preferred_element_type=jnp.float32
    )


def wide(x):
    return jnp.broadcast_to(x, (SUB, LANES))


def lower_blocks(n):
    return [(i, j) for i in range(n) for j in range(i + 1)]


def call(kernel, out_shape, specs, scratch=(), flops=0, name=None):
    return pl.pallas_call(
        kernel,
        out_shape=out_shape,
        in_specs=specs,
        out_specs=jax.tree.map(lambda _: VMEM, out_shape),
        scratch_shapes=list(scratch),
        compiler_params=pltpu.CompilerParams(vmem_limit_bytes=LIMIT),
        cost_estimate=pl.CostEstimate(flops=flops, bytes_accessed=1 << 20, transcendentals=0),
        name=name,
    )


def shape(*dims):
    return jax.ShapeDtypeStruct(dims, jnp.float32)


def operator(cells_ref, weights_ref, batch, start, count):
    foot, obs = cells_ref.shape[1], cells_ref.shape[2]
    positions = start + lax.broadcasted_iota(jnp.int32, (count, obs), 0)
    total = jnp.zeros((count, obs), jnp.float32)
    for f in range(foot):
        hit = cells_ref[batch, f:f + 1, :] == positions
        total = total + jnp.where(hit, weights_ref[batch, f:f + 1, :], 0.0)
    return total


def project_kernel(
    at_ref, cov_in, mean_in, cells_in, weights_in, send_ref, c_ref, s_ref, cov_ref, mean_ref, cells_ref, weights_ref, sems
):
    moves = [
        pltpu.make_async_copy(src, dst, sems.at[n])
        for n, (src, dst) in enumerate(
            [(cells_in, cells_ref), (weights_in, weights_ref), (cov_in, cov_ref), (mean_in, mean_ref)]
        )
    ]
    for move in moves:
        move.start()
    for move in moves:
        move.wait()
    rows, cols = cov_ref.shape
    batches, _, obs = cells_ref.shape
    plane = send_ref.shape[0]
    nb = batches * obs // LANES
    per = obs // LANES
    row_ops = []
    cov = cov_ref[...]
    for b in range(batches):
        col_op = operator(cells_ref, weights_ref, b, at_ref[1] * cols, cols)
        row_ops.append(operator(cells_ref, weights_ref, b, at_ref[0] * rows, rows))
        c_ref[:, b * obs:(b + 1) * obs] = dot(cov, col_op)
    for i in range(batches):
        for j in range(i + 1):
            s_ref[i * obs:(i + 1) * obs, j * obs:(j + 1) * obs] = dot_dims(
                row_ops[i], c_ref[:, j * obs:(j + 1) * obs], 0, 0
            )
    low = lower_blocks(nb)
    tiles = len(low) * GROUPS // plane
    lane = lax.broadcasted_iota(jnp.int32, (SUB, LANES), 1)
    sub = lax.broadcasted_iota(jnp.int32, (SUB, LANES), 0)
    mean = jnp.broadcast_to(mean_ref[...], (SUB, rows))
    mean = jnp.where(at_ref[1] == 0, mean, 0.0)
    preds = [dot(mean, row_ops[b]) for b in range(batches)]
    for n, (i, j) in enumerate(low):
        for g in range(GROUPS):
            t = s_ref[i * LANES + g * SUB:i * LANES + (g + 1) * SUB, j * LANES:(j + 1) * LANES]
            if i == j and g == 0:
                p = preds[i // per][:, (i % per) * LANES:(i % per + 1) * LANES]
                t = jnp.where((sub == 0) & (lane > 0), p, t)
                t = jnp.where((sub == 1) & (lane == LANES - 1), wide(p[:, :1]), t)
            q = n * GROUPS + g
            send_ref[q // tiles, (q % tiles) * SUB:(q % tiles + 1) * SUB, :] = t
    own = rows // plane
    for i in range(plane):
        for j in range(nb):
            at = (tiles + j) * SUB
            send_ref[i, at:at + own, :] = c_ref[i * own:(i + 1) * own, j * LANES:(j + 1) * LANES]


def inverse_factor(v, jobs):
    v = list(v)
    lane = lax.broadcasted_iota(jnp.int32, (SUB, LANES), 1)
    sub = lax.broadcasted_iota(jnp.int32, (SUB, LANES), 0)
    out = []
    following = None
    for p in range(len(v)):
        last = p + 1 == len(v)
        t = v[p]
        base = p * SUB
        inside = (lane >= base) & (lane < base + SUB)
        col = following or [wide(t[:, base + s:base + s + 1]) for s in range(SUB)]
        ahead, square = [], []
        if not last:
            nxt = base + SUB
            ahead = [wide(t[:, nxt + s:nxt + s + 1]) for s in range(SUB)]
            square = [wide(v[p + 1][:, nxt + s:nxt + s + 1]) for s in range(SUB)]
        t = jnp.where(inside, jnp.where(lane - base == sub, 1.0, 0.0), t)
        low = t
        piv = jnp.ones((SUB, LANES), jnp.float32)
        pairs = []
        for u in range(0, SUB, 2):
            a = wide(col[u][u:u + 1])
            b = wide(col[u + 1][u:u + 1])
            c = wide(col[u + 1][u + 1:u + 2])
            det = a * c - b * b
            rd = pltpu.reciprocal(det, approx=True)
            ra = pltpu.reciprocal(a, approx=True)
            here = (sub == u) | (sub == u + 1)
            c1 = jnp.where(here, 0.0, col[u])
            c2 = jnp.where(here, 0.0, col[u + 1])
            m1 = (c1 * c - c2 * b) * rd
            m2 = (c2 * a - c1 * b) * rd

            def clear(z):
                return z - (m1 * wide(z[u:u + 1]) + m2 * wide(z[u + 1:u + 2]))

            for w in range(u + 2, SUB):
                col[w] = clear(col[w])
            ahead = [clear(z) for z in ahead]
            t = clear(t)
            low = jnp.where(
                sub > u + 1, clear(low), jnp.where(sub == u + 1, low - (b * ra) * wide(low[u:u + 1]), low)
            )
            piv = jnp.where(sub == u, a, jnp.where(sub == u + 1, det * ra, piv))
            pairs.append((a * rd, b * rd, c * rd))
        out.append(jnp.where(lane <= sub + base, low * lax.rsqrt(piv), 0.0))

        def solved(z):
            q = []
            for u in range(0, SUB, 2):
                ar, br, cr = pairs[u // 2]
                z0, z1 = wide(z[u:u + 1]), wide(z[u + 1:u + 2])
                q.extend((z0 * cr - z1 * br, z1 * ar - z0 * br))
            return q

        def less(w, c, q):
            g = [c[s] * q[s] for s in range(SUB)]
            return w - (((g[0] + g[1]) + (g[2] + g[3])) + ((g[4] + g[5]) + (g[6] + g[7])))

        if not last:
            q = solved(t)
            following = None
            for j in range(p + 1, len(v)):
                c = [wide(v[j][:, base + s:base + s + 1]) for s in range(SUB)]
                v[j] = less(jnp.where(inside, 0.0, v[j]), c, q)
                if following is None:
                    following = [less(square[s], c, solved(ahead[s])) for s in range(SUB)]
        if jobs:
            jobs.pop(0)()
    while jobs:
        jobs.pop(0)()
    return jnp.concatenate(out, axis=0)


def factor_kernel(
    got_ref, values_ref, variance_ref, mean_ref, linv_ref, gain_ref, after_ref, a_ref, l_ref, e_ref, y_ref
):
    nb = values_ref.shape[0]
    rows = gain_ref.shape[0]
    low = lower_blocks(nb)
    plane = got_ref.shape[0]
    tiles = len(low) * GROUPS // plane
    own = rows // plane
    for n, (i, j) in enumerate(low):
        for g in range(GROUPS):
            q = n * GROUPS + g
            a_ref[i, j, g * SUB:(g + 1) * SUB, :] = got_ref[
                q // tiles, (q % tiles) * SUB:(q % tiles + 1) * SUB, :
            ]
    for i in range(plane):
        for j in range(nb):
            at = tiles * SUB + j * own
            e_ref[j, i * own:(i + 1) * own, :] = got_ref[i, at:at + own, :]
    r_io = lax.broadcasted_iota(jnp.int32, (LANES, LANES), 0)
    l_io = lax.broadcasted_iota(jnp.int32, (LANES, LANES), 1)
    lane = lax.broadcasted_iota(jnp.int32, (SUB, LANES), 1)
    for i in range(nb):
        first = a_ref[i, i, 0:SUB, :]
        pred = jnp.where(lane == 0, wide(first[1:2, LANES - 1:LANES]), wide(first[0:1, :]))
        e_ref[i, rows:rows + SUB, :] = wide(values_ref[i:i + 1, :]) - pred
        d = a_ref[i, i]
        below = jnp.where(r_io > l_io, d, 0.0)
        diag = jnp.where(r_io == l_io, d + variance_ref[i:i + 1, :], 0.0)
        a_ref[i, i] = below + below.T + diag
    for i in range(nb):
        for j in range(i + 1, nb):
            linv_ref[i * LANES:(i + 1) * LANES, j * LANES:(j + 1) * LANES] = jnp.zeros(
                (LANES, LANES), jnp.float32
            )

    def span(i):
        return slice(i * LANES, (i + 1) * LANES)

    def scale(j, i, x):
        l_ref[j, i] = dot_dims(a_ref[j, i], x, 1, 1)

    def reduce(j, k, i):
        a_ref[j, k] = a_ref[j, k] - dot_dims(l_ref[j, i], l_ref[k, i], 1, 1)

    def scale_rows(i, x):
        e_ref[i] = dot_dims(e_ref[i], x, 1, 1)

    def reduce_rows(k, i):
        e_ref[k] = e_ref[k] - dot_dims(e_ref[i], l_ref[k, i], 1, 1)

    def gather(i):
        acc = dot(l_ref[i, 0], linv_ref[0:LANES, 0:i * LANES])
        for k in range(1, i):
            acc = acc + dot(l_ref[i, k], linv_ref[span(k), 0:i * LANES])
        y_ref[:, 0:i * LANES] = acc

    def finish(i):
        linv_ref[span(i), 0:i * LANES] = -dot(linv_ref[span(i), span(i)], y_ref[:, 0:i * LANES])

    def work(f, *args):
        return lambda: f(*args)

    jobs = []
    for i in range(nb):
        x = inverse_factor([a_ref[i, i, g * SUB:(g + 1) * SUB, :] for g in range(GROUPS)], jobs)
        linv_ref[span(i), span(i)] = x
        if i + 1 < nb:
            scale(i + 1, i, x)
            reduce(i + 1, i + 1, i)
            for j in range(i + 2, nb):
                jobs.append(work(scale, j, i, x))
            for k in range(i + 1, nb):
                for j in range(max(k, i + 2), nb):
                    jobs.append(work(reduce, j, k, i))
            jobs.append(work(scale_rows, i, x))
            for k in range(i + 1, nb):
                jobs.append(work(reduce_rows, k, i))
            if i > 0:
                jobs.append(work(finish, i))
            jobs.append(work(gather, i + 1))
        else:
            scale_rows(i, x)
            finish(i)
    for i in range(nb):
        gain_ref[:, span(i)] = e_ref[i, 0:rows, :]
    after = mean_ref[...]
    for i in range(nb):
        after = after + dot_dims(e_ref[i, rows:rows + SUB, :], e_ref[i, 0:rows, :], 1, 1)
    after_ref[...] = after


def update_kernel(cov_ref, pieces_ref, linv_ref, gain_ref, out_ref, c_ref):
    n_row, halves, tall, _ = pieces_ref.shape
    cols, m = c_ref.shape
    nb = m // LANES
    own = tall // nb
    for h in range(halves):
        for r in range(n_row):
            z, k = divmod(r, 2)
            at = h * (cols // halves) + (k * (n_row // 2) + z) * own
            for j in range(nb):
                c_ref[at:at + own, j * LANES:(j + 1) * LANES] = pieces_ref[r, h, j * own:(j + 1) * own, :]
    gain_cols = dot_dims(c_ref[...], linv_ref[...], 1, 1)
    out_ref[...] = cov_ref[...] - dot_dims(gain_ref[...], gain_cols, 1, 1)


def on_device(covariance, state_mean, obs_values, obs_cells, obs_weights, obs_variance):
    rows, cols = covariance.shape
    n_row, n_col = lax.axis_size("row"), lax.axis_size("col")
    n_z = n_row // 2
    row, col = lax.axis_index("row"), lax.axis_index("col")
    plane = 2 * n_col
    batches, _, obs = obs_cells.shape
    m = batches * obs
    nb = m // LANES
    own = rows // plane
    c_rows = own * nb
    s_rows = nb * (nb + 1) // 2 * LANES // plane
    chunk = s_rows + c_rows
    at = jnp.stack([row, col]).astype(jnp.int32)
    mean = state_mean.reshape(1, rows)

    plane_groups = [[z * plane + i for i in range(plane)] for z in range(n_z)]
    z_groups = [[2 * z + k for z in range(n_z)] for k in range(2)]
    pairs = []
    for idx in range(n_row * n_col):
        r, c = divmod(idx, n_col)
        z, k = divmod(r, 2)
        pairs.append((idx, (2 * c + k) * n_col + z))

    send = call(
        project_kernel,
        shape(plane, chunk, LANES),
        [SMEM] + [HBM] * 4,
        [
            pltpu.VMEM((rows, m), jnp.float32),
            pltpu.VMEM((m, m), jnp.float32),
            pltpu.VMEM((rows, cols), jnp.float32),
            pltpu.VMEM((1, rows), jnp.float32),
            pltpu.VMEM(obs_cells.shape, jnp.int32),
            pltpu.VMEM(obs_weights.shape, jnp.float32),
            pltpu.SemaphoreType.DMA((4,)),
        ],
        flops=2 * rows * m * (cols + m),
        name="project",
    )(at, covariance, mean, obs_cells, obs_weights)
    got = lax.all_to_all(send, ("row", "col"), 0, 0, axis_index_groups=plane_groups)
    s_chunk = jnp.sum(got[:, :s_rows], axis=0)
    c_own = jnp.sum(got[:, s_rows:].reshape(2, n_col, c_rows, LANES), axis=1)

    s_send = jnp.broadcast_to(s_chunk[None], (n_z, s_rows, LANES))
    c_tr = lax.ppermute(c_own, ("row", "col"), pairs)
    s_all = lax.all_to_all(s_send, "row", 0, 0, axis_index_groups=z_groups)
    c_cols = lax.all_gather(c_tr, "row")
    s_full = jnp.sum(s_all, axis=0)
    send2 = jnp.concatenate(
        [
            jnp.broadcast_to(s_full[None], (plane, s_rows, LANES)),
            jnp.broadcast_to(c_own[:, None], (2, n_col, c_rows, LANES)).reshape(plane, c_rows, LANES),
        ],
        axis=1,
    )
    got2 = lax.all_to_all(send2, ("row", "col"), 0, 0, axis_index_groups=plane_groups)
    linv, gain, after = call(
        factor_kernel,
        (shape(m, m), shape(rows, m), shape(SUB, rows)),
        [VMEM] * 4,
        [
            pltpu.VMEM((nb, nb, LANES, LANES), jnp.float32),
            pltpu.VMEM((nb, nb, LANES, LANES), jnp.float32),
            pltpu.VMEM((nb, rows + SUB, LANES), jnp.float32),
            pltpu.VMEM((LANES, m), jnp.float32),
        ],
        flops=1 << 20,
        name="factor",
    )(got2, obs_values.reshape(nb, LANES), obs_variance.reshape(nb, LANES), mean)
    updated = call(
        update_kernel,
        shape(rows, cols),
        [VMEM] * 4,
        [pltpu.VMEM((cols, m), jnp.float32)],
        flops=1 << 31,
        name="update",
    )(covariance, c_cols, linv, gain)
    return (updated, after[0])


def solution(mesh):
    return jax.shard_map(
        on_device,
        mesh=mesh,
        in_specs=(P("row", "col"), P("row"), P(), P(), P(), P()),
        out_specs=(P("row", "col"), P("row")),
        check_vma=False,
    )
```

time: 167 us -> 160 us (0.958)
  between operations: 0.76 us -> 14.1 us
  starting transfers between devices: 44.5 us -> 32.5 us
  Pallas kernels: 30 us -> 24.3 us
  waiting for transfers between devices: 55.9 us -> 52.2 us
    all_to_all x2 -> x1, waiting for transfers between devices: 37.9 us -> 13.8 us  [on_device(): s_all = lax.all_to_all(s_send, 'row', 0, 0, axis_index_groups=z_groups)]
    all_gather x0 -> x1, waiting for transfers between devices: none -> 20.9 us  [on_device(): c_cols = lax.all_gather(c_tr, 'row')]
    all_to_all x2 -> x1, starting transfers between devices: 24.5 us -> 13.7 us  [on_device(): s_all = lax.all_to_all(s_send, 'row', 0, 0, axis_index_groups=z_groups)]
    ppermute x1 -> x0, starting transfers between devices: 9.03 us -> none  [on_device(): c_other = lax.ppermute(c_z, 'row', [(i, i ^ 1) for i in range(n_row)])]
    all_to_all x1, starting transfers between devices: 10.3 us -> 18.1 us  [on_device(): lax.all_to_all(send2, ('row', 'col'), 0, 0, axis_index_groups=plane_groups)]
    pallas_call x4 -> x3, Pallas kernels: 30 us -> 24.3 us  [the longest x1 17.4 us: on_device(): call(factor_kernel, (shape(m, m), shape(rows, m), shape(SUB, rows)), [VME...]
    unnamed x16 -> x20, local copies, waits for them, and re-layouts: 3.13 us -> 4.95 us
  transfers between devices with their start and end apart: 5 -> 4, of which waited for: 3 -> 3; matrix products, arithmetic and copies ran while one was open for 0% -> 1% of each run, Pallas kernels for 14% -> 11%
where the time goes in v2:
time: 160 us; the launch traced here: 159 us
  waiting for transfers between devices  52.2 us (33%)
  starting transfers between devices  32.5 us (20%)
  blocking collectives  28.5 us (18%)
  Pallas kernels  24.3 us (15%)
  between operations  14.1 us (9%)
  local copies, waits for them, and re-layouts  6.42 us (4%)
    all_to_all x1, blocking collectives, on_device(): lax.all_to_all(send, ('row', 'col'), 0, 0, axis_index_groups=plane_groups)  28.5 us
    all_gather x1, waiting for transfers between devices, on_device(): c_cols = lax.all_gather(c_tr, 'row')  20.9 us
    all_to_all x1, starting transfers between devices, on_device(): lax.all_to_all(send2, ('row', 'col'), 0, 0, axis_index_groups=plane_groups)  18.1 us
    all_to_all x1, waiting for transfers between devices, on_device(): lax.all_to_all(send2, ('row', 'col'), 0, 0, axis_index_groups=plane_groups)  17.5 us
    pallas_call x1, Pallas kernels, on_device(): call(factor_kernel, (shape(m, m), shape(rows, m), shape(SUB, rows)), [VME...  17.4 us
    all_to_all x1, waiting for transfers between devices, on_device(): s_all = lax.all_to_all(s_send, 'row', 0, 0, axis_index_groups=z_groups)  13.8 us
    all_to_all x1, starting transfers between devices, on_device(): s_all = lax.all_to_all(s_send, 'row', 0, 0, axis_index_groups=z_groups)  13.7 us
    unnamed x20, local copies, waits for them, and re-layouts  4.95 us
  transfers between devices with their start and end apart: 4, of which 3 were waited for; matrix products, arithmetic and copies ran while one was open for 1% of the time, Pallas kernels for 11%

profile of v2, /device:TPU:1, one launch (start us, length us, event | category | flops | bytes accessed | tf_op | source)
XLA Modules:
  0.0 159.4 jit_solution(14860416343038788985)
XLA Ops:
  7.2 0.1 pad_add_fusion.at_ref
  7.2 1.0 copy-done
  8.3 0.7 copy-done.2
  9.0 0.7 copy-done.3
  9.7 0.7 copy-done.4
  10.4 3.2 %project.1 = f32[32,72,128]{2,1,0:T(8,128)S(1)} custom-call(s32[2]{0:T(128)S(1)} %pad_add_fusion.at_ref, f32[256,512]{1,0:T(8,128)S(1)} %copy-done, f32[1,256]{1,0:T(1,128)S(1)} %bitcast.8, s32[2,4,256]{2,1,0:T(4,128)S(1)} %copy-done.2, f32[2,4,256]{2,1,0:T(4,128)S(1)} %copy-done.3), custom_call_target="tpu_custom_call" | custom-call | flops 268435456 | bytes 1048576 | tf_op jit(solution)/shard_map/project/pallas_call | solution.py:321
  13.6 28.5 %all_to_all.15 = f32[32,72,128]{2,1,0:T(8,128)S(1)} all-to-all(f32[32,72,128]{2,1,0:T(8,128)S(1)} %project.1), channel_id=1, replica_groups={{0,1,2,3,4,5,6,7,8,9,10,11,12,13,14,15,16,17,18,19,20,21,22,23,24,25,26..., dimensions={0} | all-to-all | bytes 2359296 | tf_op jit(solution)/shard_map/all_to_all | solution.py:337
  42.1 0.1 slice_reduce_fusion
  42.2 0.7 broadcast_in_dim.6
  42.9 13.7 %all-to-all-start.1 = ((f32[16,40,128]{2,1,0:T(8,128)}), f32[16,40,128]{2,1,0:T(8,128)S(1)}, u32[]{:S(2)}, u32[]{:S(2)}) async-start(f32[16,40,128]{2,1,0:T(8,128)} %broadcast_in_dim.6), calls=%async_computation.1 | async-start | bytes 655360 | tf_op jit(solution)/shard_map/all_to_all | solution.py:343
  56.6 0.0 all-gather.3.cloned.1.call-start
  56.7 0.7 collective-permute-start
  57.4 0.6 copy-done.7
  58.0 0.0 all-gather.3.cloned.1.call-update
  58.0 13.8 %all-to-all-done.1 = f32[16,40,128]{2,1,0:T(8,128)S(1)} async-done(((f32[16,40,128]{2,1,0:T(8,128)}), f32[16,40,128]{2,1,0:T(8,128)S(1)}, u32[]{:S(2)}, u32[]{:S(2)}) %all-to-all-start.1) | async-done | bytes 327712 | tf_op jit(solution)/shard_map/all_to_all | solution.py:343
  71.8 0.1 broadcast_in_dim.8
  71.9 1.1 pad_maximum_fusion
  73.0 18.1 %all-to-all-start.2 = ((f32[32,72,128]{2,1,0:T(8,128)}), f32[32,72,128]{2,1,0:T(8,128)S(1)}, u32[]{:S(2)}, u32[]{:S(2)}) async-start(f32[32,72,128]{2,1,0:T(8,128)} %pad_maximum_fusion), calls=%async_computation.2 | async-start | bytes 2359296 | tf_op jit(solution)/shard_map/all_to_all | solution.py:353
  91.2 17.5 %all-to-all-done.2.got_ref = f32[32,72,128]{2,1,0:T(8,128)S(1)} async-done(((f32[32,72,128]{2,1,0:T(8,128)}), f32[32,72,128]{2,1,0:T(8,128)S(1)}, u32[]{:S(2)}, u32[]{:S(2)}) %all-to-all-start.2) | async-done | bytes 1179680 | tf_op jit(solution)/shard_map/all_to_all | solution.py:353
  108.7 17.4 %factor.1 = (f32[512,512]{1,0:T(8,128)S(1)}, f32[256,512]{1,0:T(8,128)S(1)}, f32[8,256]{1,0:T(8,128)S(1)}) custom-call(f32[32,72,128]{2,1,0:T(8,128)S(1)} %all-to-all-done.2.got_ref, f32[4,128]{1,0:T(4,128)S(1)} %reshape.25.values_ref, f32[4,128]{1,0:T(4,128)S(1)} %reshape.26.variance_ref, f32[1,256]{1,0:T(1,128)S(1)} %bitcast.9), custom_call_target="tpu_custom_call" | custom-call | flops 1048576 | bytes 1048576 | tf_op jit(solution)/shard_map/factor/pallas_call | solution.py:354
  126.1 0.6 slice.11
  126.7 20.9 %all-gather.3.cloned.1.call-done = f32[64,32,128]{2,1,0:T(8,128)} async-done(((f32[2,32,128]{2,1,0:T(8,128)}), f32[64,32,128]{2,1,0:T(8,128)}) %all-gather.3.cloned.1.call-update) | async-done | bytes 1048592 | tf_op jit(solution)/shard_map/all_gather | solution.py:344
  147.6 1.2 copy-done.6
  148.9 3.7 %update.1 = f32[256,512]{1,0:T(8,128)} custom-call(f32[256,512]{1,0:T(8,128)S(1)} %copy-done.1, f32[32,2,32,128]{3,2,1,0:T(8,128)S(1)} %bitcast.10, f32[512,512]{1,0:T(8,128)S(1)} %get-tuple-element.5.linv_ref, f32[256,512]{1,0:T(8,128)S(1)} %get-tuple-element.6.gain_ref), custom_call_target="tpu_custom_call" | custom-call | flops 2147483648 | bytes 1048576 | tf_op jit(solution)/shard_map/update/pallas_call | solution.py:367
  (20 shorter events, 0.2 us)
Async XLA Ops:
  7.2 1.0 copy-start
  8.3 0.7 copy-start.2
  9.0 0.7 copy-start.3
  9.7 0.7 copy-start.4
  42.9 28.9 %all-to-all-start.1 = ((f32[16,40,128]{2,1,0:T(8,128)}), f32[16,40,128]{2,1,0:T(8,128)S(1)}, u32[]{:S(2)}, u32[]{:S(2)}) async-start(f32[16,40,128]{2,1,0:T(8,128)} %broadcast_in_dim.6), calls=%async_computation.1 | async-start | bytes 655360 | tf_op jit(solution)/shard_map/all_to_all | solution.py:343
  56.6 91.0 %all-gather.3.cloned.1.call-start = ((), (), s32[]{:S(2)}) async-start(), calls=%async_computation.3 | async-start | bytes 1081344 | tf_op jit(solution)/shard_map/all_gather | solution.py:344
  56.7 0.7 collective-permute-start
  57.4 0.6 copy-start.7
  73.0 18.1 %copy-start.8 = (f32[2,256]{1,0:T(2,128)S(1)}, f32[2,256]{1,0:T(2,128)}, u32[]{:S(2)}) copy-start(f32[2,256]{1,0:T(2,128)} %param.8) | copy-start | bytes 6148
  73.0 18.1 %copy-start.9 = (f32[2,256]{1,0:T(2,128)S(1)}, f32[2,256]{1,0:T(2,128)}, u32[]{:S(2)}) copy-start(f32[2,256]{1,0:T(2,128)} %param.11) | copy-start | bytes 6148
  73.0 35.7 %copy-start.5 = (f32[256]{0:T(256)S(1)}, f32[256]{0:T(256)}, u32[]{:S(2)}) copy-start(f32[256]{0:T(256)} %param.7) | copy-start | bytes 3076
  73.0 35.6 %all-to-all-start.2 = ((f32[32,72,128]{2,1,0:T(8,128)}), f32[32,72,128]{2,1,0:T(8,128)S(1)}, u32[]{:S(2)}, u32[]{:S(2)}) async-start(f32[32,72,128]{2,1,0:T(8,128)} %pad_maximum_fusion), calls=%async_computation.2 | async-start | bytes 2359296 | tf_op jit(solution)/shard_map/all_to_all | solution.py:353
  91.1 56.5 %copy-start.1 = (f32[256,512]{1,0:T(8,128)S(1)}, f32[256,512]{1,0:T(8,128)}, u32[]{:S(2)}) copy-start(f32[256,512]{1,0:T(8,128)} %cov_ref.1) | copy-start | bytes 1572868
  147.6 1.2 copy-start.6
Sparse Core Ops, SparseCore 0:
  59.5 88.0 all-gather.2

commit v3 on v2

--- a/solution.py
+++ b/solution.py
@@ -33,14 +33,15 @@
     return [(i, j) for i in range(n) for j in range(i + 1)]
 
 
-def call(kernel, out_shape, specs, scratch=(), flops=0, name=None):
+def call(kernel, out_shape, specs, scratch=(), flops=0, name=None, aliases=None, limit=LIMIT):
     return pl.pallas_call(
         kernel,
         out_shape=out_shape,
         in_specs=specs,
         out_specs=jax.tree.map(lambda _: VMEM, out_shape),
         scratch_shapes=list(scratch),
-        compiler_params=pltpu.CompilerParams(vmem_limit_bytes=LIMIT),
+        input_output_aliases=aliases or {},
+        compiler_params=pltpu.CompilerParams(vmem_limit_bytes=limit),
         cost_estimate=pl.CostEstimate(flops=flops, bytes_accessed=1 << 20, transcendentals=0),
         name=name,
     )
@@ -187,11 +188,9 @@
     return jnp.concatenate(out, axis=0)
 
 
-def factor_kernel(
-    got_ref, values_ref, variance_ref, mean_ref, linv_ref, gain_ref, after_ref, a_ref, l_ref, e_ref, y_ref
-):
+def prepare(got_ref, values_ref, variance_ref, linv_ref, a_ref, e_ref):
     nb = values_ref.shape[0]
-    rows = gain_ref.shape[0]
+    rows = e_ref.shape[1] - SUB
     low = lower_blocks(nb)
     plane = got_ref.shape[0]
     tiles = len(low) * GROUPS // plane
@@ -223,17 +222,21 @@
                 (LANES, LANES), jnp.float32
             )
 
+
+def factor_steps(begin, end, linv_ref, a_ref, l_ref, e_ref, y_ref):
+    nb = a_ref.shape[0]
+
     def span(i):
         return slice(i * LANES, (i + 1) * LANES)
 
-    def scale(j, i, x):
-        l_ref[j, i] = dot_dims(a_ref[j, i], x, 1, 1)
+    def scale(j, i):
+        l_ref[j, i] = dot_dims(a_ref[j, i], linv_ref[span(i), span(i)], 1, 1)
 
     def reduce(j, k, i):
         a_ref[j, k] = a_ref[j, k] - dot_dims(l_ref[j, i], l_ref[k, i], 1, 1)
 
-    def scale_rows(i, x):
-        e_ref[i] = dot_dims(e_ref[i], x, 1, 1)
+    def scale_rows(i):
+        e_ref[i] = dot_dims(e_ref[i], linv_ref[span(i), span(i)], 1, 1)
 
     def reduce_rows(k, i):
         e_ref[k] = e_ref[k] - dot_dims(e_ref[i], l_ref[k, i], 1, 1)
@@ -250,48 +253,65 @@
     def work(f, *args):
         return lambda: f(*args)
 
-    jobs = []
-    for i in range(nb):
-        x = inverse_factor([a_ref[i, i, g * SUB:(g + 1) * SUB, :] for g in range(GROUPS)], jobs)
-        linv_ref[span(i), span(i)] = x
+    def rest(i):
+        todo = [work(scale, j, i) for j in range(i + 2, nb)]
+        todo += [work(reduce, j, k, i) for k in range(i + 1, nb) for j in range(max(k, i + 2), nb)]
+        todo.append(work(scale_rows, i))
+        todo += [work(reduce_rows, k, i) for k in range(i + 1, nb)]
+        if i > 0:
+            todo.append(work(finish, i))
+        todo.append(work(gather, i + 1))
+        return todo
+
+    for i in range(begin, end):
+        jobs = rest(i - 1) if i > 0 else []
+        linv_ref[span(i), span(i)] = inverse_factor(
+            [a_ref[i, i, g * SUB:(g + 1) * SUB, :] for g in range(GROUPS)], jobs
+        )
         if i + 1 < nb:
-            scale(i + 1, i, x)
+            scale(i + 1, i)
             reduce(i + 1, i + 1, i)
-            for j in range(i + 2, nb):
-                jobs.append(work(scale, j, i, x))
-            for k in range(i + 1, nb):
-                for j in range(max(k, i + 2), nb):
-                    jobs.append(work(reduce, j, k, i))
-            jobs.append(work(scale_rows, i, x))
-            for k in range(i + 1, nb):
-                jobs.append(work(reduce_rows, k, i))
-            if i > 0:
-                jobs.append(work(finish, i))
-            jobs.append(work(gather, i + 1))
         else:
-            scale_rows(i, x)
+            scale_rows(i)
             finish(i)
-    for i in range(nb):
-        gain_ref[:, span(i)] = e_ref[i, 0:rows, :]
+
+
+def early_kernel(got_ref, values_ref, variance_ref, linv_ref, a_ref, l_ref, e_ref, y_ref):
+    prepare(got_ref, values_ref, variance_ref, linv_ref, a_ref, e_ref)
+    factor_steps(0, a_ref.shape[0] - 1, linv_ref, a_ref, l_ref, e_ref, y_ref)
+
+
+def late_kernel(
+    mean_ref, linv_in, a_in, l_in, e_in, y_in, linv_ref, a_ref, l_ref, e_ref, y_ref, after_ref
+):
+    nb = a_ref.shape[0]
+    rows = e_ref.shape[1] - SUB
+    factor_steps(nb - 1, nb, linv_ref, a_ref, l_ref, e_ref, y_ref)
     after = mean_ref[...]
     for i in range(nb):
         after = after + dot_dims(e_ref[i, rows:rows + SUB, :], e_ref[i, 0:rows, :], 1, 1)
     after_ref[...] = after
 
 
-def update_kernel(cov_ref, pieces_ref, linv_ref, gain_ref, out_ref, c_ref):
-    n_row, halves, tall, _ = pieces_ref.shape
-    cols, m = c_ref.shape
+def update_kernel(at_ref, cov_ref, mine_ref, other_ref, linv_ref, e_ref, out_ref, c_ref):
+    n_z, halves, tall, _ = mine_ref.shape
+    rows, cols = cov_ref.shape
+    m = c_ref.shape[1]
     nb = m // LANES
     own = tall // nb
-    for h in range(halves):
-        for r in range(n_row):
-            z, k = divmod(r, 2)
-            at = h * (cols // halves) + (k * (n_row // 2) + z) * own
-            for j in range(nb):
-                c_ref[at:at + own, j * LANES:(j + 1) * LANES] = pieces_ref[r, h, j * own:(j + 1) * own, :]
+    core = lax.rem(at_ref[0], 2)
+    z_here = lax.div(at_ref[0], 2)
+    for ref, k in ((mine_ref, core), (other_ref, 1 - core)):
+        for d in range(n_z):
+            start = pl.multiple_of((k * n_z + lax.bitwise_xor(z_here, d)) * own, own)
+            for h in range(halves):
+                for j in range(nb):
+                    c_ref[pl.ds(start + h * (cols // halves), own), j * LANES:(j + 1) * LANES] = ref[
+                        d, h, j * own:(j + 1) * own, :
+                    ]
     gain_cols = dot_dims(c_ref[...], linv_ref[...], 1, 1)
-    out_ref[...] = cov_ref[...] - dot_dims(gain_ref[...], gain_cols, 1, 1)
+    gain = jnp.concatenate([e_ref[j, 0:rows, :] for j in range(nb)], axis=1)
+    out_ref[...] = cov_ref[...] - dot_dims(gain, gain_cols, 1, 1)
 
 
 def on_device(covariance, state_mean, obs_values, obs_cells, obs_weights, obs_variance):
@@ -333,6 +353,7 @@
         ],
         flops=2 * rows * m * (cols + m),
         name="project",
+        limit=60 * 1024 * 1024,
     )(at, covariance, mean, obs_cells, obs_weights)
     got = lax.all_to_all(send, ("row", "col"), 0, 0, axis_index_groups=plane_groups)
     s_chunk = jnp.sum(got[:, :s_rows], axis=0)
@@ -341,7 +362,6 @@
     s_send = jnp.broadcast_to(s_chunk[None], (n_z, s_rows, LANES))
     c_tr = lax.ppermute(c_own, ("row", "col"), pairs)
     s_all = lax.all_to_all(s_send, "row", 0, 0, axis_index_groups=z_groups)
-    c_cols = lax.all_gather(c_tr, "row")
     s_full = jnp.sum(s_all, axis=0)
     send2 = jnp.concatenate(
         [
@@ -350,28 +370,51 @@
         ],
         axis=1,
     )
+    send2, c_tr = lax.optimization_barrier((send2, c_tr))
     got2 = lax.all_to_all(send2, ("row", "col"), 0, 0, axis_index_groups=plane_groups)
-    linv, gain, after = call(
-        factor_kernel,
-        (shape(m, m), shape(rows, m), shape(SUB, rows)),
-        [VMEM] * 4,
-        [
-            pltpu.VMEM((nb, nb, LANES, LANES), jnp.float32),
-            pltpu.VMEM((nb, nb, LANES, LANES), jnp.float32),
-            pltpu.VMEM((nb, rows + SUB, LANES), jnp.float32),
-            pltpu.VMEM((LANES, m), jnp.float32),
-        ],
-        flops=1 << 20,
-        name="factor",
-    )(got2, obs_values.reshape(nb, LANES), obs_variance.reshape(nb, LANES), mean)
+
+    def partner(x, bit):
+        return lax.ppermute(x, "row", [(i, i ^ bit) for i in range(n_row)])
+
+    pieces = c_tr[None]
+    bits = []
+    while 1 << len(bits) < n_z:
+        bits.append(2 << len(bits))
+    for bit in bits[:0:-1]:
+        theirs = partner(pieces, bit)
+        pieces = jnp.stack([pieces, theirs], axis=1).reshape((-1,) + c_tr.shape)
+    got2, pieces = lax.optimization_barrier((got2, pieces))
+    theirs = partner(pieces, bits[0])
+    state = (
+        shape(m, m),
+        shape(nb, nb, LANES, LANES),
+        shape(nb, nb, LANES, LANES),
+        shape(nb, rows + SUB, LANES),
+        shape(LANES, m),
+    )
+    held = call(early_kernel, state, [VMEM] * 3, flops=1 << 30, name="early")(
+        got2, obs_values.reshape(nb, LANES), obs_variance.reshape(nb, LANES)
+    )
+    held, theirs = lax.optimization_barrier((held, theirs))
+    pieces = jnp.stack([pieces, theirs], axis=1).reshape((-1,) + c_tr.shape)
+    other = partner(pieces, 1)
+    out = call(
+        late_kernel,
+        state + (shape(SUB, rows),),
+        [VMEM] * 6,
+        flops=1 << 30,
+        name="late",
+        aliases={n + 1: n for n in range(len(state))},
+    )(mean, *held)
+    linv, e, after = out[0], out[3], out[5]
     updated = call(
         update_kernel,
         shape(rows, cols),
-        [VMEM] * 4,
+        [SMEM] + [VMEM] * 5,
         [pltpu.VMEM((cols, m), jnp.float32)],
         flops=1 << 31,
         name="update",
-    )(covariance, c_cols, linv, gain)
+    )(at, covariance, pieces, other, linv, e)
     return (updated, after[0])
 
 

time: 160 us -> 146 us (0.912)
  waiting for transfers between devices: 52.2 us -> 36.6 us
  starting transfers between devices: 32.5 us -> 46.7 us
  between operations: 14.1 us -> 0.86 us
  local copies, waits for them, and re-layouts: 6.42 us -> 1.51 us
  Pallas kernels: 24.3 us -> 27.7 us
    ppermute x0 -> x5, waiting for transfers between devices: none -> 22.1 us  [partner(): return lax.ppermute(x, 'row', [(i, i ^ bit) for i in range(n_row)])]
    all_gather x1 -> x0, waiting for transfers between devices: 20.9 us -> none  [on_device(): c_cols = lax.all_gather(c_tr, 'row')]
    all_to_all x1, waiting for transfers between devices: 17.5 us -> 0.01 us  [on_device(): lax.all_to_all(send2, ('row', 'col'), 0, 0, axis_index_groups=plane_groups)]
    ppermute x0 -> x5, starting transfers between devices: none -> 17.2 us  [partner(): return lax.ppermute(x, 'row', [(i, i ^ bit) for i in range(n_row)])]
    unnamed x20 -> x10, local copies, waits for them, and re-layouts: 4.95 us -> 0.03 us
    all_to_all x1, starting transfers between devices: 18.1 us -> 15.9 us  [on_device(): lax.all_to_all(send2, ('row', 'col'), 0, 0, axis_index_groups=plane_groups)]
    pallas_call x1, Pallas kernels: 3.24 us -> 5.4 us  [on_device(): call(project_kernel, shape(plane, chunk, LANES), [SMEM] + [HBM] * 4, [plt...]
    pallas_call x2 -> x3, Pallas kernels: 21.1 us -> 22.3 us  [the longest x1 12.9 us: on_device(): call(early_kernel, state, [VMEM] * 3, flops=1 << 30, name='early')]
  transfers between devices with their start and end apart: 4 -> 8, of which waited for: 3 -> 4; matrix products, arithmetic and copies ran while one was open for 1% -> 1% of each run, Pallas kernels for 11% -> 12%
where the time goes in v3:
time: 146 us; the launch traced here: 145 us
  starting transfers between devices  46.7 us (32%)
  waiting for transfers between devices  36.6 us (25%)
  blocking collectives  29.5 us (20%)
  Pallas kernels  27.7 us (19%)
  other arithmetic  1.94 us (1%)
  local copies, waits for them, and re-layouts  1.51 us (1%)
    all_to_all x1, blocking collectives, on_device(): lax.all_to_all(send, ('row', 'col'), 0, 0, axis_index_groups=plane_groups)  29.5 us
    ppermute x5, waiting for transfers between devices, partner(): return lax.ppermute(x, 'row', [(i, i ^ bit) for i in range(n_row)])  22.1 us
    ppermute x5, starting transfers between devices, partner(): return lax.ppermute(x, 'row', [(i, i ^ bit) for i in range(n_row)])  17.2 us
    all_to_all x1, starting transfers between devices, on_device(): lax.all_to_all(send2, ('row', 'col'), 0, 0, axis_index_groups=plane_groups)  15.9 us
    all_to_all x1, waiting for transfers between devices, on_device(): s_all = lax.all_to_all(s_send, 'row', 0, 0, axis_index_groups=z_groups)  14.5 us
    all_to_all x1, starting transfers between devices, on_device(): s_all = lax.all_to_all(s_send, 'row', 0, 0, axis_index_groups=z_groups)  12.9 us
    pallas_call x1, Pallas kernels, on_device(): call(early_kernel, state, [VMEM] * 3, flops=1 << 30, name='early')  12.9 us
    pallas_call x1, Pallas kernels, on_device(): call(project_kernel, shape(plane, chunk, LANES), [SMEM] + [HBM] * 4, [plt...  5.4 us
  transfers between devices with their start and end apart: 8, of which 4 were waited for; matrix products, arithmetic and copies ran while one was open for 1% of the time, Pallas kernels for 12%

profile of v3, /device:TPU:1, one launch (start us, length us, event | category | flops | bytes accessed | tf_op | source)
XLA Modules:
  0.0 144.8 jit_solution(4875101554067408341)
XLA Ops:
  0.6 0.7 pad_add_fusion.at_ref
  1.3 5.4 %project.1 = f32[32,72,128]{2,1,0:T(8,128)} custom-call(s32[2]{0:T(128)} %pad_add_fusion.at_ref, f32[256,512]{1,0:T(8,128)} %cov_ref.1, f32[1,256]{1,0:T(1,128)} %bitcast.26, s32[2,4,256]{2,1,0:T(4,128)} %cells_in.1, f32[2,4,256]{2,1,0:T(4,128)} %weights_in.1), custom_call_target="tpu_custom_call" | custom-call | flops 268435456 | bytes 1048576 | tf_op jit(solution)/shard_map/project/pallas_call | solution.py:341
  6.7 29.5 %all_to_all.15 = f32[32,72,128]{2,1,0:T(8,128)S(1)} all-to-all(f32[32,72,128]{2,1,0:T(8,128)} %project.1), channel_id=1, replica_groups={{0,1,2,3,4,5,6,7,8,9,10,11,12,13,14,15,16,17,18,19,20,21,22,23,24,25,26..., dimensions={0} | all-to-all | bytes 2359296 | tf_op jit(solution)/shard_map/all_to_all | solution.py:358
  36.2 0.1 slice_reduce_fusion
  36.2 0.7 broadcast_in_dim.8
  37.0 12.9 %all-to-all-start.1 = ((f32[16,40,128]{2,1,0:T(8,128)}), f32[16,40,128]{2,1,0:T(8,128)S(1)}, u32[]{:S(2)}, u32[]{:S(2)}) async-start(f32[16,40,128]{2,1,0:T(8,128)} %broadcast_in_dim.8), calls=%async_computation.1 | async-start | bytes 655360 | tf_op jit(solution)/shard_map/all_to_all | solution.py:364
  49.9 0.7 collective-permute-start
  50.6 14.5 %all-to-all-done.1 = f32[16,40,128]{2,1,0:T(8,128)S(1)} async-done(((f32[16,40,128]{2,1,0:T(8,128)}), f32[16,40,128]{2,1,0:T(8,128)S(1)}, u32[]{:S(2)}, u32[]{:S(2)}) %all-to-all-start.1) | async-done | bytes 327712 | tf_op jit(solution)/shard_map/all_to_all | solution.py:364
  65.1 0.1 broadcast_in_dim.10
  65.2 1.1 pad_maximum_fusion
  66.3 15.9 %all-to-all-start.2 = ((f32[32,72,128]{2,1,0:T(8,128)}), f32[32,72,128]{2,1,0:T(8,128)S(1)}, u32[]{:S(2)}, u32[]{:S(2)}) async-start(f32[32,72,128]{2,1,0:T(8,128)} %pad_maximum_fusion), calls=%async_computation.2 | async-start | bytes 2359296 | tf_op jit(solution)/shard_map/all_to_all | solution.py:374
  82.2 0.0 copy-start.3
  82.3 5.5 %collective-permute-start.1 = (f32[1,2,32,128]{3,2,1,0:T(8,128)S(1)}, f32[1,2,32,128]{3,2,1,0:T(8,128)S(1)}, u32[]{:S(2)}, u32[]{:S(2)}) collective-permute-start(f32[1,2,32,128]{3,2,1,0:T(8,128)S(1)} %bitcast.36), channel_id=1, source_target_pairs={{0,256},{16,272},{32,288},{48,304},{64,320},{80,336},{96,352},{112... | collective-permute-start | bytes 98312 | tf_op jit(solution)/shard_map/ppermute | solution.py:377
  87.8 7.8 %collective-permute-done.1 = f32[1,2,32,128]{3,2,1,0:T(8,128)S(1)} collective-permute-done((f32[1,2,32,128]{3,2,1,0:T(8,128)S(1)}, f32[1,2,32,128]{3,2,1,0:T(8,128)S(1)}, u32[]{:S(2)}, u32[]{:S(2)}) %collective-permute-start.1) | collective-permute-done | bytes 32800 | tf_op jit(solution)/shard_map/ppermute | solution.py:377
  95.6 3.3 %collective-permute-start.2 = (f32[2,2,32,128]{3,2,1,0:T(8,128)S(1)}, f32[2,2,32,128]{3,2,1,0:T(8,128)S(1)}, u32[]{:S(2)}, u32[]{:S(2)}) collective-permute-start(f32[2,2,32,128]{3,2,1,0:T(8,128)S(1)} %get-tuple-element.39), channel_id=1, source_target_pairs={{0,128},{16,144},{32,160},{48,176},{64,192},{80,208},{96,224},{112... | collective-permute-start | bytes 196616 | tf_op jit(solution)/shard_map/ppermute | solution.py:377
  98.9 9.6 %collective-permute-done.2 = f32[2,2,32,128]{3,2,1,0:T(8,128)S(1)} collective-permute-done((f32[2,2,32,128]{3,2,1,0:T(8,128)S(1)}, f32[2,2,32,128]{3,2,1,0:T(8,128)S(1)}, u32[]{:S(2)}, u32[]{:S(2)}) %collective-permute-start.2) | collective-permute-done | bytes 65568 | tf_op jit(solution)/shard_map/ppermute | solution.py:377
  108.5 1.9 %collective-permute-start.3 = (f32[4,2,32,128]{3,2,1,0:T(8,128)S(1)}, f32[4,2,32,128]{3,2,1,0:T(8,128)S(1)}, u32[]{:S(2)}, u32[]{:S(2)}) collective-permute-start(f32[4,2,32,128]{3,2,1,0:T(8,128)S(1)} %bitcast.31), channel_id=1, source_target_pairs={{0,64},{16,80},{32,96},{48,112},{64,0},{80,16},{96,32},{112,48},{1... | collective-permute-start | bytes 393224 | tf_op jit(solution)/shard_map/ppermute | solution.py:377
  110.5 4.7 %collective-permute-done.3 = f32[4,2,32,128]{3,2,1,0:T(8,128)S(1)} collective-permute-done((f32[4,2,32,128]{3,2,1,0:T(8,128)S(1)}, f32[4,2,32,128]{3,2,1,0:T(8,128)S(1)}, u32[]{:S(2)}, u32[]{:S(2)}) %collective-permute-start.3) | collective-permute-done | bytes 131104 | tf_op jit(solution)/shard_map/ppermute | solution.py:377
  115.2 2.1 %collective-permute-start.4 = (f32[8,2,32,128]{3,2,1,0:T(8,128)S(1)}, f32[8,2,32,128]{3,2,1,0:T(8,128)S(1)}, u32[]{:S(2)}, u32[]{:S(2)}) collective-permute-start(f32[8,2,32,128]{3,2,1,0:T(8,128)S(1)} %bitcast.29), channel_id=1, source_target_pairs={{0,32},{16,48},{32,0},{48,16},{64,96},{80,112},{96,64},{112,80},{1... | collective-permute-start | bytes 786440 | tf_op jit(solution)/shard_map/ppermute | solution.py:377
  117.4 12.9 %early.1 = (f32[512,512]{1,0:T(8,128)S(1)}, f32[4,4,128,128]{3,2,1,0:T(8,128)S(1)}, f32[4,4,128,128]{3,2,1,0:T(8,128)S(1)}, f32[4,264,128]{2,1,0:T(8,128)S(1)}, f32[128,512]{1,0:T(8,128)S(1)}) custom-call(f32[32,72,128]{2,1,0:T(8,128)S(1)} %all-to-all-done.2.got_ref, f32[4,128]{1,0:T(4,128)S(1)} %reshape.40.values_ref, f32[4,128]{1,0:T(4,128)S(1)} %reshape.41.variance_ref), custom_call_target="tpu_custom_call" | custom-call | flops 1073741824 | bytes 1048576 | tf_op jit(solution)/shard_map/early/pallas_call | solution.py:395
  130.4 4.4 %collective-permute-start.5 = (f32[16,2,32,128]{3,2,1,0:T(8,128)S(1)}, f32[16,2,32,128]{3,2,1,0:T(8,128)S(1)}, u32[]{:S(2)}, u32[]{:S(2)}) collective-permute-start(f32[16,2,32,128]{3,2,1,0:T(8,128)S(1)} %bitcast.24), channel_id=1, source_target_pairs={{0,16},{16,0},{32,48},{48,32},{64,80},{80,64},{96,112},{112,96},{1... | collective-permute-start | bytes 1572872 | tf_op jit(solution)/shard_map/ppermute | solution.py:377
  134.8 5.1 %late.1 = (f32[512,512]{1,0:T(8,128)S(1)}, f32[4,4,128,128]{3,2,1,0:T(8,128)S(1)}, f32[4,4,128,128]{3,2,1,0:T(8,128)S(1)}, f32[4,264,128]{2,1,0:T(8,128)S(1)}, f...) custom-call(f32[1,256]{1,0:T(1,128)S(1)} %bitcast.27, ...), custom_call_target="tpu_custom_call", output_to_operand_aliasing={{0}: (1, {}), {1}: (2, {}), {2}: (3, {}), {3}: (4, {}), {4}... | custom-call | flops 1073741824 | bytes 1048576 | tf_op jit(solution)/shard_map/late/pallas_call | solution.py:401
  139.9 0.6 slice.11
  140.5 4.3 %update.1 = f32[256,512]{1,0:T(8,128)} custom-call(s32[2]{0:T(128)S(1)} %copy-done.2, f32[256,512]{1,0:T(8,128)S(1)} %copy-done, f32[16,2,32,128]{3,2,1,0:T(8,128)S(1)} %bitcast.25, f32[16,2,32,128]{3,2,1,0:T(8,128)S(1)} %collective-permute-done.5.other_ref, f32[512,512]{1,0:T(8,128)S(1)} %get-tuple-element.35.linv_ref, ...), custom_call_target="tpu_custom_call" | custom-call | flops 2147483648 | bytes 1048576 | tf_op jit(solution)/shard_map/update/pallas_call | solution.py:410
  (23 shorter events, 0.3 us)
Async XLA Ops:
  37.0 28.1 %all-to-all-start.1 = ((f32[16,40,128]{2,1,0:T(8,128)}), f32[16,40,128]{2,1,0:T(8,128)S(1)}, u32[]{:S(2)}, u32[]{:S(2)}) async-start(f32[16,40,128]{2,1,0:T(8,128)} %broadcast_in_dim.8), calls=%async_computation.1 | async-start | bytes 655360 | tf_op jit(solution)/shard_map/all_to_all | solution.py:364
  49.9 16.4 %collective-permute-start = (f32[2,32,128]{2,1,0:T(8,128)S(1)}, f32[2,32,128]{2,1,0:T(8,128)S(1)}, u32[]{:S(2)}, u32[]{:S(2)}) collective-permute-start(f32[2,32,128]{2,1,0:T(8,128)S(1)} %bitcast_reduce_fusion), channel_id=1, source_target_pairs={{0,0},{1,32},{2,64},{3,96},{4,128},{5,160},{6,192},{7,224},{8,256}... | collective-permute-start | bytes 98312 | tf_op jit(solution)/shard_map/ppermute | solution.py:363
  66.3 48.8 %all-to-all-start.2 = ((f32[32,72,128]{2,1,0:T(8,128)}), f32[32,72,128]{2,1,0:T(8,128)S(1)}, u32[]{:S(2)}, u32[]{:S(2)}) async-start(f32[32,72,128]{2,1,0:T(8,128)} %pad_maximum_fusion), calls=%async_computation.2 | async-start | bytes 2359296 | tf_op jit(solution)/shard_map/all_to_all | solution.py:374
  82.2 35.1 %copy-start.3 = (f32[2,256]{1,0:T(2,128)S(1)}, f32[2,256]{1,0:T(2,128)}, u32[]{:S(2)}) copy-start(f32[2,256]{1,0:T(2,128)} %param.8) | copy-start | bytes 6148
  82.2 35.1 %copy-start.4 = (f32[2,256]{1,0:T(2,128)S(1)}, f32[2,256]{1,0:T(2,128)}, u32[]{:S(2)}) copy-start(f32[2,256]{1,0:T(2,128)} %param.11) | copy-start | bytes 6148
  82.3 13.4 %collective-permute-start.1 = (f32[1,2,32,128]{3,2,1,0:T(8,128)S(1)}, f32[1,2,32,128]{3,2,1,0:T(8,128)S(1)}, u32[]{:S(2)}, u32[]{:S(2)}) collective-permute-start(f32[1,2,32,128]{3,2,1,0:T(8,128)S(1)} %bitcast.36), channel_id=1, source_target_pairs={{0,256},{16,272},{32,288},{48,304},{64,320},{80,336},{96,352},{112... | collective-permute-start | bytes 98312 | tf_op jit(solution)/shard_map/ppermute | solution.py:377
  95.6 12.9 %collective-permute-start.2 = (f32[2,2,32,128]{3,2,1,0:T(8,128)S(1)}, f32[2,2,32,128]{3,2,1,0:T(8,128)S(1)}, u32[]{:S(2)}, u32[]{:S(2)}) collective-permute-start(f32[2,2,32,128]{3,2,1,0:T(8,128)S(1)} %get-tuple-element.39), channel_id=1, source_target_pairs={{0,128},{16,144},{32,160},{48,176},{64,192},{80,208},{96,224},{112... | collective-permute-start | bytes 196616 | tf_op jit(solution)/shard_map/ppermute | solution.py:377
  108.5 6.6 %collective-permute-start.3 = (f32[4,2,32,128]{3,2,1,0:T(8,128)S(1)}, f32[4,2,32,128]{3,2,1,0:T(8,128)S(1)}, u32[]{:S(2)}, u32[]{:S(2)}) collective-permute-start(f32[4,2,32,128]{3,2,1,0:T(8,128)S(1)} %bitcast.31), channel_id=1, source_target_pairs={{0,64},{16,80},{32,96},{48,112},{64,0},{80,16},{96,32},{112,48},{1... | collective-permute-start | bytes 393224 | tf_op jit(solution)/shard_map/ppermute | solution.py:377
  115.2 15.1 %collective-permute-start.4 = (f32[8,2,32,128]{3,2,1,0:T(8,128)S(1)}, f32[8,2,32,128]{3,2,1,0:T(8,128)S(1)}, u32[]{:S(2)}, u32[]{:S(2)}) collective-permute-start(f32[8,2,32,128]{3,2,1,0:T(8,128)S(1)} %bitcast.29), channel_id=1, source_target_pairs={{0,32},{16,48},{32,0},{48,16},{64,96},{80,112},{96,64},{112,80},{1... | collective-permute-start | bytes 786440 | tf_op jit(solution)/shard_map/ppermute | solution.py:377
  117.3 17.4 %copy-start.1 = (f32[256]{0:T(256)S(1)}, f32[256]{0:T(256)}, u32[]{:S(2)}) copy-start(f32[256]{0:T(256)} %param.7) | copy-start | bytes 3076
  130.3 10.2 %copy-start = (f32[256,512]{1,0:T(8,128)S(1)}, f32[256,512]{1,0:T(8,128)}, u32[]{:S(2)}) copy-start(f32[256,512]{1,0:T(8,128)} %cov_ref.1) | copy-start | bytes 1572868
  130.4 10.2 %copy-start.2 = (s32[2]{0:T(128)S(1)}, s32[2]{0:T(128)}, u32[]{:S(2)}) copy-start(s32[2]{0:T(128)} %pad_add_fusion.at_ref) | copy-start | bytes 28
  130.4 10.2 %collective-permute-start.5 = (f32[16,2,32,128]{3,2,1,0:T(8,128)S(1)}, f32[16,2,32,128]{3,2,1,0:T(8,128)S(1)}, u32[]{:S(2)}, u32[]{:S(2)}) collective-permute-start(f32[16,2,32,128]{3,2,1,0:T(8,128)S(1)} %bitcast.24), channel_id=1, source_target_pairs={{0,16},{16,0},{32,48},{48,32},{64,80},{80,64},{96,112},{112,96},{1... | collective-permute-start | bytes 1572872 | tf_op jit(solution)/shard_map/ppermute | solution.py:377

commit v4 on v3

--- a/solution.py
+++ b/solution.py
@@ -190,28 +190,22 @@
 
 def prepare(got_ref, values_ref, variance_ref, linv_ref, a_ref, e_ref):
     nb = values_ref.shape[0]
-    rows = e_ref.shape[1] - SUB
     low = lower_blocks(nb)
     plane = got_ref.shape[0]
     tiles = len(low) * GROUPS // plane
-    own = rows // plane
     for n, (i, j) in enumerate(low):
         for g in range(GROUPS):
             q = n * GROUPS + g
             a_ref[i, j, g * SUB:(g + 1) * SUB, :] = got_ref[
                 q // tiles, (q % tiles) * SUB:(q % tiles + 1) * SUB, :
             ]
-    for i in range(plane):
-        for j in range(nb):
-            at = tiles * SUB + j * own
-            e_ref[j, i * own:(i + 1) * own, :] = got_ref[i, at:at + own, :]
     r_io = lax.broadcasted_iota(jnp.int32, (LANES, LANES), 0)
     l_io = lax.broadcasted_iota(jnp.int32, (LANES, LANES), 1)
     lane = lax.broadcasted_iota(jnp.int32, (SUB, LANES), 1)
     for i in range(nb):
         first = a_ref[i, i, 0:SUB, :]
         pred = jnp.where(lane == 0, wide(first[1:2, LANES - 1:LANES]), wide(first[0:1, :]))
-        e_ref[i, rows:rows + SUB, :] = wide(values_ref[i:i + 1, :]) - pred
+        e_ref[i] = wide(values_ref[i:i + 1, :]) - pred
         d = a_ref[i, i]
         below = jnp.where(r_io > l_io, d, 0.0)
         diag = jnp.where(r_io == l_io, d + variance_ref[i:i + 1, :], 0.0)
@@ -276,42 +270,53 @@
             finish(i)
 
 
-def early_kernel(got_ref, values_ref, variance_ref, linv_ref, a_ref, l_ref, e_ref, y_ref):
+def factor_kernel(got_ref, values_ref, variance_ref, linv_ref, e_ref, a_ref, l_ref, y_ref):
     prepare(got_ref, values_ref, variance_ref, linv_ref, a_ref, e_ref)
-    factor_steps(0, a_ref.shape[0] - 1, linv_ref, a_ref, l_ref, e_ref, y_ref)
-
-
-def late_kernel(
-    mean_ref, linv_in, a_in, l_in, e_in, y_in, linv_ref, a_ref, l_ref, e_ref, y_ref, after_ref
-):
-    nb = a_ref.shape[0]
-    rows = e_ref.shape[1] - SUB
-    factor_steps(nb - 1, nb, linv_ref, a_ref, l_ref, e_ref, y_ref)
-    after = mean_ref[...]
+    factor_steps(0, a_ref.shape[0], linv_ref, a_ref, l_ref, e_ref, y_ref)
+
+
+def gain_kernel(r_ref, mine_ref, linv_ref, e_ref, mean_ref, gain_ref, cols_ref, after_ref, c_ref):
+    plane = r_ref.shape[0]
+    rows, m = gain_ref.shape
+    own = rows // plane
+    nb = m // LANES
+    skip = r_ref.shape[1] - nb * own
+    arrange(mine_ref, c_ref)
+    cols_ref[...] = dot_dims(c_ref[...], linv_ref[...], 1, 1)
+    for i in range(plane):
+        for j in range(nb):
+            at = skip + j * own
+            c_ref[i * own:(i + 1) * own, j * LANES:(j + 1) * LANES] = r_ref[i, at:at + own, :]
+    gain = dot_dims(c_ref[...], linv_ref[...], 1, 1)
+    gain_ref[...] = gain
+    after = jnp.broadcast_to(mean_ref[...], (SUB, rows))
     for i in range(nb):
-        after = after + dot_dims(e_ref[i, rows:rows + SUB, :], e_ref[i, 0:rows, :], 1, 1)
-    after_ref[...] = after
-
-
-def update_kernel(at_ref, cov_ref, mine_ref, other_ref, linv_ref, e_ref, out_ref, c_ref):
-    n_z, halves, tall, _ = mine_ref.shape
-    rows, cols = cov_ref.shape
-    m = c_ref.shape[1]
-    nb = m // LANES
+        after = after + dot_dims(e_ref[i], gain[:, i * LANES:(i + 1) * LANES], 1, 1)
+    after_ref[...] = after[0:1]
+
+
+def arrange(pieces_ref, c_ref):
+    n_z, halves, tall, _ = pieces_ref.shape
+    nb = c_ref.shape[1] // LANES
     own = tall // nb
+    for h in range(halves):
+        for z in range(n_z):
+            at = (h * n_z + z) * own
+            for j in range(nb):
+                c_ref[at:at + own, j * LANES:(j + 1) * LANES] = pieces_ref[z, h, j * own:(j + 1) * own, :]
+
+
+def update_kernel(at_ref, cov_ref, other_ref, mine_ref, linv_ref, gain_ref, out_ref, c_ref, g_ref):
+    halves = other_ref.shape[1]
+    part = c_ref.shape[0] // halves
     core = lax.rem(at_ref[0], 2)
-    z_here = lax.div(at_ref[0], 2)
-    for ref, k in ((mine_ref, core), (other_ref, 1 - core)):
-        for d in range(n_z):
-            start = pl.multiple_of((k * n_z + lax.bitwise_xor(z_here, d)) * own, own)
-            for h in range(halves):
-                for j in range(nb):
-                    c_ref[pl.ds(start + h * (cols // halves), own), j * LANES:(j + 1) * LANES] = ref[
-                        d, h, j * own:(j + 1) * own, :
-                    ]
-    gain_cols = dot_dims(c_ref[...], linv_ref[...], 1, 1)
-    gain = jnp.concatenate([e_ref[j, 0:rows, :] for j in range(nb)], axis=1)
-    out_ref[...] = cov_ref[...] - dot_dims(gain, gain_cols, 1, 1)
+    arrange(other_ref, c_ref)
+    theirs = dot_dims(c_ref[...], linv_ref[...], 1, 1)
+    for h in range(halves):
+        for k, block in ((core, mine_ref[h * part:(h + 1) * part, :]), (1 - core, theirs[h * part:(h + 1) * part])):
+            start = pl.multiple_of((2 * h + k) * part, part)
+            g_ref[pl.ds(start, part), :] = block
+    out_ref[...] = cov_ref[...] - dot_dims(gain_ref[...], g_ref[...], 1, 1)
 
 
 def on_device(covariance, state_mean, obs_values, obs_cells, obs_weights, obs_variance):
@@ -359,63 +364,55 @@
     s_chunk = jnp.sum(got[:, :s_rows], axis=0)
     c_own = jnp.sum(got[:, s_rows:].reshape(2, n_col, c_rows, LANES), axis=1)
 
-    s_send = jnp.broadcast_to(s_chunk[None], (n_z, s_rows, LANES))
+    s_send, c_own = lax.optimization_barrier(
+        (jnp.broadcast_to(s_chunk[None], (n_z, s_rows, LANES)), c_own)
+    )
+    s_all = lax.all_to_all(s_send, "row", 0, 0, axis_index_groups=z_groups)
+    s_all, c_own = lax.optimization_barrier((s_all, c_own))
     c_tr = lax.ppermute(c_own, ("row", "col"), pairs)
-    s_all = lax.all_to_all(s_send, "row", 0, 0, axis_index_groups=z_groups)
-    s_full = jnp.sum(s_all, axis=0)
     send2 = jnp.concatenate(
         [
-            jnp.broadcast_to(s_full[None], (plane, s_rows, LANES)),
+            jnp.broadcast_to(jnp.sum(s_all, axis=0)[None], (plane, s_rows, LANES)),
             jnp.broadcast_to(c_own[:, None], (2, n_col, c_rows, LANES)).reshape(plane, c_rows, LANES),
         ],
         axis=1,
     )
-    send2, c_tr = lax.optimization_barrier((send2, c_tr))
     got2 = lax.all_to_all(send2, ("row", "col"), 0, 0, axis_index_groups=plane_groups)
-
-    def partner(x, bit):
-        return lax.ppermute(x, "row", [(i, i ^ bit) for i in range(n_row)])
-
-    pieces = c_tr[None]
-    bits = []
-    while 1 << len(bits) < n_z:
-        bits.append(2 << len(bits))
-    for bit in bits[:0:-1]:
-        theirs = partner(pieces, bit)
-        pieces = jnp.stack([pieces, theirs], axis=1).reshape((-1,) + c_tr.shape)
-    got2, pieces = lax.optimization_barrier((got2, pieces))
-    theirs = partner(pieces, bits[0])
-    state = (
-        shape(m, m),
-        shape(nb, nb, LANES, LANES),
-        shape(nb, nb, LANES, LANES),
-        shape(nb, rows + SUB, LANES),
-        shape(LANES, m),
-    )
-    held = call(early_kernel, state, [VMEM] * 3, flops=1 << 30, name="early")(
-        got2, obs_values.reshape(nb, LANES), obs_variance.reshape(nb, LANES)
-    )
-    held, theirs = lax.optimization_barrier((held, theirs))
-    pieces = jnp.stack([pieces, theirs], axis=1).reshape((-1,) + c_tr.shape)
-    other = partner(pieces, 1)
-    out = call(
-        late_kernel,
-        state + (shape(SUB, rows),),
-        [VMEM] * 6,
-        flops=1 << 30,
-        name="late",
-        aliases={n + 1: n for n in range(len(state))},
-    )(mean, *held)
-    linv, e, after = out[0], out[3], out[5]
+    got2, c_tr = lax.optimization_barrier((got2, c_tr))
+    c_z = lax.all_to_all(
+        jnp.broadcast_to(c_tr[None], (n_z,) + c_tr.shape), "row", 0, 0, axis_index_groups=z_groups
+    )
+    linv, white = call(
+        factor_kernel,
+        (shape(m, m), shape(nb, SUB, LANES)),
+        [VMEM] * 3,
+        [
+            pltpu.VMEM((nb, nb, LANES, LANES), jnp.float32),
+            pltpu.VMEM((nb, nb, LANES, LANES), jnp.float32),
+            pltpu.VMEM((LANES, m), jnp.float32),
+        ],
+        flops=1 << 20,
+        name="factor",
+    )(got2, obs_values.reshape(nb, LANES), obs_variance.reshape(nb, LANES))
+    c_z, linv = lax.optimization_barrier((c_z, linv))
+    other = lax.ppermute(c_z, "row", [(i, i ^ 1) for i in range(n_row)])
+    gain, gain_cols, after = call(
+        gain_kernel,
+        (shape(rows, m), shape(cols // 2, m), shape(1, rows)),
+        [VMEM] * 5,
+        [pltpu.VMEM((rows, m), jnp.float32)],
+        flops=1 << 31,
+        name="gain",
+    )(got2, c_z, linv, white, mean)
     updated = call(
         update_kernel,
         shape(rows, cols),
         [SMEM] + [VMEM] * 5,
-        [pltpu.VMEM((cols, m), jnp.float32)],
+        [pltpu.VMEM((cols // 2, m), jnp.float32), pltpu.VMEM((cols, m), jnp.float32)],
         flops=1 << 31,
         name="update",
-    )(at, covariance, pieces, other, linv, e)
-    return (updated, after[0])
+    )(at, covariance, other, gain_cols, linv, gain)
+    return (updated, after.reshape(rows))
 
 
 def solution(mesh):

time: 146 us -> 146 us (level)
  blocking collectives: 29.5 us -> 57.4 us
  starting transfers between devices: 46.7 us -> 30.9 us
  waiting for transfers between devices: 36.6 us -> 23.8 us
  Pallas kernels: 27.7 us -> 29.2 us
    all_to_all x0 -> x1, blocking collectives: none -> 27.9 us  [on_device(): s_all = lax.all_to_all(s_send, 'row', 0, 0, axis_index_groups=z_groups)]
    ppermute x5 -> x1, waiting for transfers between devices: 22.1 us -> 0.01 us  [on_device(): other = lax.ppermute(c_z, 'row', [(i, i ^ 1) for i in range(n_row)])]
    all_to_all x1, waiting for transfers between devices: 0.01 us -> 18 us  [on_device(): lax.all_to_all(send2, ('row', 'col'), 0, 0, axis_index_groups=plane_groups)]
    all_to_all x1, waiting for transfers between devices: 14.5 us -> 5.87 us  [on_device(): lax.all_to_all(jnp.broadcast_to(c_tr[None], (n_z,) + c_tr.shape), 'row',...]
    ppermute x5 -> x1, starting transfers between devices: 17.2 us -> 8.84 us  [on_device(): other = lax.ppermute(c_z, 'row', [(i, i ^ 1) for i in range(n_row)])]
    all_to_all x1, starting transfers between devices: 15.9 us -> 10.2 us  [on_device(): lax.all_to_all(send2, ('row', 'col'), 0, 0, axis_index_groups=plane_groups)]
    pallas_call x2, Pallas kernels: 18.1 us -> 20.2 us  [the longest x1 16.7 us: on_device(): call(factor_kernel, (shape(m, m), shape(nb, SUB, LANES)), [VMEM] * 3, [pl...]
    all_to_all x1, starting transfers between devices: 12.9 us -> 11.2 us  [on_device(): lax.all_to_all(jnp.broadcast_to(c_tr[None], (n_z,) + c_tr.shape), 'row',...]
  transfers between devices with their start and end apart: 8 -> 4, of which waited for: 4 -> 2; matrix products, arithmetic and copies ran while one was open for 1% -> 0% of each run, Pallas kernels for 12% -> 14%
where the time goes in v4:
time: 146 us; the launch traced here: 145 us
  blocking collectives  57.4 us (39%)
  starting transfers between devices  30.9 us (21%)
  Pallas kernels  29.2 us (20%)
  waiting for transfers between devices  23.8 us (16%)
  other arithmetic  1.87 us (1%)
    all_to_all x1, blocking collectives, on_device(): lax.all_to_all(send, ('row', 'col'), 0, 0, axis_index_groups=plane_groups)  29.5 us
    all_to_all x1, blocking collectives, on_device(): s_all = lax.all_to_all(s_send, 'row', 0, 0, axis_index_groups=z_groups)  27.9 us
    all_to_all x1, waiting for transfers between devices, on_device(): lax.all_to_all(send2, ('row', 'col'), 0, 0, axis_index_groups=plane_groups)  18 us
    pallas_call x1, Pallas kernels, on_device(): call(factor_kernel, (shape(m, m), shape(nb, SUB, LANES)), [VMEM] * 3, [pl...  16.7 us
    all_to_all x1, starting transfers between devices, on_device(): lax.all_to_all(jnp.broadcast_to(c_tr[None], (n_z,) + c_tr.shape), 'row',...  11.2 us
    all_to_all x1, starting transfers between devices, on_device(): lax.all_to_all(send2, ('row', 'col'), 0, 0, axis_index_groups=plane_groups)  10.2 us
    ppermute x1, starting transfers between devices, on_device(): other = lax.ppermute(c_z, 'row', [(i, i ^ 1) for i in range(n_row)])  8.84 us
    all_to_all x1, waiting for transfers between devices, on_device(): lax.all_to_all(jnp.broadcast_to(c_tr[None], (n_z,) + c_tr.shape), 'row',...  5.87 us
  transfers between devices with their start and end apart: 4, of which 2 were waited for; matrix products, arithmetic and copies ran while one was open for 0% of the time, Pallas kernels for 14%

profile of v4, /device:TPU:1, one launch (start us, length us, event | category | flops | bytes accessed | tf_op | source)
XLA Modules:
  0.0 145.0 jit_solution(329092735951180775)
XLA Ops:
  0.6 0.7 pad_add_fusion.at_ref
  1.3 5.4 %project.1 = f32[32,72,128]{2,1,0:T(8,128)} custom-call(s32[2]{0:T(128)} %pad_add_fusion.at_ref, f32[256,512]{1,0:T(8,128)} %cov_ref.1, f32[1,256]{1,0:T(1,128)} %bitcast.7, s32[2,4,256]{2,1,0:T(4,128)} %cells_in.1, f32[2,4,256]{2,1,0:T(4,128)} %weights_in.1), custom_call_target="tpu_custom_call" | custom-call | flops 268435456 | bytes 1048576 | tf_op jit(solution)/shard_map/project/pallas_call | solution.py:346
  6.7 29.5 %all_to_all.20 = f32[32,72,128]{2,1,0:T(8,128)S(1)} all-to-all(f32[32,72,128]{2,1,0:T(8,128)} %project.1), channel_id=1, replica_groups={{0,1,2,3,4,5,6,7,8,9,10,11,12,13,14,15,16,17,18,19,20,21,22,23,24,25,26..., dimensions={0} | all-to-all | bytes 2359296 | tf_op jit(solution)/shard_map/all_to_all | solution.py:363
  36.2 0.1 slice_reduce_fusion
  36.3 27.9 %all_to_all.21 = f32[16,40,128]{2,1,0:T(8,128)S(1)} all-to-all(f32[16,40,128]{2,1,0:T(8,128)S(1)} %broadcast_in_dim.8), channel_id=1, replica_groups={{0,32,64,96,128,160,192,224,256,288,320,352,384,416,448,480},{16,48,80,..., dimensions={0} | all-to-all | bytes 655360 | tf_op jit(solution)/shard_map/all_to_all | solution.py:370
  64.2 0.1 broadcast_in_dim.10
  64.3 1.1 pad_maximum_fusion
  65.4 10.2 %all-to-all-start.2 = ((f32[32,72,128]{2,1,0:T(8,128)}), f32[32,72,128]{2,1,0:T(8,128)S(1)}, u32[]{:S(2)}, u32[]{:S(2)}) async-start(f32[32,72,128]{2,1,0:T(8,128)} %pad_maximum_fusion), calls=%async_computation.2 | async-start | bytes 2359296 | tf_op jit(solution)/shard_map/all_to_all | solution.py:380
  75.7 0.0 copy-start.3
  75.7 0.0 copy-start.4
  75.7 0.7 collective-permute-start
  76.4 0.0 collective-permute-done
  76.4 18.0 %all-to-all-done.2.got_ref.r_ref = f32[32,72,128]{2,1,0:T(8,128)S(1)} async-done(((f32[32,72,128]{2,1,0:T(8,128)}), f32[32,72,128]{2,1,0:T(8,128)S(1)}, u32[]{:S(2)}, u32[]{:S(2)}) %all-to-all-start.2) | async-done | bytes 1179680 | tf_op jit(solution)/shard_map/all_to_all | solution.py:380
  94.4 0.9 broadcast_in_dim.11
  95.2 11.2 %all-to-all-start.3 = ((f32[16,2,32,128]{3,2,1,0:T(8,128)}), f32[16,2,32,128]{3,2,1,0:T(8,128)S(1)}, u32[]{:S(2)}, u32[]{:S(2)}) async-start(f32[16,2,32,128]{3,2,1,0:T(8,128)} %broadcast_in_dim.11), calls=%async_computation.3 | async-start | bytes 1048576 | tf_op jit(solution)/shard_map/all_to_all | solution.py:382
  106.4 0.0 copy-done.3
  106.4 16.7 %factor.1 = (f32[512,512]{1,0:T(8,128)S(1)}, f32[4,8,128]{2,1,0:T(8,128)S(1)}) custom-call(f32[32,72,128]{2,1,0:T(8,128)S(1)} %all-to-all-done.2.got_ref.r_ref, f32[4,128]{1,0:T(4,128)S(1)} %reshape.29.values_ref, f32[4,128]{1,0:T(4,128)S(1)} %reshape.30.variance_ref), custom_call_target="tpu_custom_call" | custom-call | flops 1048576 | bytes 1048576 | tf_op jit(solution)/shard_map/factor/pallas_call | solution.py:385
  123.2 5.9 %all-to-all-done.3.mine_ref = f32[16,2,32,128]{3,2,1,0:T(8,128)S(1)} async-done(((f32[16,2,32,128]{3,2,1,0:T(8,128)}), f32[16,2,32,128]{3,2,1,0:T(8,128)S(1)}, u32[]{:S(2)}, u32[]{:S(2)}) %all-to-all-start.3) | async-done | bytes 524320 | tf_op jit(solution)/shard_map/all_to_all | solution.py:382
  129.0 8.8 %collective-permute-start.1 = (f32[16,2,32,128]{3,2,1,0:T(8,128)S(1)}, f32[16,2,32,128]{3,2,1,0:T(8,128)S(1)}, u32[]{:S(2)}, u32[]{:S(2)}) collective-permute-start(f32[16,2,32,128]{3,2,1,0:T(8,128)S(1)} %all-to-all-done.3.mine_ref), channel_id=1, source_target_pairs={{0,16},{16,0},{32,48},{48,32},{64,80},{80,64},{96,112},{112,96},{1... | collective-permute-start | bytes 1572872 | tf_op jit(solution)/shard_map/ppermute | solution.py:398
  137.9 0.0 copy-start
  137.9 0.0 copy-start.2
  137.9 3.5 %gain.1 = (f32[256,512]{1,0:T(8,128)S(1)}, f32[256,512]{1,0:T(8,128)S(1)}, f32[1,256]{1,0:T(1,128)}) custom-call(f32[32,72,128]{2,1,0:T(8,128)S(1)} %all-to-all-done.2.got_ref.r_ref, f32[16,2,32,128]{3,2,1,0:T(8,128)S(1)} %all-to-all-done.3.mine_ref, f32[512,512]{1,0:T(8,128)S(1)} %get-tuple-element.23.linv_ref, f32[4,8,128]{2,1,0:T(8,128)S(1)} %get-tuple-element.24.e_ref, ...), custom_call_target="tpu_custom_call" | custom-call | flops 2147483648 | bytes 1048576 | tf_op jit(solution)/shard_map/gain/pallas_call | solution.py:399
  141.4 0.0 collective-permute-done.1.other_ref
  141.4 3.6 %update.1 = f32[256,512]{1,0:T(8,128)} custom-call(s32[2]{0:T(128)S(1)} %copy-done.2, f32[256,512]{1,0:T(8,128)S(1)} %copy-done, f32[16,2,32,128]{3,2,1,0:T(8,128)S(1)} %collective-permute-done.1.other_ref, f32[256,512]{1,0:T(8,128)S(1)} %get-tuple-element.25.mine_ref, f32[512,512]{1,0:T(8,128)S(1)} %get-tuple-element.23.linv_ref, ...), custom_call_target="tpu_custom_call" | custom-call | flops 2147483648 | bytes 1048576 | tf_op jit(solution)/shard_map/update/pallas_call | solution.py:407
  (11 shorter events, 0.2 us)
Async XLA Ops:
  65.4 28.9 %all-to-all-start.2 = ((f32[32,72,128]{2,1,0:T(8,128)}), f32[32,72,128]{2,1,0:T(8,128)S(1)}, u32[]{:S(2)}, u32[]{:S(2)}) async-start(f32[32,72,128]{2,1,0:T(8,128)} %pad_maximum_fusion), calls=%async_computation.2 | async-start | bytes 2359296 | tf_op jit(solution)/shard_map/all_to_all | solution.py:380
  75.7 30.7 %copy-start.3 = (f32[2,256]{1,0:T(2,128)S(1)}, f32[2,256]{1,0:T(2,128)}, u32[]{:S(2)}) copy-start(f32[2,256]{1,0:T(2,128)} %param.8) | copy-start | bytes 6148
  75.7 30.7 %copy-start.4 = (f32[2,256]{1,0:T(2,128)S(1)}, f32[2,256]{1,0:T(2,128)}, u32[]{:S(2)}) copy-start(f32[2,256]{1,0:T(2,128)} %param.11) | copy-start | bytes 6148
  75.7 0.7 collective-permute-start
  95.2 42.6 %copy-start.1 = (f32[256]{0:T(256)S(1)}, f32[256]{0:T(256)}, u32[]{:S(2)}) copy-start(f32[256]{0:T(256)} %param.7) | copy-start | bytes 3076
  95.2 33.8 %all-to-all-start.3 = ((f32[16,2,32,128]{3,2,1,0:T(8,128)}), f32[16,2,32,128]{3,2,1,0:T(8,128)S(1)}, u32[]{:S(2)}, u32[]{:S(2)}) async-start(f32[16,2,32,128]{3,2,1,0:T(8,128)} %broadcast_in_dim.11), calls=%async_computation.3 | async-start | bytes 1048576 | tf_op jit(solution)/shard_map/all_to_all | solution.py:382
  129.0 12.4 %collective-permute-start.1 = (f32[16,2,32,128]{3,2,1,0:T(8,128)S(1)}, f32[16,2,32,128]{3,2,1,0:T(8,128)S(1)}, u32[]{:S(2)}, u32[]{:S(2)}) collective-permute-start(f32[16,2,32,128]{3,2,1,0:T(8,128)S(1)} %all-to-all-done.3.mine_ref), channel_id=1, source_target_pairs={{0,16},{16,0},{32,48},{48,32},{64,80},{80,64},{96,112},{112,96},{1... | collective-permute-start | bytes 1572872 | tf_op jit(solution)/shard_map/ppermute | solution.py:398
  137.9 3.5 %copy-start = (f32[256,512]{1,0:T(8,128)S(1)}, f32[256,512]{1,0:T(8,128)}, u32[]{:S(2)}) copy-start(f32[256,512]{1,0:T(8,128)} %cov_ref.1) | copy-start | bytes 1572868
  137.9 3.5 %copy-start.2 = (s32[2]{0:T(128)S(1)}, s32[2]{0:T(128)}, u32[]{:S(2)}) copy-start(s32[2]{0:T(128)} %pad_add_fusion.at_ref) | copy-start | bytes 28

commit v5 on v2

--- a/solution.py
+++ b/solution.py
@@ -33,14 +33,14 @@
     return [(i, j) for i in range(n) for j in range(i + 1)]
 
 
-def call(kernel, out_shape, specs, scratch=(), flops=0, name=None):
+def call(kernel, out_shape, specs, scratch=(), flops=0, name=None, limit=LIMIT):
     return pl.pallas_call(
         kernel,
         out_shape=out_shape,
         in_specs=specs,
         out_specs=jax.tree.map(lambda _: VMEM, out_shape),
         scratch_shapes=list(scratch),
-        compiler_params=pltpu.CompilerParams(vmem_limit_bytes=LIMIT),
+        compiler_params=pltpu.CompilerParams(vmem_limit_bytes=limit),
         cost_estimate=pl.CostEstimate(flops=flops, bytes_accessed=1 << 20, transcendentals=0),
         name=name,
     )
@@ -273,10 +273,10 @@
             finish(i)
     for i in range(nb):
         gain_ref[:, span(i)] = e_ref[i, 0:rows, :]
-    after = mean_ref[...]
+    after = jnp.broadcast_to(mean_ref[...], (SUB, rows))
     for i in range(nb):
         after = after + dot_dims(e_ref[i, rows:rows + SUB, :], e_ref[i, 0:rows, :], 1, 1)
-    after_ref[...] = after
+    after_ref[...] = after[0:1]
 
 
 def update_kernel(cov_ref, pieces_ref, linv_ref, gain_ref, out_ref, c_ref):
@@ -333,6 +333,7 @@
         ],
         flops=2 * rows * m * (cols + m),
         name="project",
+        limit=60 * 1024 * 1024,
     )(at, covariance, mean, obs_cells, obs_weights)
     got = lax.all_to_all(send, ("row", "col"), 0, 0, axis_index_groups=plane_groups)
     s_chunk = jnp.sum(got[:, :s_rows], axis=0)
@@ -340,6 +341,7 @@
 
     s_send = jnp.broadcast_to(s_chunk[None], (n_z, s_rows, LANES))
     c_tr = lax.ppermute(c_own, ("row", "col"), pairs)
+    s_send, c_tr = lax.optimization_barrier((s_send, c_tr))
     s_all = lax.all_to_all(s_send, "row", 0, 0, axis_index_groups=z_groups)
     c_cols = lax.all_gather(c_tr, "row")
     s_full = jnp.sum(s_all, axis=0)
@@ -353,7 +355,7 @@
     got2 = lax.all_to_all(send2, ("row", "col"), 0, 0, axis_index_groups=plane_groups)
     linv, gain, after = call(
         factor_kernel,
-        (shape(m, m), shape(rows, m), shape(SUB, rows)),
+        (shape(m, m), shape(rows, m), shape(1, rows)),
         [VMEM] * 4,
         [
             pltpu.VMEM((nb, nb, LANES, LANES), jnp.float32),
@@ -372,7 +374,7 @@
         flops=1 << 31,
         name="update",
     )(covariance, c_cols, linv, gain)
-    return (updated, after[0])
+    return (updated, after.reshape(rows))
 
 
 def solution(mesh):

time: 160 us -> 158 us (0.988)
  waiting for transfers between devices: 52.2 us -> 41.4 us
  starting transfers between devices: 32.5 us -> 41.5 us
  local copies, waits for them, and re-layouts: 6.42 us -> 2.12 us
  Pallas kernels: 24.3 us -> 27.1 us
    all_to_all x1, starting transfers between devices: 13.7 us -> 28.6 us  [on_device(): s_all = lax.all_to_all(s_send, 'row', 0, 0, axis_index_groups=z_groups)]
    all_gather x1, waiting for transfers between devices: 20.9 us -> 10 us  [on_device(): c_cols = lax.all_gather(c_tr, 'row')]
    all_to_all x1, starting transfers between devices: 18.1 us -> 12.2 us  [on_device(): lax.all_to_all(send2, ('row', 'col'), 0, 0, axis_index_groups=plane_groups)]
    unnamed x20 -> x12, local copies, waits for them, and re-layouts: 4.95 us -> 1.25 us
    pallas_call x1, Pallas kernels: 3.24 us -> 5.4 us  [on_device(): call(project_kernel, shape(plane, chunk, LANES), [SMEM] + [HBM] * 4, [plt...]
where the time goes in v5:
time: 158 us
  starting transfers between devices  41.5 us (26%)
  waiting for transfers between devices  41.4 us (26%)
  blocking collectives  29.5 us (19%)
  Pallas kernels  27.1 us (17%)
  between operations  14.1 us (9%)
  local copies, waits for them, and re-layouts  2.12 us (1%)
  other arithmetic  1.88 us (1%)
    all_to_all x1, blocking collectives, on_device(): lax.all_to_all(send, ('row', 'col'), 0, 0, axis_index_groups=plane_groups)  29.5 us
    all_to_all x1, starting transfers between devices, on_device(): s_all = lax.all_to_all(s_send, 'row', 0, 0, axis_index_groups=z_groups)  28.6 us
    pallas_call x1, Pallas kernels, on_device(): call(factor_kernel, (shape(m, m), shape(rows, m), shape(1, rows)), [VMEM]...  18 us
    all_to_all x1, waiting for transfers between devices, on_device(): lax.all_to_all(send2, ('row', 'col'), 0, 0, axis_index_groups=plane_groups)  17.7 us
    all_to_all x1, waiting for transfers between devices, on_device(): s_all = lax.all_to_all(s_send, 'row', 0, 0, axis_index_groups=z_groups)  13 us
    all_to_all x1, starting transfers between devices, on_device(): lax.all_to_all(send2, ('row', 'col'), 0, 0, axis_index_groups=plane_groups)  12.2 us
    all_gather x1, waiting for transfers between devices, on_device(): c_cols = lax.all_gather(c_tr, 'row')  10 us
    pallas_call x1, Pallas kernels, on_device(): call(project_kernel, shape(plane, chunk, LANES), [SMEM] + [HBM] * 4, [plt...  5.4 us
  transfers between devices with their start and end apart: 4, of which 3 were waited for; matrix products, arithmetic and copies ran while one was open for 1% of the time, Pallas kernels for 11%

profile of v5, /device:TPU:1, one launch (start us, length us, event | category | flops | bytes accessed | tf_op | source)
XLA Modules:
  0.0 157.6 jit_solution(13850799676792688051)
XLA Ops:
  7.2 0.7 pad_add_fusion.at_ref
  7.8 5.4 %project.1 = f32[32,72,128]{2,1,0:T(8,128)} custom-call(s32[2]{0:T(128)} %pad_add_fusion.at_ref, f32[256,512]{1,0:T(8,128)} %cov_ref.1, f32[1,256]{1,0:T(1,128)} %bitcast.8, s32[2,4,256]{2,1,0:T(4,128)} %cells_in.1, f32[2,4,256]{2,1,0:T(4,128)} %weights_in.1), custom_call_target="tpu_custom_call" | custom-call | flops 268435456 | bytes 1048576 | tf_op jit(solution)/shard_map/project/pallas_call | solution.py:321
  13.2 29.5 %all_to_all.15 = f32[32,72,128]{2,1,0:T(8,128)S(1)} all-to-all(f32[32,72,128]{2,1,0:T(8,128)} %project.1), channel_id=1, replica_groups={{0,1,2,3,4,5,6,7,8,9,10,11,12,13,14,15,16,17,18,19,20,21,22,23,24,25,26..., dimensions={0} | all-to-all | bytes 2359296 | tf_op jit(solution)/shard_map/all_to_all | solution.py:338
  42.7 0.7 collective-permute-start
  43.4 0.1 slice_reduce_fusion
  43.5 0.0 collective-permute-done
  43.5 0.0 copy-start.3
  43.5 0.7 broadcast_in_dim.6
  44.2 28.6 %all-to-all-start.1 = ((f32[16,40,128]{2,1,0:T(8,128)}), f32[16,40,128]{2,1,0:T(8,128)S(1)}, u32[]{:S(2)}, u32[]{:S(2)}) async-start(f32[16,40,128]{2,1,0:T(8,128)} %broadcast_in_dim.6), calls=%async_computation.1 | async-start | bytes 655360 | tf_op jit(solution)/shard_map/all_to_all | solution.py:345
  72.8 0.0 all-gather.3.cloned.1.call-start
  72.9 0.0 copy-done.3
  72.9 0.7 all-gather.3.cloned.1.call-update
  73.6 13.0 %all-to-all-done.1 = f32[16,40,128]{2,1,0:T(8,128)S(1)} async-done(((f32[16,40,128]{2,1,0:T(8,128)}), f32[16,40,128]{2,1,0:T(8,128)S(1)}, u32[]{:S(2)}, u32[]{:S(2)}) %all-to-all-start.1) | async-done | bytes 327712 | tf_op jit(solution)/shard_map/all_to_all | solution.py:345
  86.7 0.1 broadcast_in_dim.8
  86.8 1.1 pad_maximum_fusion
  87.9 12.2 %all-to-all-start.2 = ((f32[32,72,128]{2,1,0:T(8,128)}), f32[32,72,128]{2,1,0:T(8,128)S(1)}, u32[]{:S(2)}, u32[]{:S(2)}) async-start(f32[32,72,128]{2,1,0:T(8,128)} %pad_maximum_fusion), calls=%async_computation.2 | async-start | bytes 2359296 | tf_op jit(solution)/shard_map/all_to_all | solution.py:355
  100.1 0.0 copy-done.4
  100.1 0.0 copy-start
  100.1 0.0 copy-done.5
  100.1 17.7 %all-to-all-done.2.got_ref = f32[32,72,128]{2,1,0:T(8,128)S(1)} async-done(((f32[32,72,128]{2,1,0:T(8,128)}), f32[32,72,128]{2,1,0:T(8,128)S(1)}, u32[]{:S(2)}, u32[]{:S(2)}) %all-to-all-start.2) | async-done | bytes 1179680 | tf_op jit(solution)/shard_map/all_to_all | solution.py:355
  117.8 18.0 %factor.1 = (f32[512,512]{1,0:T(8,128)S(1)}, f32[256,512]{1,0:T(8,128)S(1)}, f32[1,256]{1,0:T(1,128)}) custom-call(f32[32,72,128]{2,1,0:T(8,128)S(1)} %all-to-all-done.2.got_ref, f32[4,128]{1,0:T(4,128)S(1)} %reshape.28.values_ref, f32[4,128]{1,0:T(4,128)S(1)} %reshape.29.variance_ref, f32[1,256]{1,0:T(1,128)S(1)} %bitcast.9), custom_call_target="tpu_custom_call" | custom-call | flops 1048576 | bytes 1048576 | tf_op jit(solution)/shard_map/factor/pallas_call | solution.py:356
  135.9 10.0 %all-gather.3.cloned.1.call-done = f32[64,32,128]{2,1,0:T(8,128)} async-done(((f32[2,32,128]{2,1,0:T(8,128)}), f32[64,32,128]{2,1,0:T(8,128)}) %all-gather.3.cloned.1.call-update) | async-done | bytes 1048592 | tf_op jit(solution)/shard_map/all_gather | solution.py:346
  145.9 1.2 copy-done.2
  147.1 3.7 %update.1 = f32[256,512]{1,0:T(8,128)} custom-call(f32[256,512]{1,0:T(8,128)S(1)} %copy-done, f32[32,2,32,128]{3,2,1,0:T(8,128)S(1)} %bitcast.10, f32[512,512]{1,0:T(8,128)S(1)} %get-tuple-element.9.linv_ref, f32[256,512]{1,0:T(8,128)S(1)} %get-tuple-element.10.gain_ref), custom_call_target="tpu_custom_call" | custom-call | flops 2147483648 | bytes 1048576 | tf_op jit(solution)/shard_map/update/pallas_call | solution.py:369
  (11 shorter events, 0.1 us)
Async XLA Ops:
  42.7 0.7 collective-permute-start
  43.5 29.4 %copy-start.3 = (f32[2,32,128]{2,1,0:T(8,128)}, f32[2,32,128]{2,1,0:T(8,128)S(1)}, u32[]{:S(2)}) copy-start(f32[2,32,128]{2,1,0:T(8,128)S(1)} %collective-permute-done) | copy-start | bytes 98308
  44.2 42.4 %all-to-all-start.1 = ((f32[16,40,128]{2,1,0:T(8,128)}), f32[16,40,128]{2,1,0:T(8,128)S(1)}, u32[]{:S(2)}, u32[]{:S(2)}) async-start(f32[16,40,128]{2,1,0:T(8,128)} %broadcast_in_dim.6), calls=%async_computation.1 | async-start | bytes 655360 | tf_op jit(solution)/shard_map/all_to_all | solution.py:345
  72.8 73.1 %all-gather.3.cloned.1.call-start = ((), (), s32[]{:S(2)}) async-start(), calls=%async_computation.3 | async-start | bytes 1081344 | tf_op jit(solution)/shard_map/all_gather | solution.py:346
  87.9 12.2 %copy-start.4 = (f32[2,256]{1,0:T(2,128)S(1)}, f32[2,256]{1,0:T(2,128)}, u32[]{:S(2)}) copy-start(f32[2,256]{1,0:T(2,128)} %param.8) | copy-start | bytes 6148
  87.9 12.3 %copy-start.5 = (f32[2,256]{1,0:T(2,128)S(1)}, f32[2,256]{1,0:T(2,128)}, u32[]{:S(2)}) copy-start(f32[2,256]{1,0:T(2,128)} %param.11) | copy-start | bytes 6148
  87.9 30.0 %copy-start.1 = (f32[256]{0:T(256)S(1)}, f32[256]{0:T(256)}, u32[]{:S(2)}) copy-start(f32[256]{0:T(256)} %param.7) | copy-start | bytes 3076
  87.9 30.0 %all-to-all-start.2 = ((f32[32,72,128]{2,1,0:T(8,128)}), f32[32,72,128]{2,1,0:T(8,128)S(1)}, u32[]{:S(2)}, u32[]{:S(2)}) async-start(f32[32,72,128]{2,1,0:T(8,128)} %pad_maximum_fusion), calls=%async_computation.2 | async-start | bytes 2359296 | tf_op jit(solution)/shard_map/all_to_all | solution.py:355
  100.1 45.8 %copy-start = (f32[256,512]{1,0:T(8,128)S(1)}, f32[256,512]{1,0:T(8,128)}, u32[]{:S(2)}) copy-start(f32[256,512]{1,0:T(8,128)} %cov_ref.1) | copy-start | bytes 1572868
  145.9 1.2 copy-start.2
Sparse Core Ops, SparseCore 0:
  75.8 70.0 all-gather.2

commit v6 on v3

--- a/solution.py
+++ b/solution.py
@@ -278,7 +278,12 @@
 
 def early_kernel(got_ref, values_ref, variance_ref, linv_ref, a_ref, l_ref, e_ref, y_ref):
     prepare(got_ref, values_ref, variance_ref, linv_ref, a_ref, e_ref)
-    factor_steps(0, a_ref.shape[0] - 1, linv_ref, a_ref, l_ref, e_ref, y_ref)
+    factor_steps(0, a_ref.shape[0] - 2, linv_ref, a_ref, l_ref, e_ref, y_ref)
+
+
+def middle_kernel(linv_in, a_in, l_in, e_in, y_in, linv_ref, a_ref, l_ref, e_ref, y_ref):
+    nb = a_ref.shape[0]
+    factor_steps(nb - 2, nb - 1, linv_ref, a_ref, l_ref, e_ref, y_ref)
 
 
 def late_kernel(
@@ -287,10 +292,10 @@
     nb = a_ref.shape[0]
     rows = e_ref.shape[1] - SUB
     factor_steps(nb - 1, nb, linv_ref, a_ref, l_ref, e_ref, y_ref)
-    after = mean_ref[...]
+    after = jnp.broadcast_to(mean_ref[...], (SUB, rows))
     for i in range(nb):
         after = after + dot_dims(e_ref[i, rows:rows + SUB, :], e_ref[i, 0:rows, :], 1, 1)
-    after_ref[...] = after
+    after_ref[...] = after[0:1]
 
 
 def update_kernel(at_ref, cov_ref, mine_ref, other_ref, linv_ref, e_ref, out_ref, c_ref):
@@ -380,11 +385,12 @@
     bits = []
     while 1 << len(bits) < n_z:
         bits.append(2 << len(bits))
-    for bit in bits[:0:-1]:
-        theirs = partner(pieces, bit)
-        pieces = jnp.stack([pieces, theirs], axis=1).reshape((-1,) + c_tr.shape)
+    def doubled(x, theirs):
+        return jnp.concatenate([x[:, None], theirs[:, None]], axis=1).reshape((-1,) + c_tr.shape)
+
+    for bit in bits[:1:-1]:
+        pieces = doubled(pieces, partner(pieces, bit))
     got2, pieces = lax.optimization_barrier((got2, pieces))
-    theirs = partner(pieces, bits[0])
     state = (
         shape(m, m),
         shape(nb, nb, LANES, LANES),
@@ -392,15 +398,27 @@
         shape(nb, rows + SUB, LANES),
         shape(LANES, m),
     )
+    theirs = partner(pieces, bits[1])
     held = call(early_kernel, state, [VMEM] * 3, flops=1 << 30, name="early")(
         got2, obs_values.reshape(nb, LANES), obs_variance.reshape(nb, LANES)
     )
     held, theirs = lax.optimization_barrier((held, theirs))
-    pieces = jnp.stack([pieces, theirs], axis=1).reshape((-1,) + c_tr.shape)
+    pieces = doubled(pieces, theirs)
+    theirs = partner(pieces, bits[0])
+    held = call(
+        middle_kernel,
+        state,
+        [VMEM] * 5,
+        flops=1 << 30,
+        name="middle",
+        aliases={n: n for n in range(len(state))},
+    )(*held)
+    held, theirs = lax.optimization_barrier((held, theirs))
+    pieces = doubled(pieces, theirs)
     other = partner(pieces, 1)
     out = call(
         late_kernel,
-        state + (shape(SUB, rows),),
+        state + (shape(1, rows),),
         [VMEM] * 6,
         flops=1 << 30,
         name="late",
@@ -415,7 +433,7 @@
         flops=1 << 31,
         name="update",
     )(at, covariance, pieces, other, linv, e)
-    return (updated, after[0])
+    return (updated, after.reshape(rows))
 
 
 def solution(mesh):

time: 146 us -> 143 us (0.979)
  waiting for transfers between devices: 36.6 us -> 34.5 us
    pallas_call x1 -> x2, Pallas kernels: 5.14 us -> 10.2 us  [the longest x1 5.84 us: on_device(): call(late_kernel, state + (shape(1, rows),), [VMEM] * 6, flops=1 << 30, n...]
    pallas_call x1, Pallas kernels: 12.9 us -> 8.46 us  [on_device(): call(early_kernel, state, [VMEM] * 3, flops=1 << 30, name='early')]
    ppermute x5, waiting for transfers between devices: 22.1 us -> 20 us  [partner(): return lax.ppermute(x, 'row', [(i, i ^ bit) for i in range(n_row)])]
  transfers between devices with their start and end apart: 8 -> 8, of which waited for: 4 -> 4; matrix products, arithmetic and copies ran while one was open for 1% -> 1% of each run, Pallas kernels for 12% -> 13%
where the time goes in v6:
time: 143 us; the launch traced here: 142 us
  starting transfers between devices  46.2 us (32%)
  waiting for transfers between devices  34.5 us (24%)
  blocking collectives  29.5 us (21%)
  Pallas kernels  28.3 us (20%)
  other arithmetic  1.88 us (1%)
    all_to_all x1, blocking collectives, on_device(): lax.all_to_all(send, ('row', 'col'), 0, 0, axis_index_groups=plane_groups)  29.5 us
    ppermute x5, waiting for transfers between devices, partner(): return lax.ppermute(x, 'row', [(i, i ^ bit) for i in range(n_row)])  20 us
    ppermute x5, starting transfers between devices, partner(): return lax.ppermute(x, 'row', [(i, i ^ bit) for i in range(n_row)])  16.7 us
    all_to_all x1, starting transfers between devices, on_device(): lax.all_to_all(send2, ('row', 'col'), 0, 0, axis_index_groups=plane_groups)  15.9 us
    all_to_all x1, waiting for transfers between devices, on_device(): s_all = lax.all_to_all(s_send, 'row', 0, 0, axis_index_groups=z_groups)  14.5 us
    all_to_all x1, starting transfers between devices, on_device(): s_all = lax.all_to_all(s_send, 'row', 0, 0, axis_index_groups=z_groups)  12.9 us
    pallas_call x1, Pallas kernels, on_device(): call(early_kernel, state, [VMEM] * 3, flops=1 << 30, name='early')  8.46 us
    pallas_call x1, Pallas kernels, on_device(): call(late_kernel, state + (shape(1, rows),), [VMEM] * 6, flops=1 << 30, n...  5.84 us
  transfers between devices with their start and end apart: 8, of which 4 were waited for; matrix products, arithmetic and copies ran while one was open for 1% of the time, Pallas kernels for 13%

profile of v6, /device:TPU:1, one launch (start us, length us, event | category | flops | bytes accessed | tf_op | source)
XLA Modules:
  0.0 142.1 jit_solution(2052460411537688530)
XLA Ops:
  0.6 0.6 pad_add_fusion.at_ref
  1.2 5.4 %project.1 = f32[32,72,128]{2,1,0:T(8,128)} custom-call(s32[2]{0:T(128)} %pad_add_fusion.at_ref, f32[256,512]{1,0:T(8,128)} %cov_ref.1, f32[1,256]{1,0:T(1,128)} %bitcast.26, s32[2,4,256]{2,1,0:T(4,128)} %cells_in.1, f32[2,4,256]{2,1,0:T(4,128)} %weights_in.1), custom_call_target="tpu_custom_call" | custom-call | flops 268435456 | bytes 1048576 | tf_op jit(solution)/shard_map/project/pallas_call | solution.py:346
  6.6 29.5 %all_to_all.15 = f32[32,72,128]{2,1,0:T(8,128)S(1)} all-to-all(f32[32,72,128]{2,1,0:T(8,128)} %project.1), channel_id=1, replica_groups={{0,1,2,3,4,5,6,7,8,9,10,11,12,13,14,15,16,17,18,19,20,21,22,23,24,25,26..., dimensions={0} | all-to-all | bytes 2359296 | tf_op jit(solution)/shard_map/all_to_all | solution.py:363
  36.1 0.1 slice_reduce_fusion
  36.1 0.7 broadcast_in_dim.36
  36.9 12.9 %all-to-all-start.1 = ((f32[16,40,128]{2,1,0:T(8,128)}), f32[16,40,128]{2,1,0:T(8,128)S(1)}, u32[]{:S(2)}, u32[]{:S(2)}) async-start(f32[16,40,128]{2,1,0:T(8,128)} %broadcast_in_dim.36), calls=%async_computation.1 | async-start | bytes 655360 | tf_op jit(solution)/shard_map/all_to_all | solution.py:369
  49.9 0.7 collective-permute-start
  50.5 14.5 %all-to-all-done.1 = f32[16,40,128]{2,1,0:T(8,128)S(1)} async-done(((f32[16,40,128]{2,1,0:T(8,128)}), f32[16,40,128]{2,1,0:T(8,128)S(1)}, u32[]{:S(2)}, u32[]{:S(2)}) %all-to-all-start.1) | async-done | bytes 327712 | tf_op jit(solution)/shard_map/all_to_all | solution.py:369
  65.1 0.1 broadcast_in_dim.38
  65.2 1.1 pad_maximum_fusion
  66.3 15.9 %all-to-all-start.2 = ((f32[32,72,128]{2,1,0:T(8,128)}), f32[32,72,128]{2,1,0:T(8,128)S(1)}, u32[]{:S(2)}, u32[]{:S(2)}) async-start(f32[32,72,128]{2,1,0:T(8,128)} %pad_maximum_fusion), calls=%async_computation.2 | async-start | bytes 2359296 | tf_op jit(solution)/shard_map/all_to_all | solution.py:379
  82.2 5.5 %collective-permute-start.1 = (f32[1,2,32,128]{3,2,1,0:T(8,128)S(1)}, f32[1,2,32,128]{3,2,1,0:T(8,128)S(1)}, u32[]{:S(2)}, u32[]{:S(2)}) collective-permute-start(f32[1,2,32,128]{3,2,1,0:T(8,128)S(1)} %bitcast.36), channel_id=1, source_target_pairs={{0,256},{16,272},{32,288},{48,304},{64,320},{80,336},{96,352},{112... | collective-permute-start | bytes 98312 | tf_op jit(solution)/shard_map/ppermute | solution.py:382
  87.7 7.8 %collective-permute-done.1 = f32[1,2,32,128]{3,2,1,0:T(8,128)S(1)} collective-permute-done((f32[1,2,32,128]{3,2,1,0:T(8,128)S(1)}, f32[1,2,32,128]{3,2,1,0:T(8,128)S(1)}, u32[]{:S(2)}, u32[]{:S(2)}) %collective-permute-start.1) | collective-permute-done | bytes 32800 | tf_op jit(solution)/shard_map/ppermute | solution.py:382
  95.6 3.3 %collective-permute-start.2 = (f32[2,2,32,128]{3,2,1,0:T(8,128)S(1)}, f32[2,2,32,128]{3,2,1,0:T(8,128)S(1)}, u32[]{:S(2)}, u32[]{:S(2)}) collective-permute-start(f32[2,2,32,128]{3,2,1,0:T(8,128)S(1)} %get-tuple-element.61), channel_id=1, source_target_pairs={{0,128},{16,144},{32,160},{48,176},{64,192},{80,208},{96,224},{112... | collective-permute-start | bytes 196616 | tf_op jit(solution)/shard_map/ppermute | solution.py:382
  98.8 9.7 %collective-permute-done.2 = f32[2,2,32,128]{3,2,1,0:T(8,128)S(1)} collective-permute-done((f32[2,2,32,128]{3,2,1,0:T(8,128)S(1)}, f32[2,2,32,128]{3,2,1,0:T(8,128)S(1)}, u32[]{:S(2)}, u32[]{:S(2)}) %collective-permute-start.2) | collective-permute-done | bytes 65568 | tf_op jit(solution)/shard_map/ppermute | solution.py:382
  108.5 1.9 %collective-permute-start.3 = (f32[4,2,32,128]{3,2,1,0:T(8,128)S(1)}, f32[4,2,32,128]{3,2,1,0:T(8,128)S(1)}, u32[]{:S(2)}, u32[]{:S(2)}) collective-permute-start(f32[4,2,32,128]{3,2,1,0:T(8,128)S(1)} %bitcast.31), channel_id=1, source_target_pairs={{0,64},{16,80},{32,96},{48,112},{64,0},{80,16},{96,32},{112,48},{1... | collective-permute-start | bytes 393224 | tf_op jit(solution)/shard_map/ppermute | solution.py:382
  110.5 8.5 %early.1 = (f32[512,512]{1,0:T(8,128)S(1)}, f32[4,4,128,128]{3,2,1,0:T(8,128)S(1)}, f32[4,4,128,128]{3,2,1,0:T(8,128)S(1)}, f32[4,264,128]{2,1,0:T(8,128)S(1)}, f32[128,512]{1,0:T(8,128)S(1)}) custom-call(f32[32,72,128]{2,1,0:T(8,128)S(1)} %all-to-all-done.2.got_ref, f32[4,128]{1,0:T(4,128)S(1)} %reshape.42.values_ref, f32[4,128]{1,0:T(4,128)S(1)} %reshape.43.variance_ref), custom_call_target="tpu_custom_call" | custom-call | flops 1073741824 | bytes 1048576 | tf_op jit(solution)/shard_map/early/pallas_call | solution.py:402
  119.0 0.0 copy-start.1
  119.0 2.1 %collective-permute-start.4 = (f32[8,2,32,128]{3,2,1,0:T(8,128)S(1)}, f32[8,2,32,128]{3,2,1,0:T(8,128)S(1)}, u32[]{:S(2)}, u32[]{:S(2)}) collective-permute-start(f32[8,2,32,128]{3,2,1,0:T(8,128)S(1)} %bitcast.29), channel_id=1, source_target_pairs={{0,32},{16,48},{32,0},{48,16},{64,96},{80,112},{96,64},{112,80},{1... | collective-permute-start | bytes 786440 | tf_op jit(solution)/shard_map/ppermute | solution.py:382
  121.1 4.3 %middle.1 = (f32[512,512]{1,0:T(8,128)S(1)}, f32[4,4,128,128]{3,2,1,0:T(8,128)S(1)}, f32[4,4,128,128]{3,2,1,0:T(8,128)S(1)}, f32[4,264,128]{2,1,0:T(8,128)S(1)}, f32[128,512]{1,0:T(8,128)S(1)}) custom-call(f32[512,512]{1,0:T(8,128)S(1)} %get-tuple-element.41.linv_in, ...), custom_call_target="tpu_custom_call", output_to_operand_aliasing={{0}: (0, {}), {1}: (1, {}), {2}: (2, {}), {3}: (3, {}), {4}... | custom-call | flops 1073741824 | bytes 1048576 | tf_op jit(solution)/shard_map/middle/pallas_call | solution.py:408
  125.5 2.5 %collective-permute-done.4 = f32[8,2,32,128]{3,2,1,0:T(8,128)S(1)} collective-permute-done((f32[8,2,32,128]{3,2,1,0:T(8,128)S(1)}, f32[8,2,32,128]{3,2,1,0:T(8,128)S(1)}, u32[]{:S(2)}, u32[]{:S(2)}) %collective-permute-start.4) | collective-permute-done | bytes 262176 | tf_op jit(solution)/shard_map/ppermute | solution.py:382
  128.1 3.9 %collective-permute-start.5 = (f32[16,2,32,128]{3,2,1,0:T(8,128)S(1)}, f32[16,2,32,128]{3,2,1,0:T(8,128)S(1)}, u32[]{:S(2)}, u32[]{:S(2)}) collective-permute-start(f32[16,2,32,128]{3,2,1,0:T(8,128)S(1)} %bitcast.24), channel_id=1, source_target_pairs={{0,16},{16,0},{32,48},{48,32},{64,80},{80,64},{96,112},{112,96},{1... | collective-permute-start | bytes 1572872 | tf_op jit(solution)/shard_map/ppermute | solution.py:382
  132.0 5.8 %late.1 = (f32[512,512]{1,0:T(8,128)S(1)}, f32[4,4,128,128]{3,2,1,0:T(8,128)S(1)}, f32[4,4,128,128]{3,2,1,0:T(8,128)S(1)}, f32[4,264,128]{2,1,0:T(8,128)S(1)}, f32[128,512]{1,0:T(8,128)S(1)}, /*index=5*/f32[1,256]{1,0:T(1,128)}) custom-call(f32[1,256]{1,0:T(1,128)S(1)} %bitcast.27, ...), custom_call_target="tpu_custom_call", output_to_operand_aliasing={{0}: (1, {}), {1}: (2, {}), {2}: (3, {}), {3}: (4, {}), {4}... | custom-call | flops 1073741824 | bytes 1048576 | tf_op jit(solution)/shard_map/late/pallas_call | solution.py:419
  137.8 4.3 %update.1 = f32[256,512]{1,0:T(8,128)} custom-call(s32[2]{0:T(128)S(1)} %copy-done.2, f32[256,512]{1,0:T(8,128)S(1)} %copy-done, f32[16,2,32,128]{3,2,1,0:T(8,128)S(1)} %bitcast.25, f32[16,2,32,128]{3,2,1,0:T(8,128)S(1)} %collective-permute-done.5.other_ref, f32[512,512]{1,0:T(8,128)S(1)} %get-tuple-element.57.linv_ref, ...), custom_call_target="tpu_custom_call" | custom-call | flops 2147483648 | bytes 1048576 | tf_op jit(solution)/shard_map/update/pallas_call | solution.py:428
  (23 shorter events, 0.3 us)
Async XLA Ops:
  36.9 28.1 %all-to-all-start.1 = ((f32[16,40,128]{2,1,0:T(8,128)}), f32[16,40,128]{2,1,0:T(8,128)S(1)}, u32[]{:S(2)}, u32[]{:S(2)}) async-start(f32[16,40,128]{2,1,0:T(8,128)} %broadcast_in_dim.36), calls=%async_computation.1 | async-start | bytes 655360 | tf_op jit(solution)/shard_map/all_to_all | solution.py:369
  49.9 16.4 %collective-permute-start = (f32[2,32,128]{2,1,0:T(8,128)S(1)}, f32[2,32,128]{2,1,0:T(8,128)S(1)}, u32[]{:S(2)}, u32[]{:S(2)}) collective-permute-start(f32[2,32,128]{2,1,0:T(8,128)S(1)} %bitcast_reduce_fusion), channel_id=1, source_target_pairs={{0,0},{1,32},{2,64},{3,96},{4,128},{5,160},{6,192},{7,224},{8,256}... | collective-permute-start | bytes 98312 | tf_op jit(solution)/shard_map/ppermute | solution.py:368
  66.3 44.2 %copy-start.3 = (f32[2,256]{1,0:T(2,128)S(1)}, f32[2,256]{1,0:T(2,128)}, u32[]{:S(2)}) copy-start(f32[2,256]{1,0:T(2,128)} %param.8) | copy-start | bytes 6148
  66.3 44.2 %copy-start.4 = (f32[2,256]{1,0:T(2,128)S(1)}, f32[2,256]{1,0:T(2,128)}, u32[]{:S(2)}) copy-start(f32[2,256]{1,0:T(2,128)} %param.11) | copy-start | bytes 6148
  66.3 42.3 %all-to-all-start.2 = ((f32[32,72,128]{2,1,0:T(8,128)}), f32[32,72,128]{2,1,0:T(8,128)S(1)}, u32[]{:S(2)}, u32[]{:S(2)}) async-start(f32[32,72,128]{2,1,0:T(8,128)} %pad_maximum_fusion), calls=%async_computation.2 | async-start | bytes 2359296 | tf_op jit(solution)/shard_map/all_to_all | solution.py:379
  82.2 13.4 %collective-permute-start.1 = (f32[1,2,32,128]{3,2,1,0:T(8,128)S(1)}, f32[1,2,32,128]{3,2,1,0:T(8,128)S(1)}, u32[]{:S(2)}, u32[]{:S(2)}) collective-permute-start(f32[1,2,32,128]{3,2,1,0:T(8,128)S(1)} %bitcast.36), channel_id=1, source_target_pairs={{0,256},{16,272},{32,288},{48,304},{64,320},{80,336},{96,352},{112... | collective-permute-start | bytes 98312 | tf_op jit(solution)/shard_map/ppermute | solution.py:382
  95.6 12.9 %collective-permute-start.2 = (f32[2,2,32,128]{3,2,1,0:T(8,128)S(1)}, f32[2,2,32,128]{3,2,1,0:T(8,128)S(1)}, u32[]{:S(2)}, u32[]{:S(2)}) collective-permute-start(f32[2,2,32,128]{3,2,1,0:T(8,128)S(1)} %get-tuple-element.61), channel_id=1, source_target_pairs={{0,128},{16,144},{32,160},{48,176},{64,192},{80,208},{96,224},{112... | collective-permute-start | bytes 196616 | tf_op jit(solution)/shard_map/ppermute | solution.py:382
  108.5 10.4 %collective-permute-start.3 = (f32[4,2,32,128]{3,2,1,0:T(8,128)S(1)}, f32[4,2,32,128]{3,2,1,0:T(8,128)S(1)}, u32[]{:S(2)}, u32[]{:S(2)}) collective-permute-start(f32[4,2,32,128]{3,2,1,0:T(8,128)S(1)} %bitcast.31), channel_id=1, source_target_pairs={{0,64},{16,80},{32,96},{48,112},{64,0},{80,16},{96,32},{112,48},{1... | collective-permute-start | bytes 393224 | tf_op jit(solution)/shard_map/ppermute | solution.py:382
  119.0 12.9 %copy-start.1 = (f32[256]{0:T(256)S(1)}, f32[256]{0:T(256)}, u32[]{:S(2)}) copy-start(f32[256]{0:T(256)} %param.7) | copy-start | bytes 3076
  119.0 9.0 %collective-permute-start.4 = (f32[8,2,32,128]{3,2,1,0:T(8,128)S(1)}, f32[8,2,32,128]{3,2,1,0:T(8,128)S(1)}, u32[]{:S(2)}, u32[]{:S(2)}) collective-permute-start(f32[8,2,32,128]{3,2,1,0:T(8,128)S(1)} %bitcast.29), channel_id=1, source_target_pairs={{0,32},{16,48},{32,0},{48,16},{64,96},{80,112},{96,64},{112,80},{1... | collective-permute-start | bytes 786440 | tf_op jit(solution)/shard_map/ppermute | solution.py:382
  128.1 9.7 %copy-start = (f32[256,512]{1,0:T(8,128)S(1)}, f32[256,512]{1,0:T(8,128)}, u32[]{:S(2)}) copy-start(f32[256,512]{1,0:T(8,128)} %cov_ref.1) | copy-start | bytes 1572868
  128.1 9.7 %copy-start.2 = (s32[2]{0:T(128)S(1)}, s32[2]{0:T(128)}, u32[]{:S(2)}) copy-start(s32[2]{0:T(128)} %pad_add_fusion.at_ref) | copy-start | bytes 28
  128.1 9.7 %collective-permute-start.5 = (f32[16,2,32,128]{3,2,1,0:T(8,128)S(1)}, f32[16,2,32,128]{3,2,1,0:T(8,128)S(1)}, u32[]{:S(2)}, u32[]{:S(2)}) collective-permute-start(f32[16,2,32,128]{3,2,1,0:T(8,128)S(1)} %bitcast.24), channel_id=1, source_target_pairs={{0,16},{16,0},{32,48},{48,32},{64,80},{80,64},{96,112},{112,96},{1... | collective-permute-start | bytes 1572872 | tf_op jit(solution)/shard_map/ppermute | solution.py:382

commit v7 on v3

--- a/solution.py
+++ b/solution.py
@@ -11,7 +11,6 @@
 HI = lax.Precision.HIGHEST
 HBM = pl.BlockSpec(memory_space=pltpu.HBM)
 VMEM = pl.BlockSpec(memory_space=pltpu.VMEM)
-SMEM = pl.BlockSpec(memory_space=pltpu.SMEM)
 LIMIT = 48 * 1024 * 1024
 
 
@@ -62,7 +61,7 @@
 
 
 def project_kernel(
-    at_ref, cov_in, mean_in, cells_in, weights_in, send_ref, c_ref, s_ref, cov_ref, mean_ref, cells_ref, weights_ref, sems
+    cov_in, mean_in, cells_in, weights_in, send_ref, c_ref, s_ref, cov_ref, mean_ref, cells_ref, weights_ref, sems
 ):
     moves = [
         pltpu.make_async_copy(src, dst, sems.at[n])
@@ -72,19 +71,21 @@
     ]
     for move in moves:
         move.start()
-    for move in moves:
-        move.wait()
+    moves[0].wait()
+    moves[1].wait()
     rows, cols = cov_ref.shape
+    row, col = lax.axis_index("row"), lax.axis_index("col")
     batches, _, obs = cells_ref.shape
     plane = send_ref.shape[0]
     nb = batches * obs // LANES
     per = obs // LANES
-    row_ops = []
+    row_ops = [operator(cells_ref, weights_ref, b, row * rows, rows) for b in range(batches)]
+    col_ops = [operator(cells_ref, weights_ref, b, col * cols, cols) for b in range(batches)]
+    moves[2].wait()
+    moves[3].wait()
     cov = cov_ref[...]
     for b in range(batches):
-        col_op = operator(cells_ref, weights_ref, b, at_ref[1] * cols, cols)
-        row_ops.append(operator(cells_ref, weights_ref, b, at_ref[0] * rows, rows))
-        c_ref[:, b * obs:(b + 1) * obs] = dot(cov, col_op)
+        c_ref[:, b * obs:(b + 1) * obs] = dot(cov, col_ops[b])
     for i in range(batches):
         for j in range(i + 1):
             s_ref[i * obs:(i + 1) * obs, j * obs:(j + 1) * obs] = dot_dims(
@@ -95,7 +96,7 @@
     lane = lax.broadcasted_iota(jnp.int32, (SUB, LANES), 1)
     sub = lax.broadcasted_iota(jnp.int32, (SUB, LANES), 0)
     mean = jnp.broadcast_to(mean_ref[...], (SUB, rows))
-    mean = jnp.where(at_ref[1] == 0, mean, 0.0)
+    mean = jnp.where(col == 0, mean, 0.0)
     preds = [dot(mean, row_ops[b]) for b in range(batches)]
     for n, (i, j) in enumerate(low):
         for g in range(GROUPS):
@@ -287,20 +288,21 @@
     nb = a_ref.shape[0]
     rows = e_ref.shape[1] - SUB
     factor_steps(nb - 1, nb, linv_ref, a_ref, l_ref, e_ref, y_ref)
-    after = mean_ref[...]
+    after = jnp.broadcast_to(mean_ref[...], (SUB, rows))
     for i in range(nb):
         after = after + dot_dims(e_ref[i, rows:rows + SUB, :], e_ref[i, 0:rows, :], 1, 1)
-    after_ref[...] = after
-
-
-def update_kernel(at_ref, cov_ref, mine_ref, other_ref, linv_ref, e_ref, out_ref, c_ref):
+    after_ref[...] = after[0:1]
+
+
+def update_kernel(cov_ref, mine_ref, other_ref, linv_ref, e_ref, out_ref, c_ref):
     n_z, halves, tall, _ = mine_ref.shape
     rows, cols = cov_ref.shape
     m = c_ref.shape[1]
     nb = m // LANES
     own = tall // nb
-    core = lax.rem(at_ref[0], 2)
-    z_here = lax.div(at_ref[0], 2)
+    row = lax.axis_index("row")
+    core = lax.rem(row, 2)
+    z_here = lax.div(row, 2)
     for ref, k in ((mine_ref, core), (other_ref, 1 - core)):
         for d in range(n_z):
             start = pl.multiple_of((k * n_z + lax.bitwise_xor(z_here, d)) * own, own)
@@ -341,7 +343,7 @@
     send = call(
         project_kernel,
         shape(plane, chunk, LANES),
-        [SMEM] + [HBM] * 4,
+        [HBM] * 4,
         [
             pltpu.VMEM((rows, m), jnp.float32),
             pltpu.VMEM((m, m), jnp.float32),
@@ -354,14 +356,26 @@
         flops=2 * rows * m * (cols + m),
         name="project",
         limit=60 * 1024 * 1024,
-    )(at, covariance, mean, obs_cells, obs_weights)
+    )(covariance, mean, obs_cells, obs_weights)
     got = lax.all_to_all(send, ("row", "col"), 0, 0, axis_index_groups=plane_groups)
     s_chunk = jnp.sum(got[:, :s_rows], axis=0)
     c_own = jnp.sum(got[:, s_rows:].reshape(2, n_col, c_rows, LANES), axis=1)
 
     s_send = jnp.broadcast_to(s_chunk[None], (n_z, s_rows, LANES))
-    c_tr = lax.ppermute(c_own, ("row", "col"), pairs)
+    def partner(x, bit):
+        return lax.ppermute(x, "row", [(i, i ^ bit) for i in range(n_row)])
+
+    def doubled(x, theirs):
+        return jnp.concatenate([x[:, None], theirs[:, None]], axis=1).reshape((-1,) + c_own.shape)
+
+    bits = []
+    while 1 << len(bits) < n_z:
+        bits.append(2 << len(bits))
+    pieces = lax.ppermute(c_own, ("row", "col"), pairs)[None]
+    theirs = partner(pieces, bits[-1])
     s_all = lax.all_to_all(s_send, "row", 0, 0, axis_index_groups=z_groups)
+    s_all, pieces, theirs = lax.optimization_barrier((s_all, pieces, theirs))
+    pieces = doubled(pieces, theirs)
     s_full = jnp.sum(s_all, axis=0)
     send2 = jnp.concatenate(
         [
@@ -370,21 +384,11 @@
         ],
         axis=1,
     )
-    send2, c_tr = lax.optimization_barrier((send2, c_tr))
     got2 = lax.all_to_all(send2, ("row", "col"), 0, 0, axis_index_groups=plane_groups)
 
-    def partner(x, bit):
-        return lax.ppermute(x, "row", [(i, i ^ bit) for i in range(n_row)])
-
-    pieces = c_tr[None]
-    bits = []
-    while 1 << len(bits) < n_z:
-        bits.append(2 << len(bits))
-    for bit in bits[:0:-1]:
-        theirs = partner(pieces, bit)
-        pieces = jnp.stack([pieces, theirs], axis=1).reshape((-1,) + c_tr.shape)
+    for bit in bits[-2:0:-1]:
+        pieces = doubled(pieces, partner(pieces, bit))
     got2, pieces = lax.optimization_barrier((got2, pieces))
-    theirs = partner(pieces, bits[0])
     state = (
         shape(m, m),
         shape(nb, nb, LANES, LANES),
@@ -392,15 +396,16 @@
         shape(nb, rows + SUB, LANES),
         shape(LANES, m),
     )
+    theirs = partner(pieces, bits[0])
     held = call(early_kernel, state, [VMEM] * 3, flops=1 << 30, name="early")(
         got2, obs_values.reshape(nb, LANES), obs_variance.reshape(nb, LANES)
     )
     held, theirs = lax.optimization_barrier((held, theirs))
-    pieces = jnp.stack([pieces, theirs], axis=1).reshape((-1,) + c_tr.shape)
+    pieces = doubled(pieces, theirs)
     other = partner(pieces, 1)
     out = call(
         late_kernel,
-        state + (shape(SUB, rows),),
+        state + (shape(1, rows),),
         [VMEM] * 6,
         flops=1 << 30,
         name="late",
@@ -410,12 +415,12 @@
     updated = call(
         update_kernel,
         shape(rows, cols),
-        [SMEM] + [VMEM] * 5,
+        [VMEM] * 5,
         [pltpu.VMEM((cols, m), jnp.float32)],
         flops=1 << 31,
         name="update",
-    )(at, covariance, pieces, other, linv, e)
-    return (updated, after[0])
+    )(covariance, pieces, other, linv, e)
+    return (updated, after.reshape(rows))
 
 
 def solution(mesh):

time: 146 us -> 149 us (1.021)
  starting transfers between devices: 46.7 us -> 68.6 us
  waiting for transfers between devices: 36.6 us -> 19.2 us
    ppermute x5, starting transfers between devices: 17.2 us -> 38 us  [partner(): return lax.ppermute(x, 'row', [(i, i ^ bit) for i in range(n_row)])]
    all_to_all x1, waiting for transfers between devices: 14.5 us -> 0.01 us  [on_device(): s_all = lax.all_to_all(s_send, 'row', 0, 0, axis_index_groups=z_groups)]
    ppermute x5, waiting for transfers between devices: 22.1 us -> 19.2 us  [partner(): return lax.ppermute(x, 'row', [(i, i ^ bit) for i in range(n_row)])]
  transfers between devices with their start and end apart: 8 -> 8, of which waited for: 4 -> 3; matrix products, arithmetic and copies ran while one was open for 1% -> 0% of each run, Pallas kernels for 12% -> 13%
where the time goes in v7:
time: 149 us; the launch traced here: 148 us
  starting transfers between devices  68.6 us (46%)
  blocking collectives  29.5 us (20%)
  Pallas kernels  27.8 us (19%)
  waiting for transfers between devices  19.2 us (13%)
    ppermute x5, starting transfers between devices, partner(): return lax.ppermute(x, 'row', [(i, i ^ bit) for i in range(n_row)])  38 us
    all_to_all x1, blocking collectives, on_device(): lax.all_to_all(send, ('row', 'col'), 0, 0, axis_index_groups=plane_groups)  29.5 us
    ppermute x5, waiting for transfers between devices, partner(): return lax.ppermute(x, 'row', [(i, i ^ bit) for i in range(n_row)])  19.2 us
    all_to_all x1, starting transfers between devices, on_device(): lax.all_to_all(send2, ('row', 'col'), 0, 0, axis_index_groups=plane_groups)  17 us
    all_to_all x1, starting transfers between devices, on_device(): s_all = lax.all_to_all(s_send, 'row', 0, 0, axis_index_groups=z_groups)  12.9 us
    pallas_call x1, Pallas kernels, on_device(): call(early_kernel, state, [VMEM] * 3, flops=1 << 30, name='early')  12.9 us
    pallas_call x1, Pallas kernels, on_device(): call(late_kernel, state + (shape(1, rows),), [VMEM] * 6, flops=1 << 30, n...  5.84 us
    pallas_call x1, Pallas kernels, on_device(): call(project_kernel, shape(plane, chunk, LANES), [HBM] * 4, [pltpu.VMEM((...  5.32 us
  transfers between devices with their start and end apart: 8, of which 3 were waited for; matrix products, arithmetic and copies ran while one was open for 0% of the time, Pallas kernels for 13%

profile of v7, /device:TPU:1, one launch (start us, length us, event | category | flops | bytes accessed | tf_op | source)
XLA Modules:
  0.0 148.2 jit_solution(11180429492908998937)
XLA Ops:
  0.6 5.3 %project.1 = f32[32,72,128]{2,1,0:T(8,128)} custom-call(f32[256,512]{1,0:T(8,128)} %cov_ref.1, f32[1,256]{1,0:T(1,128)} %bitcast.24, s32[2,4,256]{2,1,0:T(4,128)} %cells_in.1, f32[2,4,256]{2,1,0:T(4,128)} %weights_in.1), custom_call_target="tpu_custom_call" | custom-call | flops 268435456 | bytes 1048576 | tf_op jit(solution)/shard_map/project/pallas_call | solution.py:343
  6.0 29.5 %all_to_all.15 = f32[32,72,128]{2,1,0:T(8,128)S(1)} all-to-all(f32[32,72,128]{2,1,0:T(8,128)} %project.1), channel_id=1, replica_groups={{0,1,2,3,4,5,6,7,8,9,10,11,12,13,14,15,16,17,18,19,20,21,22,23,24,25,26..., dimensions={0} | all-to-all | bytes 2359296 | tf_op jit(solution)/shard_map/all_to_all | solution.py:360
  35.4 0.1 slice_reduce_fusion
  35.5 0.7 broadcast_in_dim.39
  36.2 12.9 %all-to-all-start.1 = ((f32[16,40,128]{2,1,0:T(8,128)}), f32[16,40,128]{2,1,0:T(8,128)S(1)}, u32[]{:S(2)}, u32[]{:S(2)}) async-start(f32[16,40,128]{2,1,0:T(8,128)} %broadcast_in_dim.39), calls=%async_computation.1 | async-start | bytes 655360 | tf_op jit(solution)/shard_map/all_to_all | solution.py:376
  49.2 0.7 collective-permute-start
  49.9 27.8 %collective-permute-start.1 = (f32[1,2,32,128]{3,2,1,0:T(8,128)S(1)}, f32[1,2,32,128]{3,2,1,0:T(8,128)S(1)}, u32[]{:S(2)}, u32[]{:S(2)}) collective-permute-start(f32[1,2,32,128]{3,2,1,0:T(8,128)S(1)} %bitcast.34), channel_id=1, source_target_pairs={{0,256},{16,272},{32,288},{48,304},{64,320},{80,336},{96,352},{112... | collective-permute-start | bytes 98312 | tf_op jit(solution)/shard_map/ppermute | solution.py:366
  77.7 1.3 collective-permute-done.1
  79.0 0.0 all-to-all-done.1
  79.1 0.1 broadcast_in_dim.42
  79.1 1.1 pad_maximum_fusion
  80.2 17.0 %all-to-all-start.2 = ((f32[32,72,128]{2,1,0:T(8,128)}), f32[32,72,128]{2,1,0:T(8,128)S(1)}, u32[]{:S(2)}, u32[]{:S(2)}) async-start(f32[32,72,128]{2,1,0:T(8,128)} %pad_maximum_fusion), calls=%async_computation.2 | async-start | bytes 2359296 | tf_op jit(solution)/shard_map/all_to_all | solution.py:387
  97.3 0.0 copy-start.2
  97.3 0.0 copy-start.3
  97.3 3.4 %collective-permute-start.2 = (f32[2,2,32,128]{3,2,1,0:T(8,128)S(1)}, f32[2,2,32,128]{3,2,1,0:T(8,128)S(1)}, u32[]{:S(2)}, u32[]{:S(2)}) collective-permute-start(f32[2,2,32,128]{3,2,1,0:T(8,128)S(1)} %get-tuple-element.41), channel_id=1, source_target_pairs={{0,128},{16,144},{32,160},{48,176},{64,192},{80,208},{96,224},{112... | collective-permute-start | bytes 196616 | tf_op jit(solution)/shard_map/ppermute | solution.py:366
  100.7 10.6 %collective-permute-done.2 = f32[2,2,32,128]{3,2,1,0:T(8,128)S(1)} collective-permute-done((f32[2,2,32,128]{3,2,1,0:T(8,128)S(1)}, f32[2,2,32,128]{3,2,1,0:T(8,128)S(1)}, u32[]{:S(2)}, u32[]{:S(2)}) %collective-permute-start.2) | collective-permute-done | bytes 65568 | tf_op jit(solution)/shard_map/ppermute | solution.py:366
  111.4 1.9 %collective-permute-start.3 = (f32[4,2,32,128]{3,2,1,0:T(8,128)S(1)}, f32[4,2,32,128]{3,2,1,0:T(8,128)S(1)}, u32[]{:S(2)}, u32[]{:S(2)}) collective-permute-start(f32[4,2,32,128]{3,2,1,0:T(8,128)S(1)} %bitcast.29), channel_id=1, source_target_pairs={{0,64},{16,80},{32,96},{48,112},{64,0},{80,16},{96,32},{112,48},{1... | collective-permute-start | bytes 393224 | tf_op jit(solution)/shard_map/ppermute | solution.py:366
  113.3 7.3 %collective-permute-done.3 = f32[4,2,32,128]{3,2,1,0:T(8,128)S(1)} collective-permute-done((f32[4,2,32,128]{3,2,1,0:T(8,128)S(1)}, f32[4,2,32,128]{3,2,1,0:T(8,128)S(1)}, u32[]{:S(2)}, u32[]{:S(2)}) %collective-permute-start.3) | collective-permute-done | bytes 131104 | tf_op jit(solution)/shard_map/ppermute | solution.py:366
  120.7 2.1 %collective-permute-start.4 = (f32[8,2,32,128]{3,2,1,0:T(8,128)S(1)}, f32[8,2,32,128]{3,2,1,0:T(8,128)S(1)}, u32[]{:S(2)}, u32[]{:S(2)}) collective-permute-start(f32[8,2,32,128]{3,2,1,0:T(8,128)S(1)} %bitcast.27), channel_id=1, source_target_pairs={{0,32},{16,48},{32,0},{48,16},{64,96},{80,112},{96,64},{112,80},{1... | collective-permute-start | bytes 786440 | tf_op jit(solution)/shard_map/ppermute | solution.py:366
  122.8 12.9 %early.1 = (f32[512,512]{1,0:T(8,128)S(1)}, f32[4,4,128,128]{3,2,1,0:T(8,128)S(1)}, f32[4,4,128,128]{3,2,1,0:T(8,128)S(1)}, f32[4,264,128]{2,1,0:T(8,128)S(1)}, f32[128,512]{1,0:T(8,128)S(1)}) custom-call(f32[32,72,128]{2,1,0:T(8,128)S(1)} %all-to-all-done.2.got_ref, f32[4,128]{1,0:T(4,128)S(1)} %reshape.43.values_ref, f32[4,128]{1,0:T(4,128)S(1)} %reshape.44.variance_ref), custom_call_target="tpu_custom_call" | custom-call | flops 1073741824 | bytes 1048576 | tf_op jit(solution)/shard_map/early/pallas_call | solution.py:400
  135.8 0.0 copy-start
  135.8 2.7 %collective-permute-start.5 = (f32[16,2,32,128]{3,2,1,0:T(8,128)S(1)}, f32[16,2,32,128]{3,2,1,0:T(8,128)S(1)}, u32[]{:S(2)}, u32[]{:S(2)}) collective-permute-start(f32[16,2,32,128]{3,2,1,0:T(8,128)S(1)} %bitcast.22), channel_id=1, source_target_pairs={{0,16},{16,0},{32,48},{48,32},{64,80},{80,64},{96,112},{112,96},{1... | collective-permute-start | bytes 1572872 | tf_op jit(solution)/shard_map/ppermute | solution.py:366
  138.6 5.8 %late.1 = (f32[512,512]{1,0:T(8,128)S(1)}, f32[4,4,128,128]{3,2,1,0:T(8,128)S(1)}, f32[4,4,128,128]{3,2,1,0:T(8,128)S(1)}, f32[4,264,128]{2,1,0:T(8,128)S(1)}, f32[128,512]{1,0:T(8,128)S(1)}, /*index=5*/f32[1,256]{1,0:T(1,128)}) custom-call(f32[1,256]{1,0:T(1,128)S(1)} %bitcast.25, ...), custom_call_target="tpu_custom_call", output_to_operand_aliasing={{0}: (1, {}), {1}: (2, {}), {2}: (3, {}), {3}: (4, {}), {4}... | custom-call | flops 1073741824 | bytes 1048576 | tf_op jit(solution)/shard_map/late/pallas_call | solution.py:406
  144.4 3.7 %update.1 = f32[256,512]{1,0:T(8,128)} custom-call(f32[256,512]{1,0:T(8,128)S(1)} %copy-done, f32[16,2,32,128]{3,2,1,0:T(8,128)S(1)} %bitcast.23, f32[16,2,32,128]{3,2,1,0:T(8,128)S(1)} %collective-permute-done.5.other_ref, f32[512,512]{1,0:T(8,128)S(1)} %get-tuple-element.37.linv_ref, f32[4,264,128]{2,1,0:T(8,128)S(1)} %get-tuple-element.38.e_ref), custom_call_target="tpu_custom_call" | custom-call | flops 2147483648 | bytes 1048576 | tf_op jit(solution)/shard_map/update/pallas_call | solution.py:415
  (19 shorter events, 0.2 us)
Async XLA Ops:
  36.2 42.8 %all-to-all-start.1 = ((f32[16,40,128]{2,1,0:T(8,128)}), f32[16,40,128]{2,1,0:T(8,128)S(1)}, u32[]{:S(2)}, u32[]{:S(2)}) async-start(f32[16,40,128]{2,1,0:T(8,128)} %broadcast_in_dim.39), calls=%async_computation.1 | async-start | bytes 655360 | tf_op jit(solution)/shard_map/all_to_all | solution.py:376
  49.2 0.7 collective-permute-start
  49.9 29.1 %collective-permute-start.1 = (f32[1,2,32,128]{3,2,1,0:T(8,128)S(1)}, f32[1,2,32,128]{3,2,1,0:T(8,128)S(1)}, u32[]{:S(2)}, u32[]{:S(2)}) collective-permute-start(f32[1,2,32,128]{3,2,1,0:T(8,128)S(1)} %bitcast.34), channel_id=1, source_target_pairs={{0,256},{16,272},{32,288},{48,304},{64,320},{80,336},{96,352},{112... | collective-permute-start | bytes 98312 | tf_op jit(solution)/shard_map/ppermute | solution.py:366
  80.2 40.4 %all-to-all-start.2 = ((f32[32,72,128]{2,1,0:T(8,128)}), f32[32,72,128]{2,1,0:T(8,128)S(1)}, u32[]{:S(2)}, u32[]{:S(2)}) async-start(f32[32,72,128]{2,1,0:T(8,128)} %pad_maximum_fusion), calls=%async_computation.2 | async-start | bytes 2359296 | tf_op jit(solution)/shard_map/all_to_all | solution.py:387
  97.3 25.5 %copy-start.2 = (f32[2,256]{1,0:T(2,128)S(1)}, f32[2,256]{1,0:T(2,128)}, u32[]{:S(2)}) copy-start(f32[2,256]{1,0:T(2,128)} %param.8) | copy-start | bytes 6148
  97.3 25.5 %copy-start.3 = (f32[2,256]{1,0:T(2,128)S(1)}, f32[2,256]{1,0:T(2,128)}, u32[]{:S(2)}) copy-start(f32[2,256]{1,0:T(2,128)} %param.11) | copy-start | bytes 6148
  97.3 14.1 %collective-permute-start.2 = (f32[2,2,32,128]{3,2,1,0:T(8,128)S(1)}, f32[2,2,32,128]{3,2,1,0:T(8,128)S(1)}, u32[]{:S(2)}, u32[]{:S(2)}) collective-permute-start(f32[2,2,32,128]{3,2,1,0:T(8,128)S(1)} %get-tuple-element.41), channel_id=1, source_target_pairs={{0,128},{16,144},{32,160},{48,176},{64,192},{80,208},{96,224},{112... | collective-permute-start | bytes 196616 | tf_op jit(solution)/shard_map/ppermute | solution.py:366
  111.4 9.2 %collective-permute-start.3 = (f32[4,2,32,128]{3,2,1,0:T(8,128)S(1)}, f32[4,2,32,128]{3,2,1,0:T(8,128)S(1)}, u32[]{:S(2)}, u32[]{:S(2)}) collective-permute-start(f32[4,2,32,128]{3,2,1,0:T(8,128)S(1)} %bitcast.29), channel_id=1, source_target_pairs={{0,64},{16,80},{32,96},{48,112},{64,0},{80,16},{96,32},{112,48},{1... | collective-permute-start | bytes 393224 | tf_op jit(solution)/shard_map/ppermute | solution.py:366
  120.7 15.1 %collective-permute-start.4 = (f32[8,2,32,128]{3,2,1,0:T(8,128)S(1)}, f32[8,2,32,128]{3,2,1,0:T(8,128)S(1)}, u32[]{:S(2)}, u32[]{:S(2)}) collective-permute-start(f32[8,2,32,128]{3,2,1,0:T(8,128)S(1)} %bitcast.27), channel_id=1, source_target_pairs={{0,32},{16,48},{32,0},{48,16},{64,96},{80,112},{96,64},{112,80},{1... | collective-permute-start | bytes 786440 | tf_op jit(solution)/shard_map/ppermute | solution.py:366
  122.8 15.8 %copy-start.1 = (f32[256]{0:T(256)S(1)}, f32[256]{0:T(256)}, u32[]{:S(2)}) copy-start(f32[256]{0:T(256)} %param.7) | copy-start | bytes 3076
  135.8 8.6 %copy-start = (f32[256,512]{1,0:T(8,128)S(1)}, f32[256,512]{1,0:T(8,128)}, u32[]{:S(2)}) copy-start(f32[256,512]{1,0:T(8,128)} %cov_ref.1) | copy-start | bytes 1572868
  135.8 8.6 %collective-permute-start.5 = (f32[16,2,32,128]{3,2,1,0:T(8,128)S(1)}, f32[16,2,32,128]{3,2,1,0:T(8,128)S(1)}, u32[]{:S(2)}, u32[]{:S(2)}) collective-permute-start(f32[16,2,32,128]{3,2,1,0:T(8,128)S(1)} %bitcast.22), channel_id=1, source_target_pairs={{0,16},{16,0},{32,48},{48,32},{64,80},{80,64},{96,112},{112,96},{1... | collective-permute-start | bytes 1572872 | tf_op jit(solution)/shard_map/ppermute | solution.py:366

commit v8 on v7

--- a/solution.py
+++ b/solution.py
@@ -279,7 +279,12 @@
 
 def early_kernel(got_ref, values_ref, variance_ref, linv_ref, a_ref, l_ref, e_ref, y_ref):
     prepare(got_ref, values_ref, variance_ref, linv_ref, a_ref, e_ref)
-    factor_steps(0, a_ref.shape[0] - 1, linv_ref, a_ref, l_ref, e_ref, y_ref)
+    factor_steps(0, a_ref.shape[0] - 2, linv_ref, a_ref, l_ref, e_ref, y_ref)
+
+
+def middle_kernel(linv_in, a_in, l_in, e_in, y_in, linv_ref, a_ref, l_ref, e_ref, y_ref):
+    nb = a_ref.shape[0]
+    factor_steps(nb - 2, nb - 1, linv_ref, a_ref, l_ref, e_ref, y_ref)
 
 
 def late_kernel(
@@ -362,31 +367,29 @@
     c_own = jnp.sum(got[:, s_rows:].reshape(2, n_col, c_rows, LANES), axis=1)
 
     s_send = jnp.broadcast_to(s_chunk[None], (n_z, s_rows, LANES))
+    s_all = lax.all_to_all(s_send, "row", 0, 0, axis_index_groups=z_groups)
+    c_tr = lax.ppermute(c_own, ("row", "col"), pairs)
+    send2 = jnp.concatenate(
+        [
+            jnp.broadcast_to(jnp.sum(s_all, axis=0)[None], (plane, s_rows, LANES)),
+            jnp.broadcast_to(c_own[:, None], (2, n_col, c_rows, LANES)).reshape(plane, c_rows, LANES),
+        ],
+        axis=1,
+    )
+    send2, c_tr = lax.optimization_barrier((send2, c_tr))
+    got2 = lax.all_to_all(send2, ("row", "col"), 0, 0, axis_index_groups=plane_groups)
+
     def partner(x, bit):
         return lax.ppermute(x, "row", [(i, i ^ bit) for i in range(n_row)])
 
     def doubled(x, theirs):
-        return jnp.concatenate([x[:, None], theirs[:, None]], axis=1).reshape((-1,) + c_own.shape)
+        return jnp.concatenate([x[:, None], theirs[:, None]], axis=1).reshape((-1,) + c_tr.shape)
 
     bits = []
     while 1 << len(bits) < n_z:
         bits.append(2 << len(bits))
-    pieces = lax.ppermute(c_own, ("row", "col"), pairs)[None]
-    theirs = partner(pieces, bits[-1])
-    s_all = lax.all_to_all(s_send, "row", 0, 0, axis_index_groups=z_groups)
-    s_all, pieces, theirs = lax.optimization_barrier((s_all, pieces, theirs))
-    pieces = doubled(pieces, theirs)
-    s_full = jnp.sum(s_all, axis=0)
-    send2 = jnp.concatenate(
-        [
-            jnp.broadcast_to(s_full[None], (plane, s_rows, LANES)),
-            jnp.broadcast_to(c_own[:, None], (2, n_col, c_rows, LANES)).reshape(plane, c_rows, LANES),
-        ],
-        axis=1,
-    )
-    got2 = lax.all_to_all(send2, ("row", "col"), 0, 0, axis_index_groups=plane_groups)
-
-    for bit in bits[-2:0:-1]:
+    pieces = c_tr[None]
+    for bit in bits[:2:-1]:
         pieces = doubled(pieces, partner(pieces, bit))
     got2, pieces = lax.optimization_barrier((got2, pieces))
     state = (
@@ -396,13 +399,24 @@
         shape(nb, rows + SUB, LANES),
         shape(LANES, m),
     )
-    theirs = partner(pieces, bits[0])
+    theirs = partner(pieces, bits[2])
     held = call(early_kernel, state, [VMEM] * 3, flops=1 << 30, name="early")(
         got2, obs_values.reshape(nb, LANES), obs_variance.reshape(nb, LANES)
     )
     held, theirs = lax.optimization_barrier((held, theirs))
     pieces = doubled(pieces, theirs)
-    other = partner(pieces, 1)
+    theirs = partner(pieces, bits[1])
+    held = call(
+        middle_kernel,
+        state,
+        [VMEM] * 5,
+        flops=1 << 30,
+        name="middle",
+        aliases={n: n for n in range(len(state))},
+    )(*held)
+    held, theirs = lax.optimization_barrier((held, theirs))
+    pieces = doubled(pieces, theirs)
+    theirs = partner(pieces, bits[0])
     out = call(
         late_kernel,
         state + (shape(1, rows),),
@@ -411,6 +425,9 @@
         name="late",
         aliases={n + 1: n for n in range(len(state))},
     )(mean, *held)
+    out, theirs = lax.optimization_barrier((out, theirs))
+    pieces = doubled(pieces, theirs)
+    other = partner(pieces, 1)
     linv, e, after = out[0], out[3], out[5]
     updated = call(
         update_kernel,

time: 149 us -> 141 us (0.946)
  starting transfers between devices: 68.6 us -> 46.2 us
  waiting for transfers between devices: 19.2 us -> 33.8 us
    ppermute x5, starting transfers between devices: 38 us -> 16.7 us  [partner(): return lax.ppermute(x, 'row', [(i, i ^ bit) for i in range(n_row)])]
    all_to_all x1, waiting for transfers between devices: 0.01 us -> 14.5 us  [on_device(): s_all = lax.all_to_all(s_send, 'row', 0, 0, axis_index_groups=z_groups)]
    pallas_call x1, Pallas kernels: 12.9 us -> 8.45 us  [on_device(): call(early_kernel, state, [VMEM] * 3, flops=1 << 30, name='early')]
    all_to_all x1, waiting for transfers between devices: 0.01 us -> 4.36 us  [on_device(): lax.all_to_all(send2, ('row', 'col'), 0, 0, axis_index_groups=plane_groups)]
    pallas_call x0 -> x1, Pallas kernels: none -> 4.32 us  [on_device(): call(middle_kernel, state, [VMEM] * 5, flops=1 << 30, name='middle', alia...]
    ppermute x5, waiting for transfers between devices: 19.2 us -> 14.9 us  [partner(): return lax.ppermute(x, 'row', [(i, i ^ bit) for i in range(n_row)])]
  transfers between devices with their start and end apart: 8 -> 8, of which waited for: 3 -> 7; matrix products, arithmetic and copies ran while one was open for 0% -> 1% of each run, Pallas kernels for 13% -> 13%
where the time goes in v8:
time: 141 us; the launch traced here: 140 us
  starting transfers between devices  46.2 us (33%)
  waiting for transfers between devices  33.8 us (24%)
  blocking collectives  29.5 us (21%)
  Pallas kernels  27.7 us (20%)
    all_to_all x1, blocking collectives, on_device(): lax.all_to_all(send, ('row', 'col'), 0, 0, axis_index_groups=plane_groups)  29.5 us
    ppermute x5, starting transfers between devices, partner(): return lax.ppermute(x, 'row', [(i, i ^ bit) for i in range(n_row)])  16.7 us
    all_to_all x1, starting transfers between devices, on_device(): lax.all_to_all(send2, ('row', 'col'), 0, 0, axis_index_groups=plane_groups)  15.9 us
    ppermute x5, waiting for transfers between devices, partner(): return lax.ppermute(x, 'row', [(i, i ^ bit) for i in range(n_row)])  14.9 us
    all_to_all x1, waiting for transfers between devices, on_device(): s_all = lax.all_to_all(s_send, 'row', 0, 0, axis_index_groups=z_groups)  14.5 us
    all_to_all x1, starting transfers between devices, on_device(): s_all = lax.all_to_all(s_send, 'row', 0, 0, axis_index_groups=z_groups)  12.9 us
    pallas_call x1, Pallas kernels, on_device(): call(early_kernel, state, [VMEM] * 3, flops=1 << 30, name='early')  8.45 us
    pallas_call x1, Pallas kernels, on_device(): call(late_kernel, state + (shape(1, rows),), [VMEM] * 6, flops=1 << 30, n...  5.84 us
  transfers between devices with their start and end apart: 8, of which 7 were waited for; matrix products, arithmetic and copies ran while one was open for 1% of the time, Pallas kernels for 13%

profile of v8, /device:TPU:1, one launch (start us, length us, event | category | flops | bytes accessed | tf_op | source)
XLA Modules:
  0.0 140.1 jit_solution(8775667594620399503)
XLA Ops:
  0.6 5.3 %project.1 = f32[32,72,128]{2,1,0:T(8,128)} custom-call(f32[256,512]{1,0:T(8,128)} %cov_ref.1, f32[1,256]{1,0:T(1,128)} %bitcast.21, s32[2,4,256]{2,1,0:T(4,128)} %cells_in.1, f32[2,4,256]{2,1,0:T(4,128)} %weights_in.1), custom_call_target="tpu_custom_call" | custom-call | flops 268435456 | bytes 1048576 | tf_op jit(solution)/shard_map/project/pallas_call | solution.py:348
  6.0 29.5 %all_to_all.15 = f32[32,72,128]{2,1,0:T(8,128)S(1)} all-to-all(f32[32,72,128]{2,1,0:T(8,128)} %project.1), channel_id=1, replica_groups={{0,1,2,3,4,5,6,7,8,9,10,11,12,13,14,15,16,17,18,19,20,21,22,23,24,25,26..., dimensions={0} | all-to-all | bytes 2359296 | tf_op jit(solution)/shard_map/all_to_all | solution.py:365
  35.4 0.1 slice_reduce_fusion
  35.5 0.7 broadcast_in_dim.36
  36.2 12.9 %all-to-all-start.1 = ((f32[16,40,128]{2,1,0:T(8,128)}), f32[16,40,128]{2,1,0:T(8,128)S(1)}, u32[]{:S(2)}, u32[]{:S(2)}) async-start(f32[16,40,128]{2,1,0:T(8,128)} %broadcast_in_dim.36), calls=%async_computation.1 | async-start | bytes 655360 | tf_op jit(solution)/shard_map/all_to_all | solution.py:370
  49.2 0.7 collective-permute-start
  49.9 14.5 %all-to-all-done.1 = f32[16,40,128]{2,1,0:T(8,128)S(1)} async-done(((f32[16,40,128]{2,1,0:T(8,128)}), f32[16,40,128]{2,1,0:T(8,128)S(1)}, u32[]{:S(2)}, u32[]{:S(2)}) %all-to-all-start.1) | async-done | bytes 327712 | tf_op jit(solution)/shard_map/all_to_all | solution.py:370
  64.5 1.1 pad_maximum_fusion
  65.6 15.9 %all-to-all-start.2 = ((f32[32,72,128]{2,1,0:T(8,128)}), f32[32,72,128]{2,1,0:T(8,128)S(1)}, u32[]{:S(2)}, u32[]{:S(2)}) async-start(f32[32,72,128]{2,1,0:T(8,128)} %pad_maximum_fusion), calls=%async_computation.2 | async-start | bytes 2359296 | tf_op jit(solution)/shard_map/all_to_all | solution.py:380
  81.5 5.5 %collective-permute-start.1 = (f32[1,2,32,128]{3,2,1,0:T(8,128)S(1)}, f32[1,2,32,128]{3,2,1,0:T(8,128)S(1)}, u32[]{:S(2)}, u32[]{:S(2)}) collective-permute-start(f32[1,2,32,128]{3,2,1,0:T(8,128)S(1)} %bitcast.32), channel_id=1, source_target_pairs={{0,256},{16,272},{32,288},{48,304},{64,320},{80,336},{96,352},{112... | collective-permute-start | bytes 98312 | tf_op jit(solution)/shard_map/ppermute | solution.py:383
  87.1 7.8 %collective-permute-done.1 = f32[1,2,32,128]{3,2,1,0:T(8,128)S(1)} collective-permute-done((f32[1,2,32,128]{3,2,1,0:T(8,128)S(1)}, f32[1,2,32,128]{3,2,1,0:T(8,128)S(1)}, u32[]{:S(2)}, u32[]{:S(2)}) %collective-permute-start.1) | collective-permute-done | bytes 32800 | tf_op jit(solution)/shard_map/ppermute | solution.py:383
  94.9 4.4 %all-to-all-done.2.got_ref = f32[32,72,128]{2,1,0:T(8,128)S(1)} async-done(((f32[32,72,128]{2,1,0:T(8,128)}), f32[32,72,128]{2,1,0:T(8,128)S(1)}, u32[]{:S(2)}, u32[]{:S(2)}) %all-to-all-start.2) | async-done | bytes 1179680 | tf_op jit(solution)/shard_map/all_to_all | solution.py:380
  99.2 3.4 %collective-permute-start.2 = (f32[2,2,32,128]{3,2,1,0:T(8,128)S(1)}, f32[2,2,32,128]{3,2,1,0:T(8,128)S(1)}, u32[]{:S(2)}, u32[]{:S(2)}) collective-permute-start(f32[2,2,32,128]{3,2,1,0:T(8,128)S(1)} %maximum_bitcast_fusion), channel_id=1, source_target_pairs={{0,128},{16,144},{32,160},{48,176},{64,192},{80,208},{96,224},{112... | collective-permute-start | bytes 196616 | tf_op jit(solution)/shard_map/ppermute | solution.py:383
  102.6 8.4 %early.1 = (f32[512,512]{1,0:T(8,128)S(1)}, f32[4,4,128,128]{3,2,1,0:T(8,128)S(1)}, f32[4,4,128,128]{3,2,1,0:T(8,128)S(1)}, f32[4,264,128]{2,1,0:T(8,128)S(1)}, f32[128,512]{1,0:T(8,128)S(1)}) custom-call(f32[32,72,128]{2,1,0:T(8,128)S(1)} %all-to-all-done.2.got_ref, f32[4,128]{1,0:T(4,128)S(1)} %reshape.41.values_ref, f32[4,128]{1,0:T(4,128)S(1)} %reshape.42.variance_ref), custom_call_target="tpu_custom_call" | custom-call | flops 1073741824 | bytes 1048576 | tf_op jit(solution)/shard_map/early/pallas_call | solution.py:403
  111.0 1.2 collective-permute-done.2
  112.3 1.9 %collective-permute-start.3 = (f32[4,2,32,128]{3,2,1,0:T(8,128)S(1)}, f32[4,2,32,128]{3,2,1,0:T(8,128)S(1)}, u32[]{:S(2)}, u32[]{:S(2)}) collective-permute-start(f32[4,2,32,128]{3,2,1,0:T(8,128)S(1)} %bitcast.26), channel_id=1, source_target_pairs={{0,64},{16,80},{32,96},{48,112},{64,0},{80,16},{96,32},{112,48},{1... | collective-permute-start | bytes 393224 | tf_op jit(solution)/shard_map/ppermute | solution.py:383
  114.2 4.3 %middle.1 = (f32[512,512]{1,0:T(8,128)S(1)}, f32[4,4,128,128]{3,2,1,0:T(8,128)S(1)}, f32[4,4,128,128]{3,2,1,0:T(8,128)S(1)}, f32[4,264,128]{2,1,0:T(8,128)S(1)}, f32[128,512]{1,0:T(8,128)S(1)}) custom-call(f32[512,512]{1,0:T(8,128)S(1)} %get-tuple-element.45.linv_in, ...), custom_call_target="tpu_custom_call", output_to_operand_aliasing={{0}: (0, {}), {1}: (1, {}), {2}: (2, {}), {3}: (3, {}), {4}... | custom-call | flops 1073741824 | bytes 1048576 | tf_op jit(solution)/shard_map/middle/pallas_call | solution.py:409
  118.6 3.6 %collective-permute-done.3 = f32[4,2,32,128]{3,2,1,0:T(8,128)S(1)} collective-permute-done((f32[4,2,32,128]{3,2,1,0:T(8,128)S(1)}, f32[4,2,32,128]{3,2,1,0:T(8,128)S(1)}, u32[]{:S(2)}, u32[]{:S(2)}) %collective-permute-start.3) | collective-permute-done | bytes 131104 | tf_op jit(solution)/shard_map/ppermute | solution.py:383
  122.2 2.3 %collective-permute-start.4 = (f32[8,2,32,128]{3,2,1,0:T(8,128)S(1)}, f32[8,2,32,128]{3,2,1,0:T(8,128)S(1)}, u32[]{:S(2)}, u32[]{:S(2)}) collective-permute-start(f32[8,2,32,128]{3,2,1,0:T(8,128)S(1)} %bitcast.24), channel_id=1, source_target_pairs={{0,32},{16,48},{32,0},{48,16},{64,96},{80,112},{96,64},{112,80},{1... | collective-permute-start | bytes 786440 | tf_op jit(solution)/shard_map/ppermute | solution.py:383
  124.4 5.8 %late.1 = (f32[512,512]{1,0:T(8,128)S(1)}, f32[4,4,128,128]{3,2,1,0:T(8,128)S(1)}, f32[4,4,128,128]{3,2,1,0:T(8,128)S(1)}, f32[4,264,128]{2,1,0:T(8,128)S(1)}, f32[128,512]{1,0:T(8,128)S(1)}, /*index=5*/f32[1,256]{1,0:T(1,128)}) custom-call(f32[1,256]{1,0:T(1,128)S(1)} %bitcast.22, ...), custom_call_target="tpu_custom_call", output_to_operand_aliasing={{0}: (1, {}), {1}: (2, {}), {2}: (3, {}), {3}: (4, {}), {4}... | custom-call | flops 1073741824 | bytes 1048576 | tf_op jit(solution)/shard_map/late/pallas_call | solution.py:420
  130.3 0.9 collective-permute-done.4
  131.2 3.6 %collective-permute-start.5 = (f32[16,2,32,128]{3,2,1,0:T(8,128)S(1)}, f32[16,2,32,128]{3,2,1,0:T(8,128)S(1)}, u32[]{:S(2)}, u32[]{:S(2)}) collective-permute-start(f32[16,2,32,128]{3,2,1,0:T(8,128)S(1)} %bitcast.19), channel_id=1, source_target_pairs={{0,16},{16,0},{32,48},{48,32},{64,80},{80,64},{96,112},{112,96},{1... | collective-permute-start | bytes 1572872 | tf_op jit(solution)/shard_map/ppermute | solution.py:383
  134.9 1.5 %collective-permute-done.5.other_ref = f32[16,2,32,128]{3,2,1,0:T(8,128)S(1)} collective-permute-done((f32[16,2,32,128]{3,2,1,0:T(8,128)S(1)}, f32[16,2,32,128]{3,2,1,0:T(8,128)S(1)}, u32[]{:S(2)}, u32[]{:S(2)}) %collective-permute-start.5) | collective-permute-done | bytes 524320 | tf_op jit(solution)/shard_map/ppermute | solution.py:383
  136.4 3.7 %update.1 = f32[256,512]{1,0:T(8,128)} custom-call(f32[256,512]{1,0:T(8,128)S(1)} %copy-done, f32[16,2,32,128]{3,2,1,0:T(8,128)S(1)} %bitcast.20, f32[16,2,32,128]{3,2,1,0:T(8,128)S(1)} %collective-permute-done.5.other_ref, f32[512,512]{1,0:T(8,128)S(1)} %get-tuple-element.65.linv_ref, f32[4,264,128]{2,1,0:T(8,128)S(1)} %get-tuple-element.66.e_ref), custom_call_target="tpu_custom_call" | custom-call | flops 2147483648 | bytes 1048576 | tf_op jit(solution)/shard_map/update/pallas_call | solution.py:432
  (20 shorter events, 0.3 us)
Async XLA Ops:
  36.2 28.1 %all-to-all-start.1 = ((f32[16,40,128]{2,1,0:T(8,128)}), f32[16,40,128]{2,1,0:T(8,128)S(1)}, u32[]{:S(2)}, u32[]{:S(2)}) async-start(f32[16,40,128]{2,1,0:T(8,128)} %broadcast_in_dim.36), calls=%async_computation.1 | async-start | bytes 655360 | tf_op jit(solution)/shard_map/all_to_all | solution.py:370
  49.2 16.4 %collective-permute-start = (f32[2,32,128]{2,1,0:T(8,128)S(1)}, f32[2,32,128]{2,1,0:T(8,128)S(1)}, u32[]{:S(2)}, u32[]{:S(2)}) collective-permute-start(f32[2,32,128]{2,1,0:T(8,128)S(1)} %bitcast_reduce_fusion), channel_id=1, source_target_pairs={{0,0},{1,32},{2,64},{3,96},{4,128},{5,160},{6,192},{7,224},{8,256}... | collective-permute-start | bytes 98312 | tf_op jit(solution)/shard_map/ppermute | solution.py:371
  65.6 21.4 %copy-start.2 = (f32[2,256]{1,0:T(2,128)S(1)}, f32[2,256]{1,0:T(2,128)}, u32[]{:S(2)}) copy-start(f32[2,256]{1,0:T(2,128)} %param.8) | copy-start | bytes 6148
  65.6 21.5 %copy-start.3 = (f32[2,256]{1,0:T(2,128)S(1)}, f32[2,256]{1,0:T(2,128)}, u32[]{:S(2)}) copy-start(f32[2,256]{1,0:T(2,128)} %param.11) | copy-start | bytes 6148
  65.6 33.6 %all-to-all-start.2 = ((f32[32,72,128]{2,1,0:T(8,128)}), f32[32,72,128]{2,1,0:T(8,128)S(1)}, u32[]{:S(2)}, u32[]{:S(2)}) async-start(f32[32,72,128]{2,1,0:T(8,128)} %pad_maximum_fusion), calls=%async_computation.2 | async-start | bytes 2359296 | tf_op jit(solution)/shard_map/all_to_all | solution.py:380
  81.5 13.4 %collective-permute-start.1 = (f32[1,2,32,128]{3,2,1,0:T(8,128)S(1)}, f32[1,2,32,128]{3,2,1,0:T(8,128)S(1)}, u32[]{:S(2)}, u32[]{:S(2)}) collective-permute-start(f32[1,2,32,128]{3,2,1,0:T(8,128)S(1)} %bitcast.32), channel_id=1, source_target_pairs={{0,256},{16,272},{32,288},{48,304},{64,320},{80,336},{96,352},{112... | collective-permute-start | bytes 98312 | tf_op jit(solution)/shard_map/ppermute | solution.py:383
  99.2 13.0 %collective-permute-start.2 = (f32[2,2,32,128]{3,2,1,0:T(8,128)S(1)}, f32[2,2,32,128]{3,2,1,0:T(8,128)S(1)}, u32[]{:S(2)}, u32[]{:S(2)}) collective-permute-start(f32[2,2,32,128]{3,2,1,0:T(8,128)S(1)} %maximum_bitcast_fusion), channel_id=1, source_target_pairs={{0,128},{16,144},{32,160},{48,176},{64,192},{80,208},{96,224},{112... | collective-permute-start | bytes 196616 | tf_op jit(solution)/shard_map/ppermute | solution.py:383
  112.3 12.2 %copy-start.1 = (f32[256]{0:T(256)S(1)}, f32[256]{0:T(256)}, u32[]{:S(2)}) copy-start(f32[256]{0:T(256)} %param.7) | copy-start | bytes 3076
  112.3 9.8 %collective-permute-start.3 = (f32[4,2,32,128]{3,2,1,0:T(8,128)S(1)}, f32[4,2,32,128]{3,2,1,0:T(8,128)S(1)}, u32[]{:S(2)}, u32[]{:S(2)}) collective-permute-start(f32[4,2,32,128]{3,2,1,0:T(8,128)S(1)} %bitcast.26), channel_id=1, source_target_pairs={{0,64},{16,80},{32,96},{48,112},{64,0},{80,16},{96,32},{112,48},{1... | collective-permute-start | bytes 393224 | tf_op jit(solution)/shard_map/ppermute | solution.py:383
  122.1 14.2 %copy-start = (f32[256,512]{1,0:T(8,128)S(1)}, f32[256,512]{1,0:T(8,128)}, u32[]{:S(2)}) copy-start(f32[256,512]{1,0:T(8,128)} %cov_ref.1) | copy-start | bytes 1572868
  122.2 9.0 %collective-permute-start.4 = (f32[8,2,32,128]{3,2,1,0:T(8,128)S(1)}, f32[8,2,32,128]{3,2,1,0:T(8,128)S(1)}, u32[]{:S(2)}, u32[]{:S(2)}) collective-permute-start(f32[8,2,32,128]{3,2,1,0:T(8,128)S(1)} %bitcast.24), channel_id=1, source_target_pairs={{0,32},{16,48},{32,0},{48,16},{64,96},{80,112},{96,64},{112,80},{1... | collective-permute-start | bytes 786440 | tf_op jit(solution)/shard_map/ppermute | solution.py:383
  131.2 5.1 %collective-permute-start.5 = (f32[16,2,32,128]{3,2,1,0:T(8,128)S(1)}, f32[16,2,32,128]{3,2,1,0:T(8,128)S(1)}, u32[]{:S(2)}, u32[]{:S(2)}) collective-permute-start(f32[16,2,32,128]{3,2,1,0:T(8,128)S(1)} %bitcast.19), channel_id=1, source_target_pairs={{0,16},{16,0},{32,48},{48,32},{64,80},{80,64},{96,112},{112,96},{1... | collective-permute-start | bytes 1572872 | tf_op jit(solution)/shard_map/ppermute | solution.py:383

commit v9 on v8

--- a/solution.py
+++ b/solution.py
@@ -299,26 +299,33 @@
     after_ref[...] = after[0:1]
 
 
-def update_kernel(cov_ref, mine_ref, other_ref, linv_ref, e_ref, out_ref, c_ref):
-    n_z, halves, tall, _ = mine_ref.shape
-    rows, cols = cov_ref.shape
-    m = c_ref.shape[1]
-    nb = m // LANES
+def half_kernel(pieces_ref, linv_ref, out_ref, c_ref):
+    n_z, halves, tall, _ = pieces_ref.shape
+    nb = c_ref.shape[1] // LANES
     own = tall // nb
-    row = lax.axis_index("row")
-    core = lax.rem(row, 2)
-    z_here = lax.div(row, 2)
-    for ref, k in ((mine_ref, core), (other_ref, 1 - core)):
-        for d in range(n_z):
-            start = pl.multiple_of((k * n_z + lax.bitwise_xor(z_here, d)) * own, own)
-            for h in range(halves):
-                for j in range(nb):
-                    c_ref[pl.ds(start + h * (cols // halves), own), j * LANES:(j + 1) * LANES] = ref[
-                        d, h, j * own:(j + 1) * own, :
-                    ]
-    gain_cols = dot_dims(c_ref[...], linv_ref[...], 1, 1)
-    gain = jnp.concatenate([e_ref[j, 0:rows, :] for j in range(nb)], axis=1)
-    out_ref[...] = cov_ref[...] - dot_dims(gain, gain_cols, 1, 1)
+    here = lax.div(lax.axis_index("row"), 2)
+    for d in range(n_z):
+        start = pl.multiple_of(lax.bitwise_xor(here, d) * own, own)
+        for h in range(halves):
+            for j in range(nb):
+                c_ref[pl.ds(start + h * n_z * own, own), j * LANES:(j + 1) * LANES] = pieces_ref[
+                    d, h, j * own:(j + 1) * own, :
+                ]
+    out_ref[...] = dot_dims(c_ref[...], linv_ref[...], 1, 1)
+
+
+def update_kernel(cov_ref, mine_ref, other_ref, linv_ref, e_ref, out_ref, c_ref, t_ref, g_ref):
+    rows, m = cov_ref.shape[0], c_ref.shape[1]
+    halves = other_ref.shape[1]
+    part = c_ref.shape[0] // halves
+    core = lax.rem(lax.axis_index("row"), 2)
+    half_kernel(other_ref, linv_ref, t_ref, c_ref)
+    for h in range(halves):
+        for k, ref in ((core, mine_ref), (1 - core, t_ref)):
+            start = pl.multiple_of((2 * h + k) * part, part)
+            g_ref[pl.ds(start, part), :] = ref[h * part:(h + 1) * part, :]
+    gain = jnp.concatenate([e_ref[j, 0:rows, :] for j in range(m // LANES)], axis=1)
+    out_ref[...] = cov_ref[...] - dot_dims(gain, g_ref[...], 1, 1)
 
 
 def on_device(covariance, state_mean, obs_values, obs_cells, obs_weights, obs_variance):
@@ -429,14 +436,23 @@
     pieces = doubled(pieces, theirs)
     other = partner(pieces, 1)
     linv, e, after = out[0], out[3], out[5]
+    half = (cols // 2, m)
+    mine = call(
+        half_kernel,
+        shape(*half),
+        [VMEM] * 2,
+        [pltpu.VMEM(half, jnp.float32)],
+        flops=1 << 30,
+        name="half",
+    )(pieces, linv)
     updated = call(
         update_kernel,
         shape(rows, cols),
         [VMEM] * 5,
-        [pltpu.VMEM((cols, m), jnp.float32)],
+        [pltpu.VMEM(half, jnp.float32), pltpu.VMEM(half, jnp.float32), pltpu.VMEM((cols, m), jnp.float32)],
         flops=1 << 31,
         name="update",
-    )(covariance, pieces, other, linv, e)
+    )(covariance, mine, other, linv, e)
     return (updated, after.reshape(rows))
 
 

time: 141 us -> 140 us (level)
    pallas_call x1 -> x2, Pallas kernels: 3.74 us -> 4.18 us  [the longest x1 3.1 us: on_device(): call(update_kernel, shape(rows, cols), [VMEM] * 5, [pltpu.VMEM(half, jnp....]
  transfers between devices with their start and end apart: 8 -> 8, of which waited for: 7 -> 7; matrix products, arithmetic and copies ran while one was open for 1% -> 1% of each run, Pallas kernels for 13% -> 14%
where the time goes in v9:
time: 140 us; the launch traced here: 139 us
  starting transfers between devices  46.2 us (33%)
  waiting for transfers between devices  32.7 us (23%)
  blocking collectives  29.5 us (21%)
  Pallas kernels  28.1 us (20%)
    all_to_all x1, blocking collectives, on_device(): lax.all_to_all(send, ('row', 'col'), 0, 0, axis_index_groups=plane_groups)  29.5 us
    ppermute x5, starting transfers between devices, partner(): return lax.ppermute(x, 'row', [(i, i ^ bit) for i in range(n_row)])  16.7 us
    all_to_all x1, starting transfers between devices, on_device(): lax.all_to_all(send2, ('row', 'col'), 0, 0, axis_index_groups=plane_groups)  15.9 us
    all_to_all x1, waiting for transfers between devices, on_device(): s_all = lax.all_to_all(s_send, 'row', 0, 0, axis_index_groups=z_groups)  14.5 us
    ppermute x5, waiting for transfers between devices, partner(): return lax.ppermute(x, 'row', [(i, i ^ bit) for i in range(n_row)])  13.8 us
    all_to_all x1, starting transfers between devices, on_device(): s_all = lax.all_to_all(s_send, 'row', 0, 0, axis_index_groups=z_groups)  12.9 us
    pallas_call x1, Pallas kernels, on_device(): call(early_kernel, state, [VMEM] * 3, flops=1 << 30, name='early')  8.45 us
    pallas_call x1, Pallas kernels, on_device(): call(late_kernel, state + (shape(1, rows),), [VMEM] * 6, flops=1 << 30, n...  5.84 us
  transfers between devices with their start and end apart: 8, of which 7 were waited for; matrix products, arithmetic and copies ran while one was open for 1% of the time, Pallas kernels for 14%

profile of v9, /device:TPU:1, one launch (start us, length us, event | category | flops | bytes accessed | tf_op | source)
XLA Modules:
  0.0 139.5 jit_solution(2301757160072126502)
XLA Ops:
  0.6 5.3 %project.1 = f32[32,72,128]{2,1,0:T(8,128)} custom-call(f32[256,512]{1,0:T(8,128)} %cov_ref.1, f32[1,256]{1,0:T(1,128)} %bitcast.21, s32[2,4,256]{2,1,0:T(4,128)} %cells_in.1, f32[2,4,256]{2,1,0:T(4,128)} %weights_in.1), custom_call_target="tpu_custom_call" | custom-call | flops 268435456 | bytes 1048576 | tf_op jit(solution)/shard_map/project/pallas_call | solution.py:355
  6.0 29.5 %all_to_all.15 = f32[32,72,128]{2,1,0:T(8,128)S(1)} all-to-all(f32[32,72,128]{2,1,0:T(8,128)} %project.1), channel_id=1, replica_groups={{0,1,2,3,4,5,6,7,8,9,10,11,12,13,14,15,16,17,18,19,20,21,22,23,24,25,26..., dimensions={0} | all-to-all | bytes 2359296 | tf_op jit(solution)/shard_map/all_to_all | solution.py:372
  35.5 0.7 broadcast_in_dim.36
  36.2 12.9 %all-to-all-start.1 = ((f32[16,40,128]{2,1,0:T(8,128)}), f32[16,40,128]{2,1,0:T(8,128)S(1)}, u32[]{:S(2)}, u32[]{:S(2)}) async-start(f32[16,40,128]{2,1,0:T(8,128)} %broadcast_in_dim.36), calls=%async_computation.1 | async-start | bytes 655360 | tf_op jit(solution)/shard_map/all_to_all | solution.py:377
  49.2 0.7 collective-permute-start
  49.9 14.5 %all-to-all-done.1 = f32[16,40,128]{2,1,0:T(8,128)S(1)} async-done(((f32[16,40,128]{2,1,0:T(8,128)}), f32[16,40,128]{2,1,0:T(8,128)S(1)}, u32[]{:S(2)}, u32[]{:S(2)}) %all-to-all-start.1) | async-done | bytes 327712 | tf_op jit(solution)/shard_map/all_to_all | solution.py:377
  64.5 1.1 pad_maximum_fusion
  65.6 15.9 %all-to-all-start.2 = ((f32[32,72,128]{2,1,0:T(8,128)}), f32[32,72,128]{2,1,0:T(8,128)S(1)}, u32[]{:S(2)}, u32[]{:S(2)}) async-start(f32[32,72,128]{2,1,0:T(8,128)} %pad_maximum_fusion), calls=%async_computation.2 | async-start | bytes 2359296 | tf_op jit(solution)/shard_map/all_to_all | solution.py:387
  81.5 5.5 %collective-permute-start.1 = (f32[1,2,32,128]{3,2,1,0:T(8,128)S(1)}, f32[1,2,32,128]{3,2,1,0:T(8,128)S(1)}, u32[]{:S(2)}, u32[]{:S(2)}) collective-permute-start(f32[1,2,32,128]{3,2,1,0:T(8,128)S(1)} %bitcast.32), channel_id=1, source_target_pairs={{0,256},{16,272},{32,288},{48,304},{64,320},{80,336},{96,352},{112... | collective-permute-start | bytes 98312 | tf_op jit(solution)/shard_map/ppermute | solution.py:390
  87.1 7.8 %collective-permute-done.1 = f32[1,2,32,128]{3,2,1,0:T(8,128)S(1)} collective-permute-done((f32[1,2,32,128]{3,2,1,0:T(8,128)S(1)}, f32[1,2,32,128]{3,2,1,0:T(8,128)S(1)}, u32[]{:S(2)}, u32[]{:S(2)}) %collective-permute-start.1) | collective-permute-done | bytes 32800 | tf_op jit(solution)/shard_map/ppermute | solution.py:390
  94.9 4.4 %all-to-all-done.2.got_ref = f32[32,72,128]{2,1,0:T(8,128)S(1)} async-done(((f32[32,72,128]{2,1,0:T(8,128)}), f32[32,72,128]{2,1,0:T(8,128)S(1)}, u32[]{:S(2)}, u32[]{:S(2)}) %all-to-all-start.2) | async-done | bytes 1179680 | tf_op jit(solution)/shard_map/all_to_all | solution.py:387
  99.2 3.4 %collective-permute-start.2 = (f32[2,2,32,128]{3,2,1,0:T(8,128)S(1)}, f32[2,2,32,128]{3,2,1,0:T(8,128)S(1)}, u32[]{:S(2)}, u32[]{:S(2)}) collective-permute-start(f32[2,2,32,128]{3,2,1,0:T(8,128)S(1)} %maximum_bitcast_fusion), channel_id=1, source_target_pairs={{0,128},{16,144},{32,160},{48,176},{64,192},{80,208},{96,224},{112... | collective-permute-start | bytes 196616 | tf_op jit(solution)/shard_map/ppermute | solution.py:390
  102.6 8.4 %early.1 = (f32[512,512]{1,0:T(8,128)S(1)}, f32[4,4,128,128]{3,2,1,0:T(8,128)S(1)}, f32[4,4,128,128]{3,2,1,0:T(8,128)S(1)}, f32[4,264,128]{2,1,0:T(8,128)S(1)}, f32[128,512]{1,0:T(8,128)S(1)}) custom-call(f32[32,72,128]{2,1,0:T(8,128)S(1)} %all-to-all-done.2.got_ref, f32[4,128]{1,0:T(4,128)S(1)} %reshape.41.values_ref, f32[4,128]{1,0:T(4,128)S(1)} %reshape.42.variance_ref), custom_call_target="tpu_custom_call" | custom-call | flops 1073741824 | bytes 1048576 | tf_op jit(solution)/shard_map/early/pallas_call | solution.py:410
  111.0 1.2 collective-permute-done.2
  112.3 1.9 %collective-permute-start.3 = (f32[4,2,32,128]{3,2,1,0:T(8,128)S(1)}, f32[4,2,32,128]{3,2,1,0:T(8,128)S(1)}, u32[]{:S(2)}, u32[]{:S(2)}) collective-permute-start(f32[4,2,32,128]{3,2,1,0:T(8,128)S(1)} %bitcast.26), channel_id=1, source_target_pairs={{0,64},{16,80},{32,96},{48,112},{64,0},{80,16},{96,32},{112,48},{1... | collective-permute-start | bytes 393224 | tf_op jit(solution)/shard_map/ppermute | solution.py:390
  114.2 4.3 %middle.1 = (f32[512,512]{1,0:T(8,128)S(1)}, f32[4,4,128,128]{3,2,1,0:T(8,128)S(1)}, f32[4,4,128,128]{3,2,1,0:T(8,128)S(1)}, f32[4,264,128]{2,1,0:T(8,128)S(1)}, f32[128,512]{1,0:T(8,128)S(1)}) custom-call(f32[512,512]{1,0:T(8,128)S(1)} %get-tuple-element.45.linv_in, ...), custom_call_target="tpu_custom_call", output_to_operand_aliasing={{0}: (0, {}), {1}: (1, {}), {2}: (2, {}), {3}: (3, {}), {4}... | custom-call | flops 1073741824 | bytes 1048576 | tf_op jit(solution)/shard_map/middle/pallas_call | solution.py:416
  118.6 3.6 %collective-permute-done.3 = f32[4,2,32,128]{3,2,1,0:T(8,128)S(1)} collective-permute-done((f32[4,2,32,128]{3,2,1,0:T(8,128)S(1)}, f32[4,2,32,128]{3,2,1,0:T(8,128)S(1)}, u32[]{:S(2)}, u32[]{:S(2)}) %collective-permute-start.3) | collective-permute-done | bytes 131104 | tf_op jit(solution)/shard_map/ppermute | solution.py:390
  122.1 2.1 %collective-permute-start.4 = (f32[8,2,32,128]{3,2,1,0:T(8,128)S(1)}, f32[8,2,32,128]{3,2,1,0:T(8,128)S(1)}, u32[]{:S(2)}, u32[]{:S(2)}) collective-permute-start(f32[8,2,32,128]{3,2,1,0:T(8,128)S(1)} %bitcast.24), channel_id=1, source_target_pairs={{0,32},{16,48},{32,0},{48,16},{64,96},{80,112},{96,64},{112,80},{1... | collective-permute-start | bytes 786440 | tf_op jit(solution)/shard_map/ppermute | solution.py:390
  124.3 5.8 %late.1 = (f32[512,512]{1,0:T(8,128)S(1)}, f32[4,4,128,128]{3,2,1,0:T(8,128)S(1)}, f32[4,4,128,128]{3,2,1,0:T(8,128)S(1)}, f32[4,264,128]{2,1,0:T(8,128)S(1)}, f32[128,512]{1,0:T(8,128)S(1)}, /*index=5*/f32[1,256]{1,0:T(1,128)}) custom-call(f32[1,256]{1,0:T(1,128)S(1)} %bitcast.22, ...), custom_call_target="tpu_custom_call", output_to_operand_aliasing={{0}: (1, {}), {1}: (2, {}), {2}: (3, {}), {3}: (4, {}), {4}... | custom-call | flops 1073741824 | bytes 1048576 | tf_op jit(solution)/shard_map/late/pallas_call | solution.py:427
  130.1 0.9 collective-permute-done.4
  131.1 3.8 %collective-permute-start.5 = (f32[16,2,32,128]{3,2,1,0:T(8,128)S(1)}, f32[16,2,32,128]{3,2,1,0:T(8,128)S(1)}, u32[]{:S(2)}, u32[]{:S(2)}) collective-permute-start(f32[16,2,32,128]{3,2,1,0:T(8,128)S(1)} %bitcast.19), channel_id=1, source_target_pairs={{0,16},{16,0},{32,48},{48,32},{64,80},{80,64},{96,112},{112,96},{1... | collective-permute-start | bytes 1572872 | tf_op jit(solution)/shard_map/ppermute | solution.py:390
  134.9 1.1 half.1.mine_ref
  136.0 0.4 collective-permute-done.5.other_ref
  136.4 3.1 %update.1 = f32[256,512]{1,0:T(8,128)} custom-call(f32[256,512]{1,0:T(8,128)S(1)} %copy-done, f32[256,512]{1,0:T(8,128)S(1)} %half.1.mine_ref, f32[16,2,32,128]{3,2,1,0:T(8,128)S(1)} %collective-permute-done.5.other_ref, f32[512,512]{1,0:T(8,128)S(1)} %get-tuple-element.65.linv_ref, f32[4,264,128]{2,1,0:T(8,128)S(1)} %get-tuple-element.66.e_ref), custom_call_target="tpu_custom_call" | custom-call | flops 2147483648 | bytes 1048576 | tf_op jit(solution)/shard_map/update/pallas_call | solution.py:448
  (21 shorter events, 0.3 us)
Async XLA Ops:
  36.2 28.1 %all-to-all-start.1 = ((f32[16,40,128]{2,1,0:T(8,128)}), f32[16,40,128]{2,1,0:T(8,128)S(1)}, u32[]{:S(2)}, u32[]{:S(2)}) async-start(f32[16,40,128]{2,1,0:T(8,128)} %broadcast_in_dim.36), calls=%async_computation.1 | async-start | bytes 655360 | tf_op jit(solution)/shard_map/all_to_all | solution.py:377
  49.2 16.4 %collective-permute-start = (f32[2,32,128]{2,1,0:T(8,128)S(1)}, f32[2,32,128]{2,1,0:T(8,128)S(1)}, u32[]{:S(2)}, u32[]{:S(2)}) collective-permute-start(f32[2,32,128]{2,1,0:T(8,128)S(1)} %bitcast_reduce_fusion), channel_id=1, source_target_pairs={{0,0},{1,32},{2,64},{3,96},{4,128},{5,160},{6,192},{7,224},{8,256}... | collective-permute-start | bytes 98312 | tf_op jit(solution)/shard_map/ppermute | solution.py:378
  65.6 21.4 %copy-start.2 = (f32[2,256]{1,0:T(2,128)S(1)}, f32[2,256]{1,0:T(2,128)}, u32[]{:S(2)}) copy-start(f32[2,256]{1,0:T(2,128)} %param.8) | copy-start | bytes 6148
  65.6 21.5 %copy-start.3 = (f32[2,256]{1,0:T(2,128)S(1)}, f32[2,256]{1,0:T(2,128)}, u32[]{:S(2)}) copy-start(f32[2,256]{1,0:T(2,128)} %param.11) | copy-start | bytes 6148
  65.6 33.6 %all-to-all-start.2 = ((f32[32,72,128]{2,1,0:T(8,128)}), f32[32,72,128]{2,1,0:T(8,128)S(1)}, u32[]{:S(2)}, u32[]{:S(2)}) async-start(f32[32,72,128]{2,1,0:T(8,128)} %pad_maximum_fusion), calls=%async_computation.2 | async-start | bytes 2359296 | tf_op jit(solution)/shard_map/all_to_all | solution.py:387
  81.5 13.4 %collective-permute-start.1 = (f32[1,2,32,128]{3,2,1,0:T(8,128)S(1)}, f32[1,2,32,128]{3,2,1,0:T(8,128)S(1)}, u32[]{:S(2)}, u32[]{:S(2)}) collective-permute-start(f32[1,2,32,128]{3,2,1,0:T(8,128)S(1)} %bitcast.32), channel_id=1, source_target_pairs={{0,256},{16,272},{32,288},{48,304},{64,320},{80,336},{96,352},{112... | collective-permute-start | bytes 98312 | tf_op jit(solution)/shard_map/ppermute | solution.py:390
  99.2 13.0 %collective-permute-start.2 = (f32[2,2,32,128]{3,2,1,0:T(8,128)S(1)}, f32[2,2,32,128]{3,2,1,0:T(8,128)S(1)}, u32[]{:S(2)}, u32[]{:S(2)}) collective-permute-start(f32[2,2,32,128]{3,2,1,0:T(8,128)S(1)} %maximum_bitcast_fusion), channel_id=1, source_target_pairs={{0,128},{16,144},{32,160},{48,176},{64,192},{80,208},{96,224},{112... | collective-permute-start | bytes 196616 | tf_op jit(solution)/shard_map/ppermute | solution.py:390
  112.3 12.0 %copy-start.1 = (f32[256]{0:T(256)S(1)}, f32[256]{0:T(256)}, u32[]{:S(2)}) copy-start(f32[256]{0:T(256)} %param.7) | copy-start | bytes 3076
  112.3 9.8 %collective-permute-start.3 = (f32[4,2,32,128]{3,2,1,0:T(8,128)S(1)}, f32[4,2,32,128]{3,2,1,0:T(8,128)S(1)}, u32[]{:S(2)}, u32[]{:S(2)}) collective-permute-start(f32[4,2,32,128]{3,2,1,0:T(8,128)S(1)} %bitcast.26), channel_id=1, source_target_pairs={{0,64},{16,80},{32,96},{48,112},{64,0},{80,16},{96,32},{112,48},{1... | collective-permute-start | bytes 393224 | tf_op jit(solution)/shard_map/ppermute | solution.py:390
  122.1 8.9 %collective-permute-start.4 = (f32[8,2,32,128]{3,2,1,0:T(8,128)S(1)}, f32[8,2,32,128]{3,2,1,0:T(8,128)S(1)}, u32[]{:S(2)}, u32[]{:S(2)}) collective-permute-start(f32[8,2,32,128]{3,2,1,0:T(8,128)S(1)} %bitcast.24), channel_id=1, source_target_pairs={{0,32},{16,48},{32,0},{48,16},{64,96},{80,112},{96,64},{112,80},{1... | collective-permute-start | bytes 786440 | tf_op jit(solution)/shard_map/ppermute | solution.py:390
  131.1 5.3 %copy-start = (f32[256,512]{1,0:T(8,128)S(1)}, f32[256,512]{1,0:T(8,128)}, u32[]{:S(2)}) copy-start(f32[256,512]{1,0:T(8,128)} %cov_ref.1) | copy-start | bytes 1572868
  131.1 5.3 %collective-permute-start.5 = (f32[16,2,32,128]{3,2,1,0:T(8,128)S(1)}, f32[16,2,32,128]{3,2,1,0:T(8,128)S(1)}, u32[]{:S(2)}, u32[]{:S(2)}) collective-permute-start(f32[16,2,32,128]{3,2,1,0:T(8,128)S(1)} %bitcast.19), channel_id=1, source_target_pairs={{0,16},{16,0},{32,48},{48,32},{64,80},{80,64},{96,112},{112,96},{1... | collective-permute-start | bytes 1572872 | tf_op jit(solution)/shard_map/ppermute | solution.py:390
